TPU v7x, 32 devices: a whole 2x2x4 slice. The times are simulated.
32 devices in a mesh: gz: 4 (over y, x), dev: 8 (over z, core).
Axes of the slice: x: 2, y: 2, z: 4, core: 2. Of those that a mesh axis runs over, the one named last changes fastest.
Arguments:
- source: float32 [512, 8, 2048], P(None, None, ('gz', 'dev')), may hold values from -6 to 6
- interior_inverse: float32 [512, 512], replicated, as said below
- coupling: float32 [512, 384], replicated, may hold values from -0.25 to 0.25
- trace_operator: float32 [384, 384], replicated, as said below
- face_ids: int32 [2048, 4], P(('gz', 'dev')), may hold values from 0 to 1023, as said below
- orientation: int32 [2048, 6], P(('gz', 'dev')), may hold values from 0 to 7
- element_scale: int32 [2048], P(('gz', 'dev')), may hold values from 1 to 4
Outputs:
- interior: float32 [512, 8, 2048], P(None, None, ('gz', 'dev'))
- side_traces: float32 [64, 8, 4096], P(None, None, ('gz', 'dev'))
- top_traces: float32 [64, 8, 2048], P(None, None, ('gz', 'dev'))
Inputs may be any that keep to these rules, and one draw needn't show every extreme that they name: `face_ids`: elements come in blocks of 64 (block b of a layer is the layer's elements b * 64 onward) and a layer's side faces in blocks of 128; face f of a layer belongs to block f // 128. Columns 0 and 1 of a block's elements name each face of that block exactly once. Columns 2 and 3 of a layer's elements name each face of the layer exactly once. The elements of one block name, in columns 2 and 3, at most 8 faces of any one other block, and in every layer some block reaches 8 with some other block. `interior_inverse`: symmetric positive definite. `trace_operator`: symmetric positive definite.
All inputs are finite; a program needn't handle non-finite values.
Results may differ from a plain program's by a relative error of at most 0.0001.
Values sent between devices are 32-bit elements; how exact they have to be, the bound alone decides.
No kernel may reach another device: no remote copies, remote signals or barrier semaphores. Data moves between devices by JAX's collectives and lax.ppermute only.
A program may use at most 64 MiB of HBM per device.

v0:
```python
import math

import jax
import jax.numpy as jnp
from jax import lax
from jax.sharding import PartitionSpec as P

ITERATIONS = 2


def from_behind(value, axis, steps):
    count = lax.axis_size(axis)
    first, last = (max(0, -steps), min(count, count - steps))
    return lax.ppermute(value, axis, [(source, source + steps) for source in range(first, last)])


def orient_traces(traces, codes, inverse):
    side_count, face_nodes, right_count, element_count = traces.shape
    edge = math.isqrt(face_nodes)
    grid = traces.reshape(side_count, edge, edge, right_count, element_count)
    swapped = (codes // 4 % 2 == 1)[:, None, None, None, :]
    flip_first = (codes // 2 % 2 == 1)[:, None, None, None, :]
    flip_second = (codes % 2 == 1)[:, None, None, None, :]
    if inverse:
        grid = jnp.where(flip_second, grid[:, :, ::-1], grid)
        grid = jnp.where(flip_first, grid[:, ::-1], grid)
        grid = jnp.where(swapped, jnp.swapaxes(grid, 1, 2), grid)
    else:
        grid = jnp.where(swapped, jnp.swapaxes(grid, 1, 2), grid)
        grid = jnp.where(flip_first, grid[:, ::-1], grid)
        grid = jnp.where(flip_second, grid[:, :, ::-1], grid)
    return grid.reshape(side_count, face_nodes, right_count, element_count)


def element_operator(local, trace_operator, element_scale):
    side_count, face_nodes, right_count, element_count = local.shape
    flat = local.reshape(side_count * face_nodes, right_count * element_count)
    image = jnp.dot(
        trace_operator, flat, precision=lax.Precision.HIGHEST, preferred_element_type=jnp.float32
    )
    return image.reshape(local.shape) * element_scale.astype(jnp.float32)


def inner_owned(first, second):
    return jnp.sum(first[0] * second[0], axis=(0, 2)) + jnp.sum(first[1] * second[1], axis=(0, 2))


def advance(first, factor, second):
    return jax.tree.map(lambda left, right: left + factor[:, None] * right, first, second)


def per_device(
    source, interior_inverse, coupling, trace_operator, face_ids, orientation, element_scale
):
    nodes, right_count, element_count = source.shape
    face_nodes = trace_operator.shape[0] // 6
    blocks = lax.axis_size("dev")
    capacity = element_count // blocks
    owned_count = 2 * element_count
    sides_sent = 2 * element_count
    here = lax.axis_index("dev")
    codes = orientation.T
    owners = face_ids // owned_count
    slots = face_ids % owned_count
    second_owner = owners[:, 2:4].T.reshape(-1)
    second_slot = slots[:, 2:4].T.reshape(-1)
    crossing = second_owner != here
    onehot = (
        (second_owner[:, None] == jnp.arange(blocks, dtype=jnp.int32)[None, :]) & crossing[:, None]
    ).astype(jnp.int32)
    earlier = jnp.cumsum(onehot, axis=0) - onehot
    position = jnp.sum(earlier * onehot, axis=1)
    bucket = jnp.where(crossing, second_owner * capacity + position, blocks * capacity)
    source_of = (
        jnp.full((blocks * capacity,), sides_sent, jnp.int32)
        .at[bucket]
        .set(jnp.arange(sides_sent, dtype=jnp.int32), mode="drop")
    )
    sent_slot = jnp.where(
        source_of < sides_sent,
        jnp.take(second_slot, jnp.minimum(source_of, sides_sent - 1)),
        owned_count,
    )
    wanted = lax.all_to_all(sent_slot, "dev", split_axis=0, concat_axis=0, tiled=True)
    own_slot = jnp.where(crossing, owned_count, second_slot)
    bucket_read = jnp.minimum(bucket, blocks * capacity - 1)
    keep_top = (lax.axis_index("gz") < lax.axis_size("gz") - 1).astype(jnp.float32)

    def to_faces(local):
        placed = orient_traces(local, codes, True)
        sides = jnp.zeros((face_nodes, right_count, owned_count), jnp.float32)
        sides = sides.at[:, :, slots[:, 0]].add(placed[0])
        sides = sides.at[:, :, slots[:, 1]].add(placed[1])
        second = jnp.concatenate([placed[2], placed[3]], axis=2)
        sides = sides.at[:, :, own_slot].add(second, mode="drop")
        outgoing = jnp.take(second, source_of, axis=2, mode="fill", fill_value=0.0)
        received = lax.all_to_all(outgoing, "dev", split_axis=2, concat_axis=2, tiled=True)
        sides = sides.at[:, :, wanted].add(received, mode="drop")
        from_above = from_behind(placed[4], "gz", -1)
        tops = (placed[5] + from_above) * keep_top
        return (sides, tops)

    def to_elements(traces):
        sides, tops = traces
        first_zero = jnp.take(sides, slots[:, 0], axis=2)
        first_one = jnp.take(sides, slots[:, 1], axis=2)
        reply = jnp.take(sides, wanted, axis=2, mode="fill", fill_value=0.0)
        returned = lax.all_to_all(reply, "dev", split_axis=2, concat_axis=2, tiled=True)
        nearby = jnp.take(sides, second_slot, axis=2)
        remote = jnp.take(returned, bucket_read, axis=2)
        second = jnp.where(crossing[None, None, :], remote, nearby)
        below = from_behind(tops, "gz", 1)
        local = jnp.stack(
            [
                first_zero,
                first_one,
                second[:, :, :element_count],
                second[:, :, element_count:],
                below,
                tops,
            ]
        )
        return orient_traces(local, codes, False)

    solved = jnp.dot(
        interior_inverse,
        source.reshape(nodes, right_count * element_count),
        precision=lax.Precision.HIGHEST,
        preferred_element_type=jnp.float32,
    )
    condensed = lax.dot_general(
        coupling,
        solved,
        (((0,), (0,)), ((), ())),
        precision=lax.Precision.HIGHEST,
        preferred_element_type=jnp.float32,
    )
    condensed = condensed.reshape(6, face_nodes, right_count, element_count)
    residual = to_faces(condensed)

    def apply_operator(vector):
        local = to_elements(vector)
        return (to_faces(element_operator(local, trace_operator, element_scale)), local)

    def pair_sums(vector, image):
        return lax.psum((inner_owned(vector, vector), inner_owned(vector, image)), ("gz", "dev"))

    solution = jax.tree.map(jnp.zeros_like, residual)
    image, local = apply_operator(residual)
    norm_now, product = pair_sums(residual, image)
    alpha = norm_now / product
    direction, along, direction_local = (residual, image, local)
    for step in range(ITERATIONS):
        solution = advance(solution, alpha, direction)
        residual = advance(residual, -alpha, along)
        if step + 1 < ITERATIONS:
            image, local = apply_operator(residual)
            norm_next, product = pair_sums(residual, image)
            ratio = norm_next / norm_now
            alpha = norm_next / (product - ratio * norm_next / alpha)
            direction = advance(residual, ratio, direction)
            along = advance(image, ratio, along)
            direction_local = local + ratio[:, None] * direction_local
            norm_now = norm_next
    element_traces = to_elements(solution)
    side_traces, top_traces = solution
    coupled = jnp.dot(
        coupling,
        element_traces.reshape(6 * face_nodes, right_count * element_count),
        precision=lax.Precision.HIGHEST,
        preferred_element_type=jnp.float32,
    )
    correction = jnp.dot(
        interior_inverse,
        coupled,
        precision=lax.Precision.HIGHEST,
        preferred_element_type=jnp.float32,
    )
    interior = solved.reshape(source.shape) / element_scale.astype(
        jnp.float32
    ) - correction.reshape(source.shape)
    return (interior, side_traces, top_traces)


def solution(mesh):
    placed = (
        P(None, None, ("gz", "dev")),
        P(),
        P(),
        P(),
        P(("gz", "dev"), None),
        P(("gz", "dev"), None),
        P(("gz", "dev")),
    )
    return jax.shard_map(
        per_device,
        mesh=mesh,
        in_specs=placed,
        out_specs=(
            P(None, None, ("gz", "dev")),
            P(None, None, ("gz", "dev")),
            P(None, None, ("gz", "dev")),
        ),
        check_vma=False,
    )
```

profile of v0, /device:TPU:0, one launch (start us, length us, event | category | flops | bytes accessed | tf_op | source)
XLA Modules:
  0.0 359.2 jit_solution(347469458569694132)
XLA Ops:
  4.8 6.3 %all-to-all-start = ((s32[8,8,1]{1,2,0:T(1,128)}), s32[8,8,1]{1,2,0:T(1,128)S(1)}, u32[]{:S(2)}, u32[]{:S(2)}) async-start(s32[8,8,1]{1,2,0:T(1,128)} %bitcast.20), calls=%async_computation | async-start | bytes 8192 | tf_op jit(solution)/shard_map/all_to_all | solution.py:84
  33.1 5.0 %scatter_fusion.2 = f32[64,8,128]{0,1,2:T(8,128)S(1)} fusion(f32[64,8,128]{0,1,2:T(8,128)S(1)} %scatter_fusion.1, s32[128]{0:T(128)S(1)} %get-tuple-element.83, f32[128,64,8]{1,2,0:T(8,128)S(1)} %get-tuple-element.70), kind=kCustom, calls=%fused_computation.21 | custom fusion | flops 65536 | bytes 786944 | tf_op jit(solution)/shard_map/scatter-add | solution.py:95
  38.1 5.1 %all-to-all-start.1 = ((f32[8,1,4096]{2,1,0:T(1,128)}), f32[8,1,4096]{2,1,0:T(1,128)S(1)}, u32[]{:S(2)}, u32[]{:S(2)}) async-start(f32[8,1,4096]{2,1,0:T(1,128)} %reshape.579), calls=%async_computation.1 | async-start | bytes 262144 | tf_op jit(solution)/shard_map/all_to_all | solution.py:97
  45.6 5.3 %collective-permute-start.1 = (f32[64,8,64]{2,1,0:T(8,128)S(1)}, f32[64,8,64]{2,1,0:T(8,128)}, u32[]{:S(2)}, u32[]{:S(2)}) collective-permute-start(f32[64,8,64]{2,1,0:T(8,128)S(1)} %fusion.4), channel_id=1, source_target_pairs={{0,8},{8,16},{16,24},{1,9},{9,17},{17,25},{2,10},{10,18},{18,26},{... | collective-permute-start | bytes 393224 | tf_op jit(solution)/shard_map/ppermute | solution.py:14
  56.9 5.4 %all-to-all-start.2 = ((f32[8,1,4096]{2,1,0:T(1,128)}), f32[8,1,4096]{2,1,0:T(1,128)S(1)}, u32[]{:S(2)}, u32[]{:S(2)}) async-start(f32[8,1,4096]{2,1,0:T(1,128)} %reshape.581), calls=%async_computation.2 | async-start | bytes 262144 | tf_op jit(solution)/shard_map/all_to_all | solution.py:108
  82.2 3.8 %convolution_bitcast_fusion.1 = f32[384,512]{0,1:T(8,128)S(1)} fusion(f32[384,512]{1,0:T(8,128)} %reshape_reshape.13, f32[384,384]{1,0:T(8,128)S(1)} %copy-done.5), kind=kOutput, calls=%fused_computation.51 | convolution fusion | flops 905969664 | bytes 2162688 | tf_op jit(solution)/shard_map/dot_general | solution.py:38
  100.9 3.4 all-to-all-start.3
  106.0 5.1 %scatter_fusion.4 = f32[64,8,128]{0,1,2:T(8,128)S(1)} fusion(f32[64,8,128]{0,1,2:T(8,128)S(1)} %broadcast.189.clone.1, s32[64]{0:T(128)} %copy-done.19, f32[64,64,8]{1,2,0:T(8,128)} %copy.138), kind=kCustom, calls=%fused_computation.24 | custom fusion | flops 32768 | bytes 393472 | tf_op jit(solution)/shard_map/scatter-add | solution.py:92
  111.1 5.1 %scatter_fusion.5 = f32[64,8,128]{0,1,2:T(8,128)S(1)} fusion(f32[64,8,128]{0,1,2:T(8,128)S(1)} %scatter_fusion.4, s32[64]{0:T(128)} %copy-done.17, f32[64,64,8]{1,2,0:T(8,128)} %copy.139), kind=kCustom, calls=%fused_computation.25 | custom fusion | flops 32768 | bytes 393472 | tf_op jit(solution)/shard_map/scatter-add | solution.py:93
  116.3 5.1 %scatter_fusion.6 = f32[64,8,128]{0,1,2:T(8,128)S(1)} fusion(f32[64,8,128]{0,1,2:T(8,128)S(1)} %scatter_fusion.5, s32[128]{0:T(128)} %copy-done.15, f32[128,64,8]{1,2,0:T(8,128)S(1)} %copy-done.6), kind=kCustom, calls=%fused_computation.26 | custom fusion | flops 65536 | bytes 786944 | tf_op jit(solution)/shard_map/scatter-add | solution.py:95
  126.5 52.5 %all-reduce.1 = (f32[8]{0:T(128)S(1)}, f32[8]{0:T(128)S(1)}) all-reduce(f32[8]{0:T(128)S(1)} %add.225, f32[8]{0:T(128)S(1)} %add.228), channel_id=1, replica_groups=mesh['gz'=4,'dev'=8] {'gz','dev'}, use_global_device_ids=true, to_apply=%region_9.11 | all-reduce | flops 16 | bytes 128 | tf_op jit(solution)/shard_map/psum | solution.py:146
  185.3 4.9 %collective-permute-start.3 = (f32[64,8,64]{2,1,0:T(8,128)S(1)}, f32[64,8,64]{2,1,0:T(8,128)}, u32[]{:S(2)}, u32[]{:S(2)}) collective-permute-start(f32[64,8,64]{2,1,0:T(8,128)S(1)} %multiply_add_fusion.3), channel_id=1, source_target_pairs={{0,8},{8,16},{16,24},{1,9},{9,17},{17,25},{2,10},{10,18},{18,26},{... | collective-permute-start | bytes 393224 | tf_op jit(solution)/shard_map/ppermute | solution.py:14
  192.2 3.6 all-to-all-start.4
  219.3 4.8 %convolution_bitcast_fusion = f32[384,512]{0,1:T(8,128)} fusion(f32[384,512]{1,0:T(8,128)} %reshape_reshape.14, f32[384,384]{1,0:T(8,128)} %param.18), kind=kOutput, calls=%fused_computation.50 | convolution fusion | flops 905969664 | bytes 2162688 | tf_op jit(solution)/shard_map/dot_general | solution.py:38
  240.6 4.0 %all-to-all-start.5 = ((f32[8,1,4096]{2,1,0:T(1,128)}), f32[8,1,4096]{2,1,0:T(1,128)}, u32[]{:S(2)}, u32[]{:S(2)}) async-start(f32[8,1,4096]{2,1,0:T(1,128)} %reshape.587), calls=%async_computation.5 | async-start | bytes 262144 | tf_op jit(solution)/shard_map/all_to_all | solution.py:97
  247.3 5.0 %scatter_fusion.8 = f32[64,8,128]{0,1,2:T(8,128)S(1)} fusion(f32[64,8,128]{0,1,2:T(8,128)S(1)} %broadcast.189, s32[64]{0:T(128)S(1)} %copy-done.20, f32[64,64,8]{1,2,0:T(8,128)} %copy.149), kind=kCustom, calls=%fused_computation.28 | custom fusion | flops 32768 | bytes 393472 | tf_op jit(solution)/shard_map/scatter-add | solution.py:92
  252.3 5.0 %scatter_fusion.9 = f32[64,8,128]{0,1,2:T(8,128)S(1)} fusion(f32[64,8,128]{0,1,2:T(8,128)S(1)} %scatter_fusion.8, s32[64]{0:T(128)S(1)} %copy-done.18, f32[64,64,8]{1,2,0:T(8,128)} %copy.150), kind=kCustom, calls=%fused_computation.29 | custom fusion | flops 32768 | bytes 393472 | tf_op jit(solution)/shard_map/scatter-add | solution.py:93
  257.3 9.6 %scatter_fusion.10 = f32[64,8,128]{0,1,2:T(8,128)S(1)} fusion(f32[64,8,128]{0,1,2:T(8,128)S(1)} %scatter_fusion.9, s32[128]{0:T(128)S(1)} %copy-done.16, f32[128,64,8]{1,2,0:T(8,128)} %get-tuple-element.62), kind=kCustom, calls=%fused_computation.30 | custom fusion | flops 65536 | bytes 786944 | tf_op jit(solution)/shard_map/scatter-add | solution.py:95
  271.3 5.2 %scatter_fusion.11 = f32[64,8,128]{0,1,2:T(8,128)S(1)} fusion(f32[64,8,128]{0,1,2:T(8,128)S(1)} %scatter_fusion.10, s32[64]{0:T(128)} %copy-done.34, f32[64,64,8]{1,2,0:T(8,128)} %bitcast_bitcast_fusion), kind=kCustom, calls=%fused_computation.31 | custom fusion | flops 32768 | bytes 393472 | tf_op jit(solution)/shard_map/scatter-add | solution.py:98
  276.8 42.0 %all-reduce = (f32[8]{0:T(128)S(1)}, f32[8]{0:T(128)S(1)}) all-reduce(f32[8]{0:T(128)S(1)} %add.231, f32[8]{0:T(128)S(1)} %add.233), channel_id=1, replica_groups=mesh['gz'=4,'dev'=8] {'gz','dev'}, use_global_device_ids=true, to_apply=%region_19.24 | all-reduce | flops 16 | bytes 128 | tf_op jit(solution)/shard_map/psum | solution.py:146
  325.2 4.9 %collective-permute-start.5 = (f32[64,8,64]{2,1,0:T(8,128)}, f32[64,8,64]{2,1,0:T(8,128)}, u32[]{:S(2)}, u32[]{:S(2)}) collective-permute-start(f32[64,8,64]{2,1,0:T(8,128)} %multiply_add_fusion.2), channel_id=1, source_target_pairs={{0,8},{8,16},{16,24},{1,9},{9,17},{17,25},{2,10},{10,18},{18,26},{... | collective-permute-start | bytes 393224 | tf_op jit(solution)/shard_map/ppermute | solution.py:14
  331.1 4.2 %all-to-all-start.6 = ((f32[8,1,4096]{2,1,0:T(1,128)}), f32[8,1,4096]{2,1,0:T(1,128)}, u32[]{:S(2)}, u32[]{:S(2)}) async-start(f32[8,1,4096]{2,1,0:T(1,128)} %reshape.589), calls=%async_computation.6 | async-start | bytes 262144 | tf_op jit(solution)/shard_map/all_to_all | solution.py:108
  337.6 4.5 %all-to-all-done.6 = f32[8,1,4096]{2,1,0:T(1,128)} async-done(((f32[8,1,4096]{2,1,0:T(1,128)}), f32[8,1,4096]{2,1,0:T(1,128)}, u32[]{:S(2)}, u32[]{:S(2)}) %all-to-all-start.6) | async-done | bytes 131104 | tf_op jit(solution)/shard_map/all_to_all | solution.py:108
  351.9 3.9 %fusion.42 = f32[512,512]{1,0:T(8,128)S(1)} fusion(f32[384,512]{1,0:T(8,128)} %reshape_reshape.15, f32[512,384]{1,0:T(8,128)S(1)} %copy-done.4), kind=kOutput, calls=%fused_computation.210 | convolution fusion | flops 1207959552 | bytes 2621440 | tf_op jit(solution)/shard_map/dot_general | solution.py:167
  (308 shorter events, 153.1 us)
Async XLA Ops:
  4.8 33.3 %all-to-all-start = ((s32[8,8,1]{1,2,0:T(1,128)}), s32[8,8,1]{1,2,0:T(1,128)S(1)}, u32[]{:S(2)}, u32[]{:S(2)}) async-start(s32[8,8,1]{1,2,0:T(1,128)} %bitcast.20), calls=%async_computation | async-start | bytes 8192 | tf_op jit(solution)/shard_map/all_to_all | solution.py:84
  21.9 22.7 %collective-permute-start = (f32[64,8,64]{2,1,0:T(8,128)}, f32[64,8,64]{2,1,0:T(8,128)}, u32[]{:S(2)}, u32[]{:S(2)}) collective-permute-start(f32[64,8,64]{2,1,0:T(8,128)} %bitcast.25), channel_id=1, source_target_pairs={{8,0},{16,8},{24,16},{9,1},{17,9},{25,17},{10,2},{18,10},{26,18},{... | collective-permute-start | bytes 393224 | tf_op jit(solution)/shard_map/ppermute | solution.py:14
  23.2 75.7 %copy-start.32 = (pred[64]{0:T(512)(128)(4,1)}, pred[64]{0:T(512)(128)(4,1)S(1)}, u32[]{:S(2)}) copy-start(pred[64]{0:T(512)(128)(4,1)S(1)} %compare_and_fusion.5) | copy-start | bytes 196
  23.3 47.6 %copy-start.10 = (pred[128]{0:T(512)(128)(4,1)}, pred[128]{0:T(512)(128)(4,1)S(1)}, u32[]{:S(2)}) copy-start(pred[128]{0:T(512)(128)(4,1)S(1)} %get-tuple-element.35) | copy-start | bytes 388
  23.3 47.5 %copy-start.27 = (pred[128]{0:T(512)(128)(4,1)}, pred[128]{0:T(512)(128)(4,1)S(1)}, u32[]{:S(2)}) copy-start(pred[128]{0:T(512)(128)(4,1)S(1)} %compare_and_fusion.1) | copy-start | bytes 388
  23.4 40.4 %copy-start.13 = (pred[64]{0:T(512)(128)(4,1)}, pred[64]{0:T(512)(128)(4,1)S(1)}, u32[]{:S(2)}) copy-start(pred[64]{0:T(512)(128)(4,1)S(1)} %get-tuple-element.74) | copy-start | bytes 196
  23.4 41.3 %copy-start.11 = (pred[64]{0:T(512)(128)(4,1)}, pred[64]{0:T(512)(128)(4,1)S(1)}, u32[]{:S(2)}) copy-start(pred[64]{0:T(512)(128)(4,1)S(1)} %get-tuple-element.37) | copy-start | bytes 196
  23.4 74.2 %copy-start.26 = (s32[1024]{0:T(1024)}, s32[1024]{0:T(1024)S(1)}, u32[]{:S(2)}) copy-start(s32[1024]{0:T(1024)S(1)} %pad_clamp_fusion.5) | copy-start | bytes 12292
  27.4 42.6 %copy-start.21 = (s32[1024]{0:T(1024)}, s32[1024]{0:T(1024)S(1)}, u32[]{:S(2)}) copy-start(s32[1024]{0:T(1024)S(1)} %pad_clamp_fusion.1) | copy-start | bytes 12292
  27.5 62.1 %copy-start.35 = (f32[64]{0:T(128)}, f32[64]{0:T(128)S(1)}, u32[]{:S(2)}) copy-start(f32[64]{0:T(128)S(1)} %convert_element_type.11) | copy-start | bytes 772
  27.5 35.6 %copy-start.24 = (s32[1024]{0:T(1024)}, s32[1024]{0:T(1024)S(1)}, u32[]{:S(2)}) copy-start(s32[1024]{0:T(1024)S(1)} %get-tuple-element.87) | copy-start | bytes 12292
  27.5 36.5 %copy-start.23 = (s32[1024]{0:T(1024)}, s32[1024]{0:T(1024)S(1)}, u32[]{:S(2)}) copy-start(s32[1024]{0:T(1024)S(1)} %get-tuple-element.86) | copy-start | bytes 12292
  38.1 12.8 %all-to-all-start.1 = ((f32[8,1,4096]{2,1,0:T(1,128)}), f32[8,1,4096]{2,1,0:T(1,128)S(1)}, u32[]{:S(2)}, u32[]{:S(2)}) async-start(f32[8,1,4096]{2,1,0:T(1,128)} %reshape.579), calls=%async_computation.1 | async-start | bytes 262144 | tf_op jit(solution)/shard_map/all_to_all | solution.py:97
  45.6 27.9 %collective-permute-start.1 = (f32[64,8,64]{2,1,0:T(8,128)S(1)}, f32[64,8,64]{2,1,0:T(8,128)}, u32[]{:S(2)}, u32[]{:S(2)}) collective-permute-start(f32[64,8,64]{2,1,0:T(8,128)S(1)} %fusion.4), channel_id=1, source_target_pairs={{0,8},{8,16},{16,24},{1,9},{9,17},{17,25},{2,10},{10,18},{18,26},{... | collective-permute-start | bytes 393224 | tf_op jit(solution)/shard_map/ppermute | solution.py:14
  56.9 12.1 %all-to-all-start.2 = ((f32[8,1,4096]{2,1,0:T(1,128)}), f32[8,1,4096]{2,1,0:T(1,128)S(1)}, u32[]{:S(2)}, u32[]{:S(2)}) async-start(f32[8,1,4096]{2,1,0:T(1,128)} %reshape.581), calls=%async_computation.2 | async-start | bytes 262144 | tf_op jit(solution)/shard_map/all_to_all | solution.py:108
  92.7 28.7 %collective-permute-start.2 = (f32[64,8,64]{2,1,0:T(8,128)}, f32[64,8,64]{2,1,0:T(8,128)S(1)}, u32[]{:S(2)}, u32[]{:S(2)}) collective-permute-start(f32[64,8,64]{2,1,0:T(8,128)} %bitcast.51), channel_id=1, source_target_pairs={{8,0},{16,8},{24,16},{9,1},{17,9},{25,17},{10,2},{18,10},{26,18},{... | collective-permute-start | bytes 393224 | tf_op jit(solution)/shard_map/ppermute | solution.py:14
  100.9 21.3 %all-to-all-start.3 = ((f32[8,1,4096]{2,1,0:T(1,128)}), f32[8,1,4096]{2,1,0:T(1,128)S(1)}, u32[]{:S(2)}, u32[]{:S(2)}) async-start(f32[8,1,4096]{2,1,0:T(1,128)} %reshape.583), calls=%async_computation.3 | async-start | bytes 262144 | tf_op jit(solution)/shard_map/all_to_all | solution.py:97
  185.3 25.3 %collective-permute-start.3 = (f32[64,8,64]{2,1,0:T(8,128)S(1)}, f32[64,8,64]{2,1,0:T(8,128)}, u32[]{:S(2)}, u32[]{:S(2)}) collective-permute-start(f32[64,8,64]{2,1,0:T(8,128)S(1)} %multiply_add_fusion.3), channel_id=1, source_target_pairs={{0,8},{8,16},{16,24},{1,9},{9,17},{17,25},{2,10},{10,18},{18,26},{... | collective-permute-start | bytes 393224 | tf_op jit(solution)/shard_map/ppermute | solution.py:14
  192.2 10.3 %all-to-all-start.4 = ((f32[8,1,4096]{2,1,0:T(1,128)}), f32[8,1,4096]{2,1,0:T(1,128)S(1)}, u32[]{:S(2)}, u32[]{:S(2)}) async-start(f32[8,1,4096]{2,1,0:T(1,128)} %reshape.585), calls=%async_computation.4 | async-start | bytes 262144 | tf_op jit(solution)/shard_map/all_to_all | solution.py:108
  232.1 34.8 %collective-permute-start.4 = (f32[64,8,64]{2,1,0:T(8,128)}, f32[64,8,64]{2,1,0:T(8,128)}, u32[]{:S(2)}, u32[]{:S(2)}) collective-permute-start(f32[64,8,64]{2,1,0:T(8,128)} %bitcast.76), channel_id=1, source_target_pairs={{8,0},{16,8},{24,16},{9,1},{17,9},{25,17},{10,2},{18,10},{26,18},{... | collective-permute-start | bytes 393224 | tf_op jit(solution)/shard_map/ppermute | solution.py:14
  240.6 28.0 %all-to-all-start.5 = ((f32[8,1,4096]{2,1,0:T(1,128)}), f32[8,1,4096]{2,1,0:T(1,128)}, u32[]{:S(2)}, u32[]{:S(2)}) async-start(f32[8,1,4096]{2,1,0:T(1,128)} %reshape.587), calls=%async_computation.5 | async-start | bytes 262144 | tf_op jit(solution)/shard_map/all_to_all | solution.py:97
  270.5 50.4 %copy-start.28 = (f32[8]{0:T(128)S(1)}, f32[8]{0:T(128)}, u32[]{:S(2)}) copy-start(f32[8]{0:T(128)} %get-tuple-element.34) | copy-start | bytes 100
  325.2 22.8 %collective-permute-start.5 = (f32[64,8,64]{2,1,0:T(8,128)}, f32[64,8,64]{2,1,0:T(8,128)}, u32[]{:S(2)}, u32[]{:S(2)}) collective-permute-start(f32[64,8,64]{2,1,0:T(8,128)} %multiply_add_fusion.2), channel_id=1, source_target_pairs={{0,8},{8,16},{16,24},{1,9},{9,17},{17,25},{2,10},{10,18},{18,26},{... | collective-permute-start | bytes 393224 | tf_op jit(solution)/shard_map/ppermute | solution.py:14
  331.1 11.0 %all-to-all-start.6 = ((f32[8,1,4096]{2,1,0:T(1,128)}), f32[8,1,4096]{2,1,0:T(1,128)}, u32[]{:S(2)}, u32[]{:S(2)}) async-start(f32[8,1,4096]{2,1,0:T(1,128)} %reshape.589), calls=%async_computation.6 | async-start | bytes 262144 | tf_op jit(solution)/shard_map/all_to_all | solution.py:108
  (34 other events, 282.0 us)
where the time goes:
time: 365 us; the launch traced here: 359 us
  other arithmetic  105 us (29%)
  blocking collectives  94.6 us (26%)
  local copies, waits for them, and re-layouts  77.2 us (21%)
  starting transfers between devices  50.8 us (14%)
  matrix products  19.3 us (5%)
  waiting for transfers between devices  10.2 us (3%)
    psum x2, blocking collectives, pair_sums(): lax.psum((inner_owned(vector, vector), inner_owned(vector, image)), ('gz'...  94.6 us
    scatter-add x3, other arithmetic, to_faces(): sides = sides.at[:, :, own_slot].add(second, mode='drop')  19.7 us
    ppermute x6, starting transfers between devices, from_behind(): lax.ppermute(value, axis, [(source, source + steps) for source in range(f...  18.9 us
    unnamed x118, local copies, waits for them, and re-layouts  18 us
    all_to_all x3, starting transfers between devices, to_elements(): lax.all_to_all(reply, 'dev', split_axis=2, concat_axis=2, tiled=True)  13.1 us
    scatter-add x3, other arithmetic, to_faces(): sides = sides.at[:, :, slots[:, 0]].add(placed[0])  12.9 us
    scatter-add x3, other arithmetic, to_faces(): sides = sides.at[:, :, slots[:, 1]].add(placed[1])  12.9 us
    all_to_all x3, starting transfers between devices, to_faces(): lax.all_to_all(outgoing, 'dev', split_axis=2, concat_axis=2, tiled=True)  12.5 us
  transfers between devices with their start and end apart: 13, of which 3 were waited for; matrix products, arithmetic and copies ran while one was open for 33% of the time, Pallas kernels for 0%

commit v1 on v0

v1 whole, which is shorter than its diff:
```python
import functools
import math

import jax
import jax.numpy as jnp
from jax import lax
from jax.experimental import pallas as pl
from jax.experimental.pallas import tpu as pltpu
from jax.sharding import PartitionSpec as P

F32, BF16, I32 = jnp.float32, jnp.bfloat16, jnp.int32
VMEM_BYTES = 24 * 1024 * 1024
STATS = 9


def call(body, outs, args, scratch=(), flops=0):
    return pl.pallas_call(
        body,
        out_shape=[jax.ShapeDtypeStruct(shape, kind) for shape, kind in outs],
        scratch_shapes=list(scratch),
        compiler_params=pltpu.CompilerParams(vmem_limit_bytes=VMEM_BYTES),
        cost_estimate=pl.CostEstimate(
            flops=flops, bytes_accessed=sum(arg.size * 4 for arg in args), transcendentals=0
        ),
    )(*args)


def halves(value):
    high = value.astype(BF16)
    return high, (value - high.astype(F32)).astype(BF16)


def dot(left, right):
    return jnp.dot(left, right, preferred_element_type=F32)


def dot_split(left, right):
    return dot(left[0], right[0]) + (dot(left[1], right[0]) + dot(left[0], right[1]))


def pick(onehot, value):
    high, low = halves(value)
    return dot(onehot, high) + dot(onehot, low)


def iota(shape, axis):
    return lax.broadcasted_iota(I32, shape, axis)


def column_of(row):
    size = row.shape[1]
    mask = iota((size, size), 0) == iota((size, size), 1)
    spread = jnp.where(mask, row.astype(F32), 0.0)
    return jnp.sum(spread, axis=1, keepdims=True).astype(I32)


def swap_blocks(source, target, rows, columns, block):
    low = iota((block, 2 * block), 1) < block
    for r in range(0, rows, 2):
        for c in range(0, columns, 2):
            lanes = slice(c * block, (c + 2) * block)
            first = source[r * block : (r + 1) * block, lanes]
            second = source[(r + 1) * block : (r + 2) * block, lanes]
            lanes = slice(r * block, (r + 2) * block)
            target[c * block : (c + 1) * block, lanes] = jnp.where(
                low, first, pltpu.roll(second, block, 1)
            )
            target[(c + 1) * block : (c + 2) * block, lanes] = jnp.where(
                low, pltpu.roll(first, block, 1), second
            )


def turn(value, table):
    width = table.shape[1]
    return jnp.concatenate(
        [
            jnp.take_along_axis(
                value[:, at : at + width], table, axis=1, mode="promise_in_bounds"
            )
            for at in range(0, value.shape[1], width)
        ],
        axis=1,
    )


def second_sides(ids_ref, owned, capacity):
    row = jnp.concatenate([ids_ref[2:3, :], ids_ref[3:4, :]], axis=1)
    owner, slot = lax.div(row, owned), lax.rem(row, owned)
    count = row.shape[1]
    crossing = owner != lax.axis_index("dev")
    owner_column = column_of(owner)
    same = (owner_column == owner) & (iota((count, count), 0) < iota((count, count), 1))
    rank = jnp.sum(jnp.where(same, 1.0, 0.0), axis=0, keepdims=True).astype(I32)
    return owner, slot, crossing, rank


def wishes_body(owned, capacity, ids, out):
    owner, slot, crossing, rank = second_sides(ids, owned, capacity)
    shape = (out.shape[0], owner.shape[1])
    place = jnp.where(crossing, owner * capacity + rank, -1)
    line = iota(shape, 0)
    position = lax.div(line, 2 * capacity) * capacity + lax.rem(line, capacity)
    chosen = jnp.where(position == place, (slot + 1).astype(F32), 0.0)
    out[...] = jnp.broadcast_to(
        jnp.sum(chosen, axis=1, keepdims=True).astype(I32), out.shape
    )


def start_body(
    face_nodes, source, inverse, coupling, orientation, solved, sides, bottom, top, forward, back,
    flat, grid
):
    columns = orientation.shape[0]
    count = orientation.shape[1]
    edge = math.isqrt(face_nodes)
    pair = 2 * face_nodes
    lane = iota((count, pair), 1)
    half = lane - lax.rem(lane, face_nodes)
    node = lax.rem(lane, face_nodes)
    a, b = lax.div(node, edge), lax.rem(node, edge)
    for c in range(columns):
        code = jnp.broadcast_to(column_of(orientation[c : c + 1, :]), (count, pair))
        swapped = (code & 4) != 0
        first = (code & 2) != 0
        second = (code & 1) != 0
        i = jnp.where(first, edge - 1 - a, a)
        j = jnp.where(second, edge - 1 - b, b)
        forward[c * count : (c + 1) * count, :] = half + jnp.where(
            swapped, j * edge + i, i * edge + j
        )
        i, j = jnp.where(swapped, b, a), jnp.where(swapped, a, b)
        i = jnp.where(first, edge - 1 - i, i)
        j = jnp.where(second, edge - 1 - j, j)
        back[c * count : (c + 1) * count, :] = half + i * edge + j
    image = dot_split(halves(source[...]), halves(inverse[...]))
    solved[...] = image
    flat[...] = dot_split(halves(image), halves(coupling[...]))
    swap_blocks(flat, grid, flat.shape[0] // count, columns, count)
    store_faces(grid, back, sides, bottom, top)


def store_faces(grid, back, sides, bottom, top):
    side_count = sides.shape[0]
    count = bottom.shape[0]
    layer = lax.axis_index("gz")
    has_below = (layer > 0).astype(F32)
    has_above = (layer < lax.axis_size("gz") - 1).astype(F32)
    sides[...] = turn(grid[:side_count, :], back[:side_count, :])
    below = slice(side_count, side_count + count)
    bottom[...] = turn(grid[below, :], back[below, :]) * has_below
    above = slice(side_count + count, side_count + 2 * count)
    top[...] = turn(grid[above, :], back[above, :]) * has_above


def send_body(owned, capacity, ids, wanted, sides, send, chooser):
    owner, slot, crossing, rank = second_sides(ids, owned, capacity)
    shape = (send.shape[0], owner.shape[1])
    line = iota(shape, 0)
    place = jnp.where(crossing, owner * (2 * capacity) + rank, -1)
    given = line == place
    first = lax.rem(jnp.concatenate([ids[0:1, :], ids[1:2, :]], axis=1), owned)
    own = lax.rem(line, 2 * capacity) >= capacity
    held = own & (wanted[:, : shape[1]] == first + 1)
    chooser[...] = jnp.concatenate([held, given], axis=1).astype(F32).astype(BF16)
    send[...] = pick(chooser[...], sides[...])


def tables_body(
    owned, capacity, ids, wanted, sides, inverse, coupling, operator,
    partner, taker, sorter, lift, operator_high, operator_low, near
):
    owner, slot, crossing, rank = second_sides(ids, owned, capacity)
    lines = wanted.shape[0]
    shape = (lines, owner.shape[1])
    line = iota(shape, 0)
    place = jnp.where(crossing, owner * (2 * capacity) + capacity + rank, -1)
    given = line == place
    first = lax.rem(jnp.concatenate([ids[0:1, :], ids[1:2, :]], axis=1), owned)
    own = lax.rem(line, 2 * capacity) < capacity
    held = own & (wanted[:, : shape[1]] == first + 1)
    both = jnp.concatenate([held, given], axis=1).astype(F32)
    taker[...] = both.T.astype(BF16)
    here = jnp.where(crossing, -1, slot)
    count = slot.shape[1]
    across = (column_of(first) == here).astype(F32)
    partner[0] = across.astype(BF16)
    partner[1] = across.T.astype(BF16)
    sorter[...] = (iota((owned, count), 0) == first).astype(F32).astype(BF16)
    high, low = halves(dot_split(halves(inverse[...]), halves(coupling[...])))
    lift[0] = high
    lift[1] = low
    high, low = halves(operator[...])
    operator_high[...] = high
    operator_low[...] = low
    add_near(partner, sides, near)


def add_near(partner, sides, near):
    count = sides.shape[0] // 2
    near[:count, :] = pick(partner[0], sides[count:, :])
    near[count:, :] = pick(partner[1], sides[:count, :])


def add_up(sides, near, taker, received, bottom, top, up, down, grid):
    side_count = sides.shape[0]
    count = bottom.shape[0]
    grid[:side_count, :] = (sides[...] + near[...]) + pick(taker[...], received[...])
    grid[side_count : side_count + count, :] = bottom[...] + up[...]
    grid[side_count + count :, :] = top[...] + down[...]


def scales(scale, columns):
    return jnp.concatenate([column_of(scale[...])] * columns, axis=0).astype(F32)


def apply_body(
    sides, near, taker, received, bottom, top, up, down, forward, back, high, low, scale, chooser,
    total, local, local_flat, image, sides_out, bottom_out, top_out, send, flat
):
    count = bottom.shape[0]
    columns = total.shape[0] // count
    rights = flat.shape[0] // count
    add_up(sides, near, taker, received, bottom, top, up, down, total)
    local[...] = turn(total[...], forward[...])
    swap_blocks(local, local_flat, columns, rights, count)
    flat[...] = dot_split(halves(local_flat[...]), (high[...], low[...])) * scales(scale, rights)
    swap_blocks(flat, image, rights, columns, count)
    store_faces(image, back, sides_out, bottom_out, top_out)
    send[...] = pick(chooser[...], sides_out[...])


def dot_across(left, right):
    return lax.dot_general(left, right, (((1,), (1,)), ((), ())), preferred_element_type=F32)


def lifted(flat, lift):
    high, low = halves(flat)
    return dot_across(high, lift[0]) + (dot_across(low, lift[0]) + dot_across(high, lift[1]))


def store_traces(total, sorter, side_traces, top_traces, rights):
    owned = sorter.shape[0]
    count = top_traces.shape[1]
    sides = pick(sorter[...], total[:owned, :]).T
    tops = total[total.shape[0] - count :, :].T
    nodes = sides.shape[0] // rights
    for r in range(rights):
        rows = slice(r * nodes, (r + 1) * nodes)
        side_traces[pl.ds(r, nodes, stride=rights), :] = sides[rows, :]
        top_traces[pl.ds(r, nodes, stride=rights), :] = tops[rows, :]


def beside_body(
    partner, sides, total, local_flat, lift, solved, scale, sorter,
    near, lifted_out, scaled, side_traces, top_traces
):
    rights = solved.shape[0] // scale.shape[1]
    add_near(partner, sides, near)
    lifted_out[...] = lifted(local_flat[...], lift)
    scaled[...] = solved[...] / scales(scale, rights)
    store_traces(total, sorter, side_traces, top_traces, rights)


def after_body(total, local_flat, lift, sorter, lifted_out, side_traces, top_traces):
    lifted_out[...] = lifted(local_flat[...], lift)
    store_traces(total, sorter, side_traces, top_traces, local_flat.shape[0] // top_traces.shape[1])


def total_rows(value):
    return jnp.sum(value, axis=0, keepdims=True)


def grouped(rows, group):
    high, rest = halves(rows)
    middle = rest.astype(F32)
    low = (rows - high.astype(F32) - middle).astype(BF16)
    return dot(high, group) + (dot(rest, group) + dot(low, group))


def stats_body(
    sides, near, taker, received, bottom, top, up, down, forward, high, low, scale,
    total, local, image, total_next, next_flat, stats, next_local, flat, next_image
):
    count = bottom.shape[0]
    columns = total.shape[0] // count
    rights = flat.shape[0] // count
    owned = sides.shape[0] // 2
    lanes = total.shape[1]
    width = lanes // rights
    add_up(sides, near, taker, received, bottom, top, up, down, total_next)
    next_local[...] = turn(total_next[...], forward[...])
    swap_blocks(next_local, next_flat, columns, rights, count)
    flat[...] = dot_split(halves(next_flat[...]), (high[...], low[...])) * scales(scale, rights)
    swap_blocks(flat, next_image, rights, columns, count)
    last = (columns - 1) * count
    b = jnp.concatenate([total[:owned, :], total[last:, :]], axis=0)
    w = jnp.concatenate([total_next[:owned, :], total_next[last:, :]], axis=0)
    group = lax.div(iota((lanes, lanes), 0), width) == lax.div(iota((lanes, lanes), 1), width)
    ww = total_rows(w * w)
    ones = jnp.ones((6, lanes), F32)
    pair = grouped(
        jnp.concatenate([total_rows(b * w), ww, ones], axis=0), group.astype(F32).astype(BF16)
    )
    sigma = jnp.where(pair[1:2] > 0.0, pair[0:1] / pair[1:2], 0.0)
    r = b - sigma * w
    g = local[...] - sigma * next_local[...]
    h = image[...] - sigma * next_image[...]
    every = jnp.concatenate(
        [
            total_rows(b * b),
            total_rows(local[...] * image[...]),
            total_rows(r * r),
            total_rows(r * w),
            ww,
            total_rows(g * h),
            total_rows(g * next_image[...]),
            total_rows(next_local[...] * next_image[...]),
            sigma * (1.0 / width),
            jnp.zeros((16 - STATS, lanes), F32),
        ],
        axis=0,
    )
    out = stats.shape[2]
    spread = lax.div(iota((lanes, out), 0), width) == lax.rem(iota((lanes, out), 1), rights)
    sums = grouped(every, spread.astype(F32).astype(BF16))
    mine = lax.div(iota(sums.shape, 1), rights) == iota(sums.shape, 0)
    packed = jnp.sum(jnp.where(mine, sums, 0.0), axis=0, keepdims=True)
    stats[...] = jnp.broadcast_to(packed[None], stats.shape)


def finish_body(
    stats, side_first, side_next, top_first, top_next, scaled, lifted_first, lifted_next,
    interior, side_traces, top_traces
):
    rights = side_traces.shape[1]
    every = stats[:, 0, :]
    lanes = every.shape[1]

    def quantity(index):
        return every if index == 0 else pltpu.roll(every, lanes - index * rights, 1)

    mu0, mu1 = total_rows(quantity(0)), total_rows(quantity(1))
    alpha = mu0 / mu1
    shift = quantity(8) - alpha
    norm = total_rows(quantity(2) + shift * (2.0 * quantity(3) + shift * quantity(4)))
    energy = total_rows(quantity(5) + shift * (2.0 * quantity(6) + shift * quantity(7)))
    beta = norm / mu0
    alpha_next = norm / (energy - beta * norm / alpha)
    diagonal = iota((rights, lanes), 0) == iota((rights, lanes), 1)

    def column(row):
        return jnp.sum(jnp.where(diagonal, row, 0.0), axis=1, keepdims=True)

    first = column(alpha + alpha_next * (1.0 + beta))
    following = column(-alpha_next * alpha)
    side_traces[...] = first[None] * side_first[...] + following[None] * side_next[...]
    top_traces[...] = first[None] * top_first[...] + following[None] * top_next[...]
    block = scaled.shape[0] // rights
    for r in range(rights):
        rows = slice(r * block, (r + 1) * block)
        interior[rows, :] = scaled[rows, :] - (
            first[r : r + 1, :] * lifted_first[rows, :]
            + following[r : r + 1, :] * lifted_next[rows, :]
        )


def per_device(
    source, interior_inverse, coupling, trace_operator, face_ids, orientation, element_scale
):
    nodes, rights, count = source.shape
    traces = trace_operator.shape[0]
    columns = orientation.shape[1]
    face_nodes = traces // columns
    blocks = lax.axis_size("dev")
    layers = lax.axis_size("gz")
    capacity = count // blocks
    owned = 2 * count
    lines = 2 * blocks * capacity
    flat_rows = rights * count
    lanes = rights * face_nodes
    grid_rows = columns * count
    side_rows = (columns - 2) * count
    ids, codes = face_ids.T, orientation.T
    scale = element_scale.reshape(1, count)
    flat_source = source.transpose(1, 2, 0).reshape(flat_rows, nodes)
    grid = ((grid_rows, lanes), F32)
    faces = [((side_rows, lanes), F32), ((count, lanes), F32), ((count, lanes), F32)]
    flat = ((flat_rows, traces), F32)
    whole = ((flat_rows, nodes), F32)
    table = ((grid_rows, 2 * face_nodes), I32)
    message = ((lines, lanes), F32)
    side_shape = ((face_nodes * rights, owned), F32)
    top_shape = ((face_nodes * rights, count), F32)

    def vmem(entry):
        return pltpu.VMEM(*entry)

    def across(message):
        parts = message.reshape(blocks, 2 * capacity, message.shape[1])
        return lax.all_to_all(parts, "dev", 0, 0, tiled=True).reshape(message.shape)

    def climb(value):
        return lax.ppermute(value, "gz", [(at, (at + 1) % layers) for at in range(layers)])

    def sink(value):
        return lax.ppermute(value, "gz", [((at + 1) % layers, at) for at in range(layers)])

    (wishes,) = call(
        functools.partial(wishes_body, owned, capacity), [((lines, owned), I32)], [ids]
    )
    wanted = across(wishes)
    solved, sides, bottom, top, forward, back = call(
        functools.partial(start_body, face_nodes),
        [whole] + faces + [table, table],
        [flat_source, interior_inverse, coupling, codes],
        [vmem(flat), vmem(grid)],
        flops=6 * flat_rows * nodes * (nodes + traces),
    )
    send, chooser = call(
        functools.partial(send_body, owned, capacity),
        [message, ((lines, side_rows), BF16)],
        [ids, wanted, sides],
        flops=4 * lines * side_rows * lanes,
    )
    up, down, received = climb(top), sink(bottom), across(send)
    partner, taker, sorter, lift, high, low, near = call(
        functools.partial(tables_body, owned, capacity),
        [
            ((2, owned, owned), BF16),
            ((side_rows, lines), BF16),
            ((owned, owned), BF16),
            ((2, nodes, traces), BF16),
            ((traces, traces), BF16),
            ((traces, traces), BF16),
            faces[0],
        ],
        [ids, wanted, sides, interior_inverse, coupling, trace_operator],
        flops=6 * nodes * nodes * traces,
    )
    total, local, local_flat, image, sides, bottom, top, send = call(
        apply_body,
        [grid, grid, flat, grid] + faces + [message],
        [sides, near, taker, received, bottom, top, up, down, forward, back, high, low, scale,
         chooser],
        [vmem(flat)],
        flops=6 * flat_rows * traces * traces,
    )
    up, down, received = climb(top), sink(bottom), across(send)
    near, lifted_first, scaled, side_first, top_first = call(
        beside_body,
        [faces[0], whole, whole, side_shape, top_shape],
        [partner, sides, total, local_flat, lift, solved, scale, sorter],
        flops=6 * flat_rows * traces * nodes,
    )
    total_next, next_flat, stats = call(
        stats_body,
        [grid, flat, ((layers * blocks, 1, 128), F32)],
        [sides, near, taker, received, bottom, top, up, down, forward, high, low, scale, total,
         local, image],
        [vmem(grid), vmem(flat), vmem(grid)],
        flops=6 * flat_rows * traces * traces,
    )
    stats = lax.all_to_all(stats, ("gz", "dev"), 0, 0, tiled=True)
    lifted_next, side_next, top_next = call(
        after_body,
        [whole, side_shape, top_shape],
        [total_next, next_flat, lift, sorter],
        flops=6 * flat_rows * traces * nodes,
    )
    side_form = (face_nodes, rights, owned)
    top_form = (face_nodes, rights, count)
    interior, side_traces, top_traces = call(
        finish_body,
        [whole, (side_form, F32), (top_form, F32)],
        [stats, side_first.reshape(side_form), side_next.reshape(side_form),
         top_first.reshape(top_form), top_next.reshape(top_form), scaled, lifted_first,
         lifted_next],
    )
    interior = interior.reshape(rights, count, nodes).transpose(2, 0, 1)
    return (interior, side_traces, top_traces)


def solution(mesh):
    placed = (
        P(None, None, ("gz", "dev")),
        P(),
        P(),
        P(),
        P(("gz", "dev"), None),
        P(("gz", "dev"), None),
        P(("gz", "dev")),
    )
    return jax.shard_map(
        per_device,
        mesh=mesh,
        in_specs=placed,
        out_specs=(
            P(None, None, ("gz", "dev")),
            P(None, None, ("gz", "dev")),
            P(None, None, ("gz", "dev")),
        ),
        check_vma=False,
    )
```

time: 365 us -> 96.3 us (0.26); the launches traced: 359 us -> 94.9 us
  other arithmetic: 105 us -> 0 us
  blocking collectives: 94.6 us -> 0 us
  local copies, waits for them, and re-layouts: 77.2 us -> 46.4 us
  starting transfers between devices: 50.8 us -> 26.9 us
  matrix products: 19.3 us -> 0 us
  Pallas kernels: 0 us -> 18.7 us
  waiting for transfers between devices: 10.2 us -> 2.13 us
    psum x2 -> x0, blocking collectives: 94.6 us -> none  [pair_sums(): lax.psum((inner_owned(vector, vector), inner_owned(vector, image)), ('gz'...]
    scatter-add x12 -> x0, other arithmetic: 56.3 us -> none  [the longest x3 19.7 us: to_faces(): sides = sides.at[:, :, own_slot].add(second, mode='drop')]
    unnamed x118 -> x124, local copies, waits for them, and re-layouts: 18 us -> 46.4 us
    gather x19 -> x0, local copies, waits for them, and re-layouts: 19.7 us -> none  [the longest x3 4.13 us: to_elements(): remote = jnp.take(returned, bucket_read, axis=2)]
    select_n x35 -> x0, other arithmetic: 19.4 us -> none  [the longest x6 5.62 us: orient_traces(): grid = jnp.where(flip_second, grid[:, :, ::-1], grid)]
    dot_general x6 -> x0, matrix products: 19.3 us -> none  [the longest x2 8.58 us: element_operator(): jnp.dot(trace_operator, flat, precision=lax.Precision.HIGHEST, preferred_...]
    pallas_call x0 -> x9, Pallas kernels: none -> 18.7 us  [call(): pl.pallas_call(body, out_shape=[jax.ShapeDtypeStruct(shape, kind) for sha...]
    ppermute x6 -> x4, starting transfers between devices: 18.9 us -> 5.85 us  [the longest x2 2.99 us: climb(): lax.ppermute(value, 'gz', [(at, (at + 1) % layers) for at in range(layers)])]
  transfers between devices with their start and end apart: 13 -> 8, of which waited for: 3 -> 2; matrix products, arithmetic and copies ran while one was open for 33% -> 0% of each run, Pallas kernels for 0% -> 7%
where the time goes in v1:
time: 96.3 us; the launch traced here: 94.9 us
  local copies, waits for them, and re-layouts  46.4 us (48%)
  starting transfers between devices  26.9 us (28%)
  Pallas kernels  18.7 us (19%)
  waiting for transfers between devices  2.13 us (2%)
    unnamed x124, local copies, waits for them, and re-layouts  46.4 us
    pallas_call x9, Pallas kernels, call(): pl.pallas_call(body, out_shape=[jax.ShapeDtypeStruct(shape, kind) for sha...  18.7 us
    all_to_all x3, starting transfers between devices, across(): return lax.all_to_all(parts, 'dev', 0, 0, tiled=True).reshape(message.shape)  16.4 us
    all_to_all x1, starting transfers between devices, per_device(): stats = lax.all_to_all(stats, ('gz', 'dev'), 0, 0, tiled=True)  4.67 us
    ppermute x2, starting transfers between devices, climb(): lax.ppermute(value, 'gz', [(at, (at + 1) % layers) for at in range(layers)])  2.99 us
    ppermute x2, starting transfers between devices, sink(): lax.ppermute(value, 'gz', [((at + 1) % layers, at) for at in range(layers)])  2.86 us
  transfers between devices with their start and end apart: 8, of which 2 were waited for; matrix products, arithmetic and copies ran while one was open for 0% of the time, Pallas kernels for 7%

profile of v1, /device:TPU:0, one launch (start us, length us, event | category | flops | bytes accessed | tf_op | source)
XLA Modules:
  0.0 94.9 jit_solution(18382685150348701208)
XLA Ops:
  2.2 6.5 %all-to-all-start = ((s32[8,16,128]{2,1,0:T(8,128)}), s32[8,16,128]{2,1,0:T(8,128)S(1)}, u32[]{:S(2)}, u32[]{:S(2)}) async-start(s32[8,16,128]{2,1,0:T(8,128)} %bitcast.4), calls=%async_computation | async-start | bytes 131072 | tf_op jit(solution)/shard_map/all_to_all | solution.py:400
  8.7 1.2 %copy-done = f32[512,512]{1,0:T(8,128)S(1)} copy-done((f32[512,512]{1,0:T(8,128)S(1)}, f32[512,512]{1,0:T(8,128)}, u32[]{:S(2)}) %copy-start) | copy-done | bytes 1048600
  9.9 1.1 %copy-done.10 = f32[512,384]{1,0:T(8,128)S(1)} copy-done((f32[512,384]{1,0:T(8,128)S(1)}, f32[512,384]{1,0:T(8,128)}, u32[]{:S(2)}) %copy-start.10) | copy-done | bytes 786456
  11.1 1.2 %copy-done.60 = f32[512,8,64]{0,2,1:T(8,128)S(1)} copy-done((f32[512,8,64]{0,2,1:T(8,128)S(1)}, f32[512,8,64]{0,2,1:T(8,128)}, u32[]{:S(2)}) %copy-start.60) | copy-done | bytes 1048600
  12.3 3.2 %shard_map.94 = (f32[512,512]{1,0:T(8,128)S(1)}, f32[256,512]{1,0:T(8,128)S(1)}, f32[64,512]{1,0:T(8,128)}, f32[64,512]{1,0:T(8,128)}, s32[384,128]{1,0:T(8,128)S(1)}, /*index=5*/s32[384,128]{1,0:T(8,128)S(1)}) custom-call(f32[512,512]{1,0:T(8,128)S(1)} %bitcast.34, f32[512,512]{1,0:T(8,128)S(1)} %copy-done, f32[512,384]{1,0:T(8,128)S(1)} %copy-done.10, ...), custom_call_target="tpu_custom_call" | custom-call | flops 1409286144 | bytes 2885120 | tf_op jit(solution)/shard_map/pallas_call | solution.py:17
  19.5 5.1 %all-to-all-start.1 = ((f32[8,16,512]{2,1,0:T(8,128)}), f32[8,16,512]{2,1,0:T(8,128)S(1)}, u32[]{:S(2)}, u32[]{:S(2)}) async-start(f32[8,16,512]{2,1,0:T(8,128)} %bitcast.6), calls=%async_computation.1 | async-start | bytes 524288 | tf_op jit(solution)/shard_map/all_to_all | solution.py:400
  24.6 1.5 %collective-permute-start = (f32[64,512]{1,0:T(8,128)}, f32[64,512]{1,0:T(8,128)S(1)}, u32[]{:S(2)}, u32[]{:S(2)}) collective-permute-start(f32[64,512]{1,0:T(8,128)} %get-tuple-element.45.top), channel_id=1, source_target_pairs={{0,8},{8,16},{16,24},{24,0},{1,9},{9,17},{17,25},{25,1},{2,10},{10... | collective-permute-start | bytes 393224 | tf_op jit(solution)/shard_map/ppermute | solution.py:403
  26.1 1.4 %collective-permute-start.1 = (f32[64,512]{1,0:T(8,128)}, f32[64,512]{1,0:T(8,128)S(1)}, u32[]{:S(2)}, u32[]{:S(2)}) collective-permute-start(f32[64,512]{1,0:T(8,128)} %get-tuple-element.44.bottom), channel_id=1, source_target_pairs={{8,0},{16,8},{24,16},{0,24},{9,1},{17,9},{25,17},{1,25},{10,2},{18... | collective-permute-start | bytes 393224 | tf_op jit(solution)/shard_map/ppermute | solution.py:406
  27.6 1.1 %copy-done.11 = f32[512,384]{1,0:T(8,128)S(1)} copy-done((f32[512,384]{1,0:T(8,128)S(1)}, f32[512,384]{1,0:T(8,128)}, u32[]{:S(2)}) %copy-start.11) | copy-done | bytes 786456
  29.8 1.2 %shard_map.96 = (bf16[2,128,128]{2,1,0:T(8,128)(2,1)S(1)}, bf16[256,128]{1,0:T(8,128)(2,1)S(1)}, bf16[128,128]{1,0:T(8,128)(2,1)S(1)}, bf16[2,512,384]{2,1,0:T(8...) custom-call(s32[4,64]{1,0:T(4,128)S(1)} %bitcast.30, ...), custom_call_target="tpu_custom_call" | custom-call | flops 603979776 | bytes 3015680 | tf_op jit(solution)/shard_map/pallas_call | solution.py:17
  41.4 4.0 %shard_map.98 = (f32[384,512]{1,0:T(8,128)S(1)}, f32[384,512]{1,0:T(8,128)S(1)}, f32[512,384]{1,0:T(8,128)S(1)}, f32[384,512]{1,0:T(8,128)S(1)}, f32[256,512]{1,...) custom-call(f32[256,512]{1,0:T(8,128)S(1)} %get-tuple-element.40.sides, ...), custom_call_target="tpu_custom_call" | custom-call | flops 452984832 | bytes 3670272 | tf_op jit(solution)/shard_map/pallas_call | solution.py:17
  49.4 4.9 %all-to-all-start.2 = ((f32[8,16,512]{2,1,0:T(8,128)}), f32[8,16,512]{2,1,0:T(8,128)S(1)}, u32[]{:S(2)}, u32[]{:S(2)}) async-start(f32[8,16,512]{2,1,0:T(8,128)} %bitcast.27), calls=%async_computation.2 | async-start | bytes 524288 | tf_op jit(solution)/shard_map/all_to_all | solution.py:400
  54.3 1.5 %collective-permute-start.2 = (f32[64,512]{1,0:T(8,128)}, f32[64,512]{1,0:T(8,128)S(1)}, u32[]{:S(2)}, u32[]{:S(2)}) collective-permute-start(f32[64,512]{1,0:T(8,128)} %get-tuple-element.61.top), channel_id=1, source_target_pairs={{0,8},{8,16},{16,24},{24,0},{1,9},{9,17},{17,25},{25,1},{2,10},{10... | collective-permute-start | bytes 393224 | tf_op jit(solution)/shard_map/ppermute | solution.py:403
  55.8 1.4 %collective-permute-start.3 = (f32[64,512]{1,0:T(8,128)S(1)}, f32[64,512]{1,0:T(8,128)S(1)}, u32[]{:S(2)}, u32[]{:S(2)}) collective-permute-start(f32[64,512]{1,0:T(8,128)S(1)} %copy-done.48), channel_id=1, source_target_pairs={{8,0},{16,8},{24,16},{0,24},{9,1},{17,9},{25,17},{1,25},{10,2},{18... | collective-permute-start | bytes 393224 | tf_op jit(solution)/shard_map/ppermute | solution.py:406
  57.2 1.2 %copy-done.3 = f32[512,512]{1,0:T(8,128)S(1)} copy-done((f32[512,512]{1,0:T(8,128)S(1)}, f32[512,512]{1,0:T(8,128)}, u32[]{:S(2)}) %copy-start.3) | copy-done | bytes 1048600
  58.4 1.1 %copy-done.13 = f32[512,384]{1,0:T(8,128)S(1)} copy-done((f32[512,384]{1,0:T(8,128)S(1)}, f32[512,384]{1,0:T(8,128)}, u32[]{:S(2)}) %copy-start.13) | copy-done | bytes 786456
  59.6 1.4 %shard_map.99 = (f32[256,512]{1,0:T(8,128)S(1)}, f32[512,512]{1,0:T(8,128)S(1)}, f32[512,512]{1,0:T(8,128)S(1)}, f32[512,128]{1,0:T(8,128)S(1)}, f32[512,64]{1,0:T(8,128)S(1)}) custom-call(bf16[2,128,128]{2,1,0:T(8,128)(2,1)S(1)} %copy-done.54, f32[256,512]{1,0:T(8,128)S(1)} %get-tuple-element.51.sides, f32[384,512]{1,0:T(8,128)S(1)} %get-tuple-element.53.total, ...), custom_call_target="tpu_custom_call" | custom-call | flops 603979776 | bytes 4915456 | tf_op jit(solution)/shard_map/pallas_call | solution.py:17
  66.5 1.1 %copy-done.19 = f32[384,512]{1,0:T(8,128)S(1)} copy-done((f32[384,512]{1,0:T(8,128)S(1)}, f32[384,512]{1,0:T(8,128)}, u32[]{:S(2)}) %copy-start.19) | copy-done | bytes 786456
  71.6 4.1 %shard_map.100 = (f32[384,512]{1,0:T(8,128)S(1)}, f32[512,384]{1,0:T(8,128)S(1)}, f32[32,1,128]{2,1,0:T(1,128)}) custom-call(f32[256,512]{1,0:T(8,128)S(1)} %get-tuple-element.51.sides, f32[256,512]{1,0:T(8,128)S(1)} %copy-done.29, bf16[256,128]{1,0:T(8,128)(2,1)S(1)} %get-tuple-element.42.taker, f32[128,512]{1,0:T(8,128)S(1)} %bitcast.20, ...), custom_call_target="tpu_custom_call" | custom-call | flops 452984832 | bytes 5701888 | tf_op jit(solution)/shard_map/pallas_call | solution.py:17
  77.5 4.7 %all-to-all-start.3 = ((f32[32,1,128]{2,1,0:T(1,128)}), f32[32,1,128]{2,1,0:T(1,128)S(1)}, u32[]{:S(2)}, u32[]{:S(2)}) async-start(f32[32,1,128]{2,1,0:T(1,128)} %get-tuple-element.64), calls=%async_computation.3 | async-start | bytes 32768 | tf_op jit(solution)/shard_map/all_to_all | solution.py:463
  84.5 1.2 %shard_map.101 = (f32[512,512]{1,0:T(8,128)S(1)}, f32[512,128]{1,0:T(8,128)S(1)}, f32[512,64]{1,0:T(8,128)S(1)}) custom-call(f32[384,512]{1,0:T(8,128)S(1)} %copy-done.15, f32[512,384]{1,0:T(8,128)S(1)} %copy-done.17, bf16[2,512,384]{2,1,0:T(8,128)(2,1)S(1)} %get-tuple-element.55.lift, bf16[128,128]{1,0:T(8,128)(2,1)S(1)} %copy-done.42), custom_call_target="tpu_custom_call" | custom-call | flops 603979776 | bytes 3211264 | tf_op jit(solution)/shard_map/pallas_call | solution.py:17
  88.0 1.3 %all-to-all-done.3.stats = f32[32,1,128]{2,1,0:T(1,128)S(1)} async-done(((f32[32,1,128]{2,1,0:T(1,128)}), f32[32,1,128]{2,1,0:T(1,128)S(1)}, u32[]{:S(2)}, u32[]{:S(2)}) %all-to-all-start.3) | async-done | bytes 16416 | tf_op jit(solution)/shard_map/all_to_all | solution.py:463
  89.3 1.2 %copy-done.9 = f32[512,512]{1,0:T(8,128)S(1)} copy-done((f32[512,512]{1,0:T(8,128)S(1)}, f32[512,512]{1,0:T(8,128)}, u32[]{:S(2)}) %copy-start.9) | copy-done | bytes 1048600
  93.4 1.5 %shard_map.102 = (f32[512,512]{1,0:T(8,128)}, f32[64,8,128]{2,1,0:T(8,128)}, f32[64,8,64]{2,1,0:T(8,128)}) custom-call(f32[32,1,128]{2,1,0:T(1,128)S(1)} %all-to-all-done.3.stats, f32[64,8,128]{2,1,0:T(8,128)S(1)} %bitcast.23, f32[64,8,128]{2,1,0:T(8,128)S(1)} %bitcast.25, f32[64,8,64]{2,1,0:T(8,128)S(1)} %bitcast.24, f32[64,8,64]{2,1,0:T(8,128)S(1)} %bitcast.26, ...), custom_call_target="tpu_custom_call" | custom-call | bytes 3948544 | tf_op jit(solution)/shard_map/pallas_call | solution.py:17
  (125 shorter events, 39.8 us)
Async XLA Ops:
  2.2 6.5 %copy-start.61 = (s32[64,6]{0,1:T(8,128)S(1)}, s32[64,6]{0,1:T(8,128)}, u32[]{:S(2)}) copy-start(s32[64,6]{0,1:T(8,128)} %param.12) | copy-start | bytes 4612
  2.2 15.6 %all-to-all-start = ((s32[8,16,128]{2,1,0:T(8,128)}), s32[8,16,128]{2,1,0:T(8,128)S(1)}, u32[]{:S(2)}, u32[]{:S(2)}) async-start(s32[8,16,128]{2,1,0:T(8,128)} %bitcast.4), calls=%async_computation | async-start | bytes 131072 | tf_op jit(solution)/shard_map/all_to_all | solution.py:400
  8.7 1.2 %copy-start = (f32[512,512]{1,0:T(8,128)S(1)}, f32[512,512]{1,0:T(8,128)}, u32[]{:S(2)}) copy-start(f32[512,512]{1,0:T(8,128)} %inverse.3) | copy-start | bytes 3145732
  11.1 1.2 %copy-start.60 = (f32[512,8,64]{0,2,1:T(8,128)S(1)}, f32[512,8,64]{0,2,1:T(8,128)}, u32[]{:S(2)}) copy-start(f32[512,8,64]{0,2,1:T(8,128)} %param.7) | copy-start | bytes 3145732
  12.3 5.5 %copy-start.58 = (s32[64,4]{0,1:T(4,128)S(1)}, s32[64,4]{0,1:T(4,128)}, u32[]{:S(2)}) copy-start(s32[64,4]{0,1:T(4,128)} %param.11) | copy-start | bytes 3076
  17.8 9.8 %copy-start.1 = (f32[512,512]{1,0:T(8,128)S(1)}, f32[512,512]{1,0:T(8,128)}, u32[]{:S(2)}) copy-start(f32[512,512]{1,0:T(8,128)} %inverse.3) | copy-start | bytes 3145732
  19.5 15.6 %all-to-all-start.1 = ((f32[8,16,512]{2,1,0:T(8,128)}), f32[8,16,512]{2,1,0:T(8,128)S(1)}, u32[]{:S(2)}, u32[]{:S(2)}) async-start(f32[8,16,512]{2,1,0:T(8,128)} %bitcast.6), calls=%async_computation.1 | async-start | bytes 524288 | tf_op jit(solution)/shard_map/all_to_all | solution.py:400
  24.6 8.4 %collective-permute-start = (f32[64,512]{1,0:T(8,128)}, f32[64,512]{1,0:T(8,128)S(1)}, u32[]{:S(2)}, u32[]{:S(2)}) collective-permute-start(f32[64,512]{1,0:T(8,128)} %get-tuple-element.45.top), channel_id=1, source_target_pairs={{0,8},{8,16},{16,24},{24,0},{1,9},{9,17},{17,25},{25,1},{2,10},{10... | collective-permute-start | bytes 393224 | tf_op jit(solution)/shard_map/ppermute | solution.py:403
  26.1 8.4 %collective-permute-start.1 = (f32[64,512]{1,0:T(8,128)}, f32[64,512]{1,0:T(8,128)S(1)}, u32[]{:S(2)}, u32[]{:S(2)}) collective-permute-start(f32[64,512]{1,0:T(8,128)} %get-tuple-element.44.bottom), channel_id=1, source_target_pairs={{8,0},{16,8},{24,16},{0,24},{9,1},{17,9},{25,17},{1,25},{10,2},{18... | collective-permute-start | bytes 393224 | tf_op jit(solution)/shard_map/ppermute | solution.py:406
  49.4 6.4 %copy-start.48 = (f32[64,512]{1,0:T(8,128)S(1)}, f32[64,512]{1,0:T(8,128)}, u32[]{:S(2)}) copy-start(f32[64,512]{1,0:T(8,128)} %copy-done.47) | copy-start | bytes 393220
  49.4 7.8 %copy-start.42 = (bf16[128,128]{1,0:T(8,128)(2,1)S(1)}, bf16[128,128]{1,0:T(8,128)(2,1)}, u32[]{:S(2)}) copy-start(bf16[128,128]{1,0:T(8,128)(2,1)} %copy-done.41) | copy-start | bytes 98308
  49.4 7.8 %copy-start.54 = (bf16[2,128,128]{2,1,0:T(8,128)(2,1)S(1)}, bf16[2,128,128]{2,1,0:T(8,128)(2,1)}, u32[]{:S(2)}) copy-start(bf16[2,128,128]{2,1,0:T(8,128)(2,1)} %copy-done.53) | copy-start | bytes 196612
  49.4 17.1 %all-to-all-start.2 = ((f32[8,16,512]{2,1,0:T(8,128)}), f32[8,16,512]{2,1,0:T(8,128)S(1)}, u32[]{:S(2)}, u32[]{:S(2)}) async-start(f32[8,16,512]{2,1,0:T(8,128)} %bitcast.27), calls=%async_computation.2 | async-start | bytes 524288 | tf_op jit(solution)/shard_map/all_to_all | solution.py:400
  54.3 10.9 %collective-permute-start.2 = (f32[64,512]{1,0:T(8,128)}, f32[64,512]{1,0:T(8,128)S(1)}, u32[]{:S(2)}, u32[]{:S(2)}) collective-permute-start(f32[64,512]{1,0:T(8,128)} %get-tuple-element.61.top), channel_id=1, source_target_pairs={{0,8},{8,16},{16,24},{24,0},{1,9},{9,17},{17,25},{25,1},{2,10},{10... | collective-permute-start | bytes 393224 | tf_op jit(solution)/shard_map/ppermute | solution.py:403
  55.8 10.1 %collective-permute-start.3 = (f32[64,512]{1,0:T(8,128)S(1)}, f32[64,512]{1,0:T(8,128)S(1)}, u32[]{:S(2)}, u32[]{:S(2)}) collective-permute-start(f32[64,512]{1,0:T(8,128)S(1)} %copy-done.48), channel_id=1, source_target_pairs={{8,0},{16,8},{24,16},{0,24},{9,1},{17,9},{25,17},{1,25},{10,2},{18... | collective-permute-start | bytes 393224 | tf_op jit(solution)/shard_map/ppermute | solution.py:406
  57.2 1.2 %copy-start.3 = (f32[512,512]{1,0:T(8,128)S(1)}, f32[512,512]{1,0:T(8,128)}, u32[]{:S(2)}) copy-start(f32[512,512]{1,0:T(8,128)} %copy-done.2) | copy-start | bytes 3145732
  59.6 6.9 %copy-start.24 = (s32[384,128]{1,0:T(8,128)S(1)}, s32[384,128]{1,0:T(8,128)}, u32[]{:S(2)}) copy-start(s32[384,128]{1,0:T(8,128)} %copy-done.22) | copy-start | bytes 589828
  66.5 1.1 %copy-start.19 = (f32[384,512]{1,0:T(8,128)S(1)}, f32[384,512]{1,0:T(8,128)}, u32[]{:S(2)}) copy-start(f32[384,512]{1,0:T(8,128)} %copy-done.18) | copy-start | bytes 2359300
  77.5 11.8 %all-to-all-start.3 = ((f32[32,1,128]{2,1,0:T(1,128)}), f32[32,1,128]{2,1,0:T(1,128)S(1)}, u32[]{:S(2)}, u32[]{:S(2)}) async-start(f32[32,1,128]{2,1,0:T(1,128)} %get-tuple-element.64), calls=%async_computation.3 | async-start | bytes 32768 | tf_op jit(solution)/shard_map/all_to_all | solution.py:463
  82.2 1.1 %copy-start.15 = (f32[384,512]{1,0:T(8,128)S(1)}, f32[384,512]{1,0:T(8,128)}, u32[]{:S(2)}) copy-start(f32[384,512]{1,0:T(8,128)} %copy-done.14) | copy-start | bytes 2359300
  84.5 4.9 %copy-start.5 = (f32[512,512]{1,0:T(8,128)S(1)}, f32[512,512]{1,0:T(8,128)}, u32[]{:S(2)}) copy-start(f32[512,512]{1,0:T(8,128)} %copy-done.4) | copy-start | bytes 3145732
  84.5 4.9 %copy-start.7 = (f32[512,512]{1,0:T(8,128)S(1)}, f32[512,512]{1,0:T(8,128)}, u32[]{:S(2)}) copy-start(f32[512,512]{1,0:T(8,128)} %copy-done.6) | copy-start | bytes 3145732
  84.5 4.9 %copy-start.31 = (f32[512,128]{1,0:T(8,128)S(1)}, f32[512,128]{1,0:T(8,128)}, u32[]{:S(2)}) copy-start(f32[512,128]{1,0:T(8,128)} %copy-done.30) | copy-start | bytes 786436
  89.3 1.2 %copy-start.9 = (f32[512,512]{1,0:T(8,128)S(1)}, f32[512,512]{1,0:T(8,128)}, u32[]{:S(2)}) copy-start(f32[512,512]{1,0:T(8,128)} %copy-done.8) | copy-start | bytes 3145732
  (46 other events, 39.3 us)

commit v2 on v1

v2 whole, which is shorter than its diff:
```python
import functools
import math

import jax
import jax.numpy as jnp
from jax import lax
from jax.experimental import pallas as pl
from jax.experimental.pallas import tpu as pltpu
from jax.sharding import PartitionSpec as P

F32, BF16, I32 = jnp.float32, jnp.bfloat16, jnp.int32
VMEM_BYTES = 24 * 1024 * 1024
STATS = 9


def far(arg):
    return pltpu.with_memory_space_constraint(arg, pltpu.HBM)


class Raw:
    def __init__(self, arg):
        self.arg = arg


def call(body, outs, args, scratch=(), copies=0, flops=0):
    anywhere, near = pl.BlockSpec(memory_space=pl.ANY), pl.BlockSpec(memory_space=pltpu.VMEM)
    scratch = [pltpu.VMEM(*entry) for entry in scratch]
    if copies:
        scratch.append(pltpu.SemaphoreType.DMA((copies,)))
    specs = [anywhere if isinstance(arg, Raw) else near for arg in args]
    args = [far(arg.arg) if isinstance(arg, Raw) else arg for arg in args]
    return pl.pallas_call(
        body,
        out_shape=[
            pltpu.HBM(*out[:2]) if len(out) > 2 else jax.ShapeDtypeStruct(*out) for out in outs
        ],
        in_specs=specs,
        out_specs=[anywhere if out[2:] == ("raw",) else near for out in outs],
        scratch_shapes=scratch,
        compiler_params=pltpu.CompilerParams(vmem_limit_bytes=VMEM_BYTES),
        cost_estimate=pl.CostEstimate(
            flops=flops, bytes_accessed=sum(arg.size * 4 for arg in args), transcendentals=0
        ),
    )(*args)


def begin(source, target, semaphore):
    copy = pltpu.make_async_copy(source, target, semaphore)
    copy.start()
    return copy


def halves(value):
    high = value.astype(BF16)
    return high, (value - high.astype(F32)).astype(BF16)


def dot(left, right):
    return jnp.dot(left, right, preferred_element_type=F32)


def dot_split(left, right):
    return dot(left[0], right[0]) + (dot(left[1], right[0]) + dot(left[0], right[1]))


def pick(onehot, value):
    high, low = halves(value)
    return dot(onehot, high) + dot(onehot, low)


def iota(shape, axis):
    return lax.broadcasted_iota(I32, shape, axis)


def column_of(row):
    size = row.shape[1]
    mask = iota((size, size), 0) == iota((size, size), 1)
    spread = jnp.where(mask, row.astype(F32), 0.0)
    return jnp.sum(spread, axis=1, keepdims=True).astype(I32)


def swap_blocks(source, target, rows, columns, block):
    low = iota((block, 2 * block), 1) < block
    for r in range(0, rows, 2):
        for c in range(0, columns, 2):
            lanes = slice(c * block, (c + 2) * block)
            first = source[r * block : (r + 1) * block, lanes]
            second = source[(r + 1) * block : (r + 2) * block, lanes]
            lanes = slice(r * block, (r + 2) * block)
            target[c * block : (c + 1) * block, lanes] = jnp.where(
                low, first, pltpu.roll(second, block, 1)
            )
            target[(c + 1) * block : (c + 2) * block, lanes] = jnp.where(
                low, pltpu.roll(first, block, 1), second
            )


def turn(value, table):
    width = table.shape[1]
    return jnp.concatenate(
        [
            jnp.take_along_axis(
                value[:, at : at + width], table, axis=1, mode="promise_in_bounds"
            )
            for at in range(0, value.shape[1], width)
        ],
        axis=1,
    )


def wishes_body(owned, capacity, faces, out, marks, ids, semaphores):
    begin(faces, ids, semaphores.at[0]).wait()
    row = jnp.concatenate([ids[2:3, :], ids[3:4, :]], axis=1)
    owner, slot = lax.div(row, owned), lax.rem(row, owned)
    count = row.shape[1]
    crossing = owner != lax.axis_index("dev")
    same = (column_of(owner) == owner) & (iota((count, count), 0) < iota((count, count), 1))
    rank = jnp.sum(jnp.where(same, 1.0, 0.0), axis=0, keepdims=True).astype(I32)
    first = lax.rem(jnp.concatenate([ids[0:1, :], ids[1:2, :]], axis=1), owned)
    place = jnp.where(crossing, owner * (2 * capacity) + rank, -1)
    here = jnp.where(crossing, -1, slot)
    marks[...] = jnp.concatenate(
        [place, first, here, jnp.zeros((marks.shape[0] - 3, count), I32)], axis=0
    )
    shape = (out.shape[0], count)
    line = iota(shape, 0)
    line = line - jnp.where(lax.rem(line, 2 * capacity) >= capacity, capacity, 0)
    chosen = jnp.where(line == place, (slot + 1).astype(F32), 0.0)
    out[...] = jnp.broadcast_to(
        jnp.sum(chosen, axis=1, keepdims=True).astype(I32), out.shape
    )


def start_body(
    face_nodes, source, inverse, coupling, codes, scales, solved, sides, bottom, top, table,
    source_here, inverse_here, coupling_here, orientation, scale, image, flat, grid, semaphores
):
    small = [begin(codes, orientation, semaphores.at[4]), begin(scales, scale, semaphores.at[5])]
    reads = [
        begin(source, source_here, semaphores.at[0]),
        begin(inverse, inverse_here, semaphores.at[1]),
        begin(coupling, coupling_here, semaphores.at[2]),
    ]
    columns = orientation.shape[0]
    count = orientation.shape[1]
    edge = math.isqrt(face_nodes)
    pair = 2 * face_nodes
    lane = iota((count, pair), 1)
    half = lane - lax.rem(lane, face_nodes)
    node = lax.rem(lane, face_nodes)
    a, b = lax.div(node, edge), lax.rem(node, edge)
    for read in small:
        read.wait()
    scaled = column_of(scale[...]) * (pair * pair)
    for c in range(columns):
        code = jnp.broadcast_to(column_of(orientation[c : c + 1, :]), (count, pair))
        swapped = (code & 4) != 0
        first = (code & 2) != 0
        second = (code & 1) != 0
        i = jnp.where(first, edge - 1 - a, a)
        j = jnp.where(second, edge - 1 - b, b)
        forward = half + jnp.where(swapped, j * edge + i, i * edge + j)
        i, j = jnp.where(swapped, b, a), jnp.where(swapped, a, b)
        i = jnp.where(first, edge - 1 - i, i)
        j = jnp.where(second, edge - 1 - j, j)
        back = half + i * edge + j
        table[c * count : (c + 1) * count, :] = forward + pair * back + scaled
    reads[0].wait()
    reads[1].wait()
    image[...] = dot_split(halves(source_here[...]), halves(inverse_here[...]))
    write = begin(image, solved, semaphores.at[3])
    reads[2].wait()
    flat[...] = dot_split(halves(image[...]), halves(coupling_here[...]))
    swap_blocks(flat, grid, flat.shape[0] // count, columns, count)
    store_faces(grid, table, sides, bottom, top)
    write.wait()


def forward_of(table):
    return lax.rem(table, table.shape[1])


def back_of(table):
    return lax.rem(lax.div(table, table.shape[1]), table.shape[1])


def scale_of(table):
    return lax.div(table, table.shape[1] * table.shape[1]).astype(F32)


def store_faces(grid, table, sides, bottom, top):
    side_count = sides.shape[0]
    count = bottom.shape[0]
    layer = lax.axis_index("gz")
    has_below = (layer > 0).astype(F32)
    has_above = (layer < lax.axis_size("gz") - 1).astype(F32)
    sides[...] = turn(grid[:side_count, :], back_of(table[:side_count, :]))
    below = slice(side_count, side_count + count)
    bottom[...] = turn(grid[below, :], back_of(table[below, :])) * has_below
    above = slice(side_count + count, side_count + 2 * count)
    top[...] = turn(grid[above, :], back_of(table[above, :])) * has_above


def places(capacity, marks, wanted):
    place, first = marks[0:1, :], marks[1:2, :]
    line = iota(wanted.shape, 0)
    named = wanted[...] == first + 1
    later = lax.rem(line, 2 * capacity) >= capacity
    taken = jnp.concatenate([later & named, line == place], axis=1).astype(F32)
    given = jnp.concatenate([~later & named, later & (line - capacity == place)], axis=1)
    return taken, given.astype(F32)


def send_body(capacity, marks, wanted, sides, send):
    taken, _ = places(capacity, marks, wanted)
    send[...] = pick(taken.astype(BF16), sides[...])


class Maps:
    def __init__(self, ref, owned):
        self.ref, self.owned = ref, owned

    def part(self, index, width=1):
        return self.ref[:, index * self.owned : (index + width) * self.owned]

    def message(self, sides):
        return pick(self.part(0, 2), sides)

    def with_partners(self, sides):
        near, far_side = sides[: self.owned, :], sides[self.owned :, :]
        return near + pick(self.part(4), far_side), far_side + pick(self.part(5), near)

    def from_message(self, received):
        high, low = halves(received)
        first, second = self.part(2), self.part(3)
        return dot(first, high) + dot(first, low), dot(second, high) + dot(second, low)

    def by_face(self, sides):
        return pick(self.part(6), sides)


def tables_body(
    owned, capacity, marks, wanted, sides, inverse, coupling, maps, base, lift
):
    taken, given = places(capacity, marks, wanted)
    first, here = marks[1:2, :], marks[2:3, :]
    across = (column_of(first) == here).astype(F32)
    sorter = (iota((owned, owned), 0) == first).astype(F32)
    maps[...] = jnp.concatenate(
        [taken, given[:, :owned].T, given[:, owned:].T, across, across.T, sorter], axis=1
    ).astype(BF16)
    base[:owned, :], base[owned:, :] = Maps(maps, owned).with_partners(sides[...])
    high, low = halves(dot_split(halves(inverse[...]), halves(coupling[...])))
    lift[0] = high
    lift[1] = low


def add_up(base, maps, received, bottom, top, up, down, grid):
    owned = maps.owned
    count = bottom.shape[0]
    first, second = maps.from_message(received[...])
    grid[:owned, :] = base[0] + first
    grid[owned : 2 * owned, :] = base[1] + second
    grid[2 * owned : 2 * owned + count, :] = bottom[...] + up[...]
    grid[2 * owned + count :, :] = top[...] + down[...]


def operate(total, table, operator, read, local, flat, image, count):
    columns = total.shape[0] // count
    rights = flat.shape[0] // count
    local[...] = turn(total[...], forward_of(table[...]))
    swap_blocks(local, flat, columns, rights, count)
    read.wait()
    flat[...] = dot_split(halves(flat[...]), halves(operator[...]))
    swap_blocks(flat, image, rights, columns, count)
    scale = scale_of(table[...])
    image[...] = image[...] * jnp.concatenate([scale] * (rights // 2), axis=1)


def apply_body(
    owned, base, maps, received, bottom, top, up, down, table, operator,
    total_out, sides_out, bottom_out, top_out, send, total, operator_here, grid, flat, semaphores
):
    maps = Maps(maps, owned)
    read = begin(operator, operator_here, semaphores.at[0])
    add_up((base[:owned, :], base[owned:, :]), maps, received, bottom, top, up, down, total)
    write = begin(total, total_out, semaphores.at[1])
    operate(total, table, operator_here, read, grid, flat, grid, bottom.shape[0])
    store_faces(grid, table, sides_out, bottom_out, top_out)
    send[...] = maps.message(sides_out[...])
    write.wait()


def dot_across(left, right):
    return lax.dot_general(left, right, (((1,), (1,)), ((), ())), preferred_element_type=F32)


def lifted(flat, lift):
    high, low = halves(flat)
    return dot_across(high, lift[0]) + (dot_across(low, lift[0]) + dot_across(high, lift[1]))


def store_traces(total, maps, side_traces, top_traces, rights):
    count = top_traces.shape[1]
    sides = maps.by_face(total[: maps.owned, :]).T
    tops = total[total.shape[0] - count :, :].T
    nodes = sides.shape[0] // rights
    for r in range(rights):
        rows = slice(r * nodes, (r + 1) * nodes)
        side_traces[pl.ds(r, nodes, stride=rights), :] = sides[rows, :]
        top_traces[pl.ds(r, nodes, stride=rights), :] = tops[rows, :]


def lift_total(total, table, lift, count, grid, flat):
    grid[...] = turn(total[...], forward_of(table[...]))
    swap_blocks(grid, flat, total.shape[0] // count, flat.shape[0] // count, count)
    return lifted(flat[...], lift)


def beside_body(
    owned, total, table, lift, solved, maps,
    lifted_out, scaled, side_traces, top_traces, grid, flat
):
    count = top_traces.shape[1]
    rights = solved.shape[0] // count
    lifted_out[...] = lift_total(total, table, lift, count, grid, flat)
    scale = jnp.concatenate([scale_of(table[:count, :])] * rights, axis=0)
    copies = solved.shape[1] // scale.shape[1]
    scaled[...] = solved[...] / jnp.concatenate([scale] * copies, axis=1)
    store_traces(total, Maps(maps, owned), side_traces, top_traces, rights)


def after_body(
    owned, total, table, lift, maps, lifted_first, lifted_out, side_traces, top_traces, first_out,
    grid, flat, semaphores
):
    count = top_traces.shape[1]
    read = begin(lifted_first, first_out, semaphores.at[0])
    lifted_out[...] = lift_total(total, table, lift, count, grid, flat)
    store_traces(total, Maps(maps, owned), side_traces, top_traces, flat.shape[0] // count)
    read.wait()


def total_rows(value):
    return jnp.sum(value, axis=0, keepdims=True)


def grouped(rows, group):
    high, rest = halves(rows)
    middle = rest.astype(F32)
    low = (rows - high.astype(F32) - middle).astype(BF16)
    return dot(high, group) + (dot(rest, group) + dot(low, group))


def stats_body(
    owned, sides, maps, received, bottom, top, up, down, table, operator, total_in,
    next_out, stats, total, total_next, operator_here, grid, flat, semaphores
):
    count = bottom.shape[0]
    columns = total.shape[0] // count
    rights = flat.shape[0] // count
    lanes = total.shape[1]
    width = lanes // rights
    maps = Maps(maps, owned)
    read = begin(operator, operator_here, semaphores.at[0])
    read_total = begin(total_in, total, semaphores.at[1])
    add_up(maps.with_partners(sides[...]), maps, received, bottom, top, up, down, total_next)
    write = begin(total_next, next_out, semaphores.at[2])
    operate(total_next, table, operator_here, read, grid, flat, grid, count)
    read_total.wait()
    next_image = turn(grid[...], back_of(table[...]))
    image = jnp.concatenate([sides[...], bottom[...], top[...]], axis=0)
    last = (columns - 1) * count
    b = jnp.concatenate([total[:owned, :], total[last:, :]], axis=0)
    w = jnp.concatenate([total_next[:owned, :], total_next[last:, :]], axis=0)
    group = lax.div(iota((lanes, lanes), 0), width) == lax.div(iota((lanes, lanes), 1), width)
    ww = total_rows(w * w)
    ones = jnp.ones((6, lanes), F32)
    pair = grouped(
        jnp.concatenate([total_rows(b * w), ww, ones], axis=0), group.astype(F32).astype(BF16)
    )
    sigma = jnp.where(pair[1:2] > 0.0, pair[0:1] / pair[1:2], 0.0)
    r = b - sigma * w
    g = total[...] - sigma * total_next[...]
    h = image - sigma * next_image
    every = jnp.concatenate(
        [
            total_rows(b * b),
            total_rows(total[...] * image),
            total_rows(r * r),
            total_rows(r * w),
            ww,
            total_rows(g * h),
            total_rows(g * next_image),
            total_rows(total_next[...] * next_image),
            sigma * (1.0 / width),
            jnp.zeros((16 - STATS, lanes), F32),
        ],
        axis=0,
    )
    out = stats.shape[2]
    spread = lax.div(iota((lanes, out), 0), width) == lax.rem(iota((lanes, out), 1), rights)
    sums = grouped(every, spread.astype(F32).astype(BF16))
    mine = lax.div(iota(sums.shape, 1), rights) == iota(sums.shape, 0)
    packed = jnp.sum(jnp.where(mine, sums, 0.0), axis=0, keepdims=True)
    stats[...] = jnp.broadcast_to(packed[None], stats.shape)
    write.wait()


def finish_body(
    stats, side_first, side_next, top_first, top_next, scaled, lifted_first, lifted_next,
    interior, side_traces, top_traces, scaled_here, side_here, top_here, semaphores
):
    rights = side_traces.shape[1]
    block = scaled.shape[0] // rights
    parts = [pl.ds(r * block, block) for r in range(rights)]
    reads = [
        begin(scaled.at[part], scaled_here.at[part], semaphores.at[r])
        for r, part in enumerate(parts)
    ]
    reads.append(begin(side_first, side_here, semaphores.at[rights]))
    reads.append(begin(top_first, top_here, semaphores.at[rights + 1]))
    every = stats[:, 0, :]
    lanes = every.shape[1]

    def quantity(index):
        return every if index == 0 else pltpu.roll(every, lanes - index * rights, 1)

    mu0, mu1 = total_rows(quantity(0)), total_rows(quantity(1))
    alpha = mu0 / mu1
    shift = quantity(8) - alpha
    norm = total_rows(quantity(2) + shift * (2.0 * quantity(3) + shift * quantity(4)))
    energy = total_rows(quantity(5) + shift * (2.0 * quantity(6) + shift * quantity(7)))
    beta = norm / mu0
    alpha_next = norm / (energy - beta * norm / alpha)
    diagonal = iota((rights, lanes), 0) == iota((rights, lanes), 1)

    def column(row):
        return jnp.sum(jnp.where(diagonal, row, 0.0), axis=1, keepdims=True)

    first = column(alpha + alpha_next * (1.0 + beta))
    following = column(-alpha_next * alpha)
    writes = []
    for r, part in enumerate(parts):
        reads[r].wait()
        scaled_here[part, :] = scaled_here[part, :] - (
            first[r : r + 1, :] * lifted_first[part, :]
            + following[r : r + 1, :] * lifted_next[part, :]
        )
        writes.append(begin(scaled_here.at[part], interior.at[part], semaphores.at[rights + 2 + r]))
    reads[rights].wait()
    side_here[...] = first[None] * side_here[...] + following[None] * side_next[...]
    writes.append(begin(side_here, side_traces, semaphores.at[2 * rights + 2]))
    reads[rights + 1].wait()
    top_here[...] = first[None] * top_here[...] + following[None] * top_next[...]
    writes.append(begin(top_here, top_traces, semaphores.at[2 * rights + 3]))
    for write in writes:
        write.wait()


def per_device(
    source, interior_inverse, coupling, trace_operator, face_ids, orientation, element_scale
):
    nodes, rights, count = source.shape
    traces = trace_operator.shape[0]
    columns = orientation.shape[1]
    face_nodes = traces // columns
    blocks = lax.axis_size("dev")
    layers = lax.axis_size("gz")
    capacity = count // blocks
    owned = 2 * count
    lines = 2 * blocks * capacity
    flat_rows = rights * count
    lanes = rights * face_nodes
    grid_rows = columns * count
    side_rows = (columns - 2) * count
    ids, codes = face_ids.T, orientation.T
    scale = element_scale.reshape(1, count)
    flat_source = source.transpose(1, 2, 0).reshape(flat_rows, nodes)
    grid = ((grid_rows, lanes), F32)
    faces = [((side_rows, lanes), F32), ((count, lanes), F32), ((count, lanes), F32)]
    flat = ((flat_rows, traces), F32)
    whole = ((flat_rows, nodes), F32)
    table = ((grid_rows, 2 * face_nodes), I32)
    message = ((lines, lanes), F32)
    side_shape = ((face_nodes * rights, owned), F32)
    top_shape = ((face_nodes * rights, count), F32)

    def across(message):
        parts = message.reshape(blocks, 2 * capacity, message.shape[1])
        return lax.all_to_all(parts, "dev", 0, 0, tiled=True).reshape(message.shape)

    def climb(value):
        return lax.ppermute(value, "gz", [(at, (at + 1) % layers) for at in range(layers)])

    def sink(value):
        return lax.ppermute(value, "gz", [((at + 1) % layers, at) for at in range(layers)])

    wishes, marks = call(
        functools.partial(wishes_body, owned, capacity),
        [((lines, owned), I32), ((8, owned), I32)],
        [Raw(ids)],
        [(ids.shape, I32)],
        copies=1,
    )
    wanted = across(wishes)
    solved, sides, bottom, top, table = call(
        functools.partial(start_body, face_nodes),
        [whole + ("raw",)] + faces + [table],
        [Raw(flat_source), Raw(interior_inverse), Raw(coupling), Raw(codes), Raw(scale)],
        [whole, ((nodes, nodes), F32), ((nodes, traces), F32), (codes.shape, I32),
         (scale.shape, I32), whole, flat, grid],
        copies=6,
        flops=6 * flat_rows * nodes * (nodes + traces),
    )
    (send,) = call(
        functools.partial(send_body, capacity),
        [message],
        [marks, wanted, sides],
        flops=4 * lines * side_rows * lanes,
    )
    up, down, received = climb(top), sink(bottom), across(send)
    maps, base, lift = call(
        functools.partial(tables_body, owned, capacity),
        [((lines, 7 * owned), BF16), faces[0], ((2, nodes, traces), BF16, "far")],
        [marks, wanted, sides, far(interior_inverse), far(coupling)],
        flops=6 * nodes * nodes * traces,
    )
    square = ((traces, traces), F32)
    total, sides, bottom, top, send = call(
        functools.partial(apply_body, owned),
        [grid + ("raw",)] + faces + [message],
        [base, maps, received, bottom, top, up, down, table, Raw(trace_operator)],
        [grid, square, grid, flat],
        copies=2,
        flops=6 * flat_rows * traces * traces,
    )
    up, down, received = climb(top), sink(bottom), across(send)
    lifted_first, scaled, side_first, top_first = call(
        functools.partial(beside_body, owned),
        [whole + ("far",), whole + ("far",), side_shape + ("far",), top_shape + ("far",)],
        [far(total), table, far(lift), far(solved), maps],
        [grid, flat],
        flops=6 * flat_rows * traces * nodes,
    )
    total_next, stats = call(
        functools.partial(stats_body, owned),
        [grid + ("raw",), ((layers * blocks, 1, 128), F32)],
        [sides, maps, received, bottom, top, up, down, table, Raw(trace_operator),
         Raw(total)],
        [grid, grid, square, grid, flat],
        copies=3,
        flops=6 * flat_rows * traces * traces,
    )
    stats = lax.all_to_all(stats, ("gz", "dev"), 0, 0, tiled=True)
    lifted_next, side_next, top_next, lifted_first = call(
        functools.partial(after_body, owned),
        [whole, side_shape, top_shape, whole],
        [far(total_next), table, far(lift), maps, Raw(lifted_first)],
        [grid, flat],
        copies=1,
        flops=6 * flat_rows * traces * nodes,
    )
    side_form = ((face_nodes, rights, owned), F32)
    top_form = ((face_nodes, rights, count), F32)
    interior, side_traces, top_traces = call(
        finish_body,
        [whole + ("raw",), side_form + ("raw",), top_form + ("raw",)],
        [stats, Raw(side_first.reshape(side_form[0])), side_next.reshape(side_form[0]),
         Raw(top_first.reshape(top_form[0])), top_next.reshape(top_form[0]), Raw(scaled),
         lifted_first, lifted_next],
        [whole, side_form, top_form],
        copies=2 * rights + 4,
    )
    interior = interior.reshape(rights, count, nodes).transpose(2, 0, 1)
    return (interior, side_traces, top_traces)


def solution(mesh):
    placed = (
        P(None, None, ("gz", "dev")),
        P(),
        P(),
        P(),
        P(("gz", "dev"), None),
        P(("gz", "dev"), None),
        P(("gz", "dev")),
    )
    return jax.shard_map(
        per_device,
        mesh=mesh,
        in_specs=placed,
        out_specs=(
            P(None, None, ("gz", "dev")),
            P(None, None, ("gz", "dev")),
            P(None, None, ("gz", "dev")),
        ),
        check_vma=False,
    )
```

time: 96.3 us -> 65.5 us (0.68)
  local copies, waits for them, and re-layouts: 46.4 us -> 0 us
  Pallas kernels: 18.7 us -> 28.6 us
  waiting for transfers between devices: 2.13 us -> 12 us
  starting transfers between devices: 26.9 us -> 23.7 us
    unnamed x124 -> x0, local copies, waits for them, and re-layouts: 46.4 us -> none
    pallas_call x9, Pallas kernels: 18.7 us -> 28.6 us  [call(): pl.pallas_call(body, out_shape=[pltpu.HBM(*out[:2]) if len(out) > 2 else...]
    ppermute x2, waiting for transfers between devices: 0.01 us -> 5.1 us  [climb(): lax.ppermute(value, 'gz', [(at, (at + 1) % layers) for at in range(layers)])]
    all_to_all x3, waiting for transfers between devices: 0.01 us -> 2.73 us  [across(): return lax.all_to_all(parts, 'dev', 0, 0, tiled=True).reshape(message.shape)]
    all_to_all x1, waiting for transfers between devices: 1.28 us -> 3.87 us  [per_device(): stats = lax.all_to_all(stats, ('gz', 'dev'), 0, 0, tiled=True)]
    ppermute x2, starting transfers between devices: 2.99 us -> 0.6 us  [climb(): lax.ppermute(value, 'gz', [(at, (at + 1) % layers) for at in range(layers)])]
    all_to_all x3, starting transfers between devices: 16.4 us -> 14.6 us  [across(): return lax.all_to_all(parts, 'dev', 0, 0, tiled=True).reshape(message.shape)]
    ppermute x2, starting transfers between devices: 2.86 us -> 3.87 us  [sink(): lax.ppermute(value, 'gz', [((at + 1) % layers, at) for at in range(layers)])]
  transfers between devices with their start and end apart: 8 -> 8, of which waited for: 2 -> 7; matrix products, arithmetic and copies ran while one was open for 0% -> 0% of each run, Pallas kernels for 7% -> 25%
where the time goes in v2:
time: 65.5 us; the launch traced here: 64.9 us
  Pallas kernels  28.6 us (44%)
  starting transfers between devices  23.7 us (36%)
  waiting for transfers between devices  12 us (18%)
  between operations  0.69 us (1%)
    pallas_call x9, Pallas kernels, call(): pl.pallas_call(body, out_shape=[pltpu.HBM(*out[:2]) if len(out) > 2 else...  28.6 us
    all_to_all x3, starting transfers between devices, across(): return lax.all_to_all(parts, 'dev', 0, 0, tiled=True).reshape(message.shape)  14.6 us
    ppermute x2, waiting for transfers between devices, climb(): lax.ppermute(value, 'gz', [(at, (at + 1) % layers) for at in range(layers)])  5.1 us
    all_to_all x1, starting transfers between devices, per_device(): stats = lax.all_to_all(stats, ('gz', 'dev'), 0, 0, tiled=True)  4.64 us
    ppermute x2, starting transfers between devices, sink(): lax.ppermute(value, 'gz', [((at + 1) % layers, at) for at in range(layers)])  3.87 us
    all_to_all x1, waiting for transfers between devices, per_device(): stats = lax.all_to_all(stats, ('gz', 'dev'), 0, 0, tiled=True)  3.87 us
    all_to_all x3, waiting for transfers between devices, across(): return lax.all_to_all(parts, 'dev', 0, 0, tiled=True).reshape(message.shape)  2.73 us
  transfers between devices with their start and end apart: 8, of which 7 were waited for; matrix products, arithmetic and copies ran while one was open for 0% of the time, Pallas kernels for 25%

profile of v2, /device:TPU:0, one launch (start us, length us, event | category | flops | bytes accessed | tf_op | source)
XLA Modules:
  0.0 64.9 jit_solution(5089012181147644181)
XLA Ops:
  0.6 1.6 %shard_map.94 = (s32[128,128]{1,0:T(8,128)}, s32[8,128]{1,0:T(8,128)S(1)}) custom-call(s32[4,64]{1,0:T(4,128)} %bitcast.27), custom_call_target="tpu_custom_call" | custom-call | bytes 1024 | tf_op jit(solution)/shard_map/pallas_call | solution.py:32
  2.3 6.3 %all-to-all-start = ((s32[8,16,128]{2,1,0:T(8,128)}), s32[8,16,128]{2,1,0:T(8,128)S(1)}, u32[]{:S(2)}, u32[]{:S(2)}) async-start(s32[8,16,128]{2,1,0:T(8,128)} %bitcast.1), calls=%async_computation | async-start | bytes 131072 | tf_op jit(solution)/shard_map/all_to_all | solution.py:491
  8.6 4.3 %shard_map.95 = (f32[512,512]{1,0:T(8,128)}, f32[256,512]{1,0:T(8,128)S(1)}, f32[64,512]{1,0:T(8,128)S(1)}, f32[64,512]{1,0:T(8,128)S(1)}, s32[384,128]{1,0:T(8,128)S(1)}) custom-call(f32[512,512]{1,0:T(8,128)} %bitcast.28, f32[512,512]{1,0:T(8,128)} %inverse.3, f32[512,384]{1,0:T(8,128)} %coupling.3, s32[6,64]{1,0:T(8,128)} %bitcast.30, s32[1,64]{1,0:T(1,128)} %bitcast.31), custom_call_target="tpu_custom_call" | custom-call | flops 1409286144 | bytes 2885376 | tf_op jit(solution)/shard_map/pallas_call | solution.py:32
  12.9 1.6 %all-to-all-done = s32[8,16,128]{2,1,0:T(8,128)S(1)} async-done(((s32[8,16,128]{2,1,0:T(8,128)}), s32[8,16,128]{2,1,0:T(8,128)S(1)}, u32[]{:S(2)}, u32[]{:S(2)}) %all-to-all-start) | async-done | bytes 65568 | tf_op jit(solution)/shard_map/all_to_all | solution.py:491
  14.5 1.0 %shard_map.97 = f32[128,512]{1,0:T(8,128)} custom-call(s32[8,128]{1,0:T(8,128)S(1)} %get-tuple-element.31.marks, s32[128,128]{1,0:T(8,128)S(1)} %bitcast.21, f32[256,512]{1,0:T(8,128)S(1)} %get-tuple-element.33.sides), custom_call_target="tpu_custom_call" | custom-call | flops 67108864 | bytes 593920 | tf_op jit(solution)/shard_map/pallas_call | solution.py:32
  15.5 3.5 %all-to-all-start.1 = ((f32[8,16,512]{2,1,0:T(8,128)}), f32[8,16,512]{2,1,0:T(8,128)S(1)}, u32[]{:S(2)}, u32[]{:S(2)}) async-start(f32[8,16,512]{2,1,0:T(8,128)} %bitcast.7), calls=%async_computation.1 | async-start | bytes 524288 | tf_op jit(solution)/shard_map/all_to_all | solution.py:491
  19.0 2.4 %collective-permute-start.1 = (f32[64,512]{1,0:T(8,128)S(1)}, f32[64,512]{1,0:T(8,128)S(1)}, u32[]{:S(2)}, u32[]{:S(2)}) collective-permute-start(f32[64,512]{1,0:T(8,128)S(1)} %get-tuple-element.36.bottom), channel_id=1, source_target_pairs={{8,0},{16,8},{24,16},{0,24},{9,1},{17,9},{25,17},{1,25},{10,2},{18... | collective-permute-start | bytes 393224 | tf_op jit(solution)/shard_map/ppermute | solution.py:497
  21.4 3.6 %shard_map.96 = (bf16[128,896]{1,0:T(8,128)(2,1)S(1)}, f32[256,512]{1,0:T(8,128)S(1)}, bf16[2,512,384]{2,1,0:T(8,128)(2,1)}) custom-call(s32[8,128]{1,0:T(8,128)S(1)} %get-tuple-element.31.marks, s32[128,128]{1,0:T(8,128)S(1)} %bitcast.22, f32[256,512]{1,0:T(8,128)S(1)} %get-tuple-element.33.sides, f32[512,512]{1,0:T(8,128)} %inverse.3, f32[512,384]{1,0:T(8,128)} %coupling.3), custom_call_target="tpu_custom_call" | custom-call | flops 603979776 | bytes 2428928 | tf_op jit(solution)/shard_map/pallas_call | solution.py:32
  25.0 0.3 collective-permute-done.1.down
  25.3 3.4 %collective-permute-done.up = f32[64,512]{1,0:T(8,128)S(1)} collective-permute-done((f32[64,512]{1,0:T(8,128)S(1)}, f32[64,512]{1,0:T(8,128)S(1)}, u32[]{:S(2)}, u32[]{:S(2)}) %collective-permute-start) | collective-permute-done | bytes 131104 | tf_op jit(solution)/shard_map/ppermute | solution.py:494
  28.7 0.1 all-to-all-done.1
  28.7 3.5 %shard_map.98 = (f32[384,512]{1,0:T(8,128)}, f32[256,512]{1,0:T(8,128)S(1)}, f32[64,512]{1,0:T(8,128)S(1)}, f32[64,512]{1,0:T(8,128)S(1)}, f32[128,512]{1,0:T(8,128)}) custom-call(f32[256,512]{1,0:T(8,128)S(1)} %get-tuple-element.34.base, bf16[128,896]{1,0:T(8,128)(2,1)S(1)} %get-tuple-element.35.maps, f32[128,512]{1,0:T(8,128)S(1)} %bitcast.20, ...), custom_call_target="tpu_custom_call" | custom-call | flops 452984832 | bytes 2555904 | tf_op jit(solution)/shard_map/pallas_call | solution.py:32
  32.3 4.7 %all-to-all-start.2 = ((f32[8,16,512]{2,1,0:T(8,128)}), f32[8,16,512]{2,1,0:T(8,128)S(1)}, u32[]{:S(2)}, u32[]{:S(2)}) async-start(f32[8,16,512]{2,1,0:T(8,128)} %bitcast.9), calls=%async_computation.2 | async-start | bytes 524288 | tf_op jit(solution)/shard_map/all_to_all | solution.py:491
  36.9 1.4 %collective-permute-start.3 = (f32[64,512]{1,0:T(8,128)S(1)}, f32[64,512]{1,0:T(8,128)S(1)}, u32[]{:S(2)}, u32[]{:S(2)}) collective-permute-start(f32[64,512]{1,0:T(8,128)S(1)} %get-tuple-element.41.bottom), channel_id=1, source_target_pairs={{8,0},{16,8},{24,16},{0,24},{9,1},{17,9},{25,17},{1,25},{10,2},{18... | collective-permute-start | bytes 393224 | tf_op jit(solution)/shard_map/ppermute | solution.py:497
  38.4 0.6 collective-permute-start.2
  39.0 4.9 %shard_map.100 = (f32[512,512]{1,0:T(8,128)}, f32[512,512]{1,0:T(8,128)}, f32[512,128]{1,0:T(8,128)}, f32[512,64]{1,0:T(8,128)}) custom-call(f32[384,512]{1,0:T(8,128)} %get-tuple-element.43.total_in.total, s32[384,128]{1,0:T(8,128)S(1)} %get-tuple-element.38.table, bf16[2,512,384]{2,1,0:T(8,128)(2,1)} %get-tuple-element.45.lift, ...), custom_call_target="tpu_custom_call" | custom-call | flops 603979776 | bytes 4063232 | tf_op jit(solution)/shard_map/pallas_call | solution.py:32
  43.9 0.0 collective-permute-done.3.down
  43.9 1.7 %collective-permute-done.2.up = f32[64,512]{1,0:T(8,128)S(1)} collective-permute-done((f32[64,512]{1,0:T(8,128)S(1)}, f32[64,512]{1,0:T(8,128)S(1)}, u32[]{:S(2)}, u32[]{:S(2)}) %collective-permute-start.2) | collective-permute-done | bytes 131104 | tf_op jit(solution)/shard_map/ppermute | solution.py:494
  45.6 1.1 %all-to-all-done.2 = f32[8,16,512]{2,1,0:T(8,128)S(1)} async-done(((f32[8,16,512]{2,1,0:T(8,128)}), f32[8,16,512]{2,1,0:T(8,128)S(1)}, u32[]{:S(2)}, u32[]{:S(2)}) %all-to-all-start.2) | async-done | bytes 262176 | tf_op jit(solution)/shard_map/all_to_all | solution.py:491
  46.7 4.1 %shard_map.99 = (f32[384,512]{1,0:T(8,128)}, f32[32,1,128]{2,1,0:T(1,128)}) custom-call(f32[256,512]{1,0:T(8,128)S(1)} %get-tuple-element.39.sides, bf16[128,896]{1,0:T(8,128)(2,1)S(1)} %get-tuple-element.35.maps, f32[128,512]{1,0:T(8,128)S(1)} %bitcast.19, f32[64,512]{1,0:T(8,128)S(1)} %get-tuple-element.41.bottom, f32[64,512]{1,0:T(8,128)S(1)} %get-tuple-element.42.top, ...), custom_call_target="tpu_custom_call" | custom-call | flops 452984832 | bytes 3342336 | tf_op jit(solution)/shard_map/pallas_call | solution.py:32
  50.8 4.6 %all-to-all-start.3 = ((f32[32,1,128]{2,1,0:T(1,128)}), f32[32,1,128]{2,1,0:T(1,128)S(1)}, u32[]{:S(2)}, u32[]{:S(2)}) async-start(f32[32,1,128]{2,1,0:T(1,128)} %get-tuple-element.44), calls=%async_computation.3 | async-start | bytes 32768 | tf_op jit(solution)/shard_map/all_to_all | solution.py:555
  55.4 3.2 %shard_map.101 = (f32[512,512]{1,0:T(8,128)S(1)}, f32[512,128]{1,0:T(8,128)S(1)}, f32[512,64]{1,0:T(8,128)S(1)}, f32[512,512]{1,0:T(8,128)S(1)}) custom-call(f32[384,512]{1,0:T(8,128)} %get-tuple-element.48.total, s32[384,128]{1,0:T(8,128)S(1)} %get-tuple-element.38.table, bf16[2,512,384]{2,1,0:T(8,128)(2,1)} %get-tuple-element.45.lift, ...), custom_call_target="tpu_custom_call" | custom-call | flops 603979776 | bytes 4063232 | tf_op jit(solution)/shard_map/pallas_call | solution.py:32
  58.6 3.9 %all-to-all-done.3.stats = f32[32,1,128]{2,1,0:T(1,128)S(1)} async-done(((f32[32,1,128]{2,1,0:T(1,128)}), f32[32,1,128]{2,1,0:T(1,128)S(1)}, u32[]{:S(2)}, u32[]{:S(2)}) %all-to-all-start.3) | async-done | bytes 16416 | tf_op jit(solution)/shard_map/all_to_all | solution.py:555
  62.5 2.4 %shard_map.102 = (f32[512,512]{1,0:T(8,128)}, f32[64,8,128]{2,1,0:T(8,128)}, f32[64,8,64]{2,1,0:T(8,128)}) custom-call(f32[32,1,128]{2,1,0:T(1,128)S(1)} %all-to-all-done.3.stats, f32[64,8,128]{2,1,0:T(8,128)} %bitcast.25, f32[64,8,128]{2,1,0:T(8,128)S(1)} %bitcast.23, f32[64,8,64]{2,1,0:T(8,128)} %bitcast.26, f32[64,8,64]{2,1,0:T(8,128)S(1)} %bitcast.24, ...), custom_call_target="tpu_custom_call" | custom-call | bytes 3948544 | tf_op jit(solution)/shard_map/pallas_call | solution.py:32
  (1 shorter events, 0.0 us)
Async XLA Ops:
  2.3 12.3 %all-to-all-start = ((s32[8,16,128]{2,1,0:T(8,128)}), s32[8,16,128]{2,1,0:T(8,128)S(1)}, u32[]{:S(2)}, u32[]{:S(2)}) async-start(s32[8,16,128]{2,1,0:T(8,128)} %bitcast.1), calls=%async_computation | async-start | bytes 131072 | tf_op jit(solution)/shard_map/all_to_all | solution.py:491
  15.5 13.3 %all-to-all-start.1 = ((f32[8,16,512]{2,1,0:T(8,128)}), f32[8,16,512]{2,1,0:T(8,128)S(1)}, u32[]{:S(2)}, u32[]{:S(2)}) async-start(f32[8,16,512]{2,1,0:T(8,128)} %bitcast.7), calls=%async_computation.1 | async-start | bytes 524288 | tf_op jit(solution)/shard_map/all_to_all | solution.py:491
  19.0 6.3 %collective-permute-start.1 = (f32[64,512]{1,0:T(8,128)S(1)}, f32[64,512]{1,0:T(8,128)S(1)}, u32[]{:S(2)}, u32[]{:S(2)}) collective-permute-start(f32[64,512]{1,0:T(8,128)S(1)} %get-tuple-element.36.bottom), channel_id=1, source_target_pairs={{8,0},{16,8},{24,16},{0,24},{9,1},{17,9},{25,17},{1,25},{10,2},{18... | collective-permute-start | bytes 393224 | tf_op jit(solution)/shard_map/ppermute | solution.py:497
  21.4 7.2 %collective-permute-start = (f32[64,512]{1,0:T(8,128)S(1)}, f32[64,512]{1,0:T(8,128)S(1)}, u32[]{:S(2)}, u32[]{:S(2)}) collective-permute-start(f32[64,512]{1,0:T(8,128)S(1)} %get-tuple-element.37.top), channel_id=1, source_target_pairs={{0,8},{8,16},{16,24},{24,0},{1,9},{9,17},{17,25},{25,1},{2,10},{10... | collective-permute-start | bytes 393224 | tf_op jit(solution)/shard_map/ppermute | solution.py:494
  32.3 14.4 %all-to-all-start.2 = ((f32[8,16,512]{2,1,0:T(8,128)}), f32[8,16,512]{2,1,0:T(8,128)S(1)}, u32[]{:S(2)}, u32[]{:S(2)}) async-start(f32[8,16,512]{2,1,0:T(8,128)} %bitcast.9), calls=%async_computation.2 | async-start | bytes 524288 | tf_op jit(solution)/shard_map/all_to_all | solution.py:491
  36.9 6.9 %collective-permute-start.3 = (f32[64,512]{1,0:T(8,128)S(1)}, f32[64,512]{1,0:T(8,128)S(1)}, u32[]{:S(2)}, u32[]{:S(2)}) collective-permute-start(f32[64,512]{1,0:T(8,128)S(1)} %get-tuple-element.41.bottom), channel_id=1, source_target_pairs={{8,0},{16,8},{24,16},{0,24},{9,1},{17,9},{25,17},{1,25},{10,2},{18... | collective-permute-start | bytes 393224 | tf_op jit(solution)/shard_map/ppermute | solution.py:497
  38.4 7.2 %collective-permute-start.2 = (f32[64,512]{1,0:T(8,128)S(1)}, f32[64,512]{1,0:T(8,128)S(1)}, u32[]{:S(2)}, u32[]{:S(2)}) collective-permute-start(f32[64,512]{1,0:T(8,128)S(1)} %get-tuple-element.42.top), channel_id=1, source_target_pairs={{0,8},{8,16},{16,24},{24,0},{1,9},{9,17},{17,25},{25,1},{2,10},{10... | collective-permute-start | bytes 393224 | tf_op jit(solution)/shard_map/ppermute | solution.py:494
  50.8 11.7 %all-to-all-start.3 = ((f32[32,1,128]{2,1,0:T(1,128)}), f32[32,1,128]{2,1,0:T(1,128)S(1)}, u32[]{:S(2)}, u32[]{:S(2)}) async-start(f32[32,1,128]{2,1,0:T(1,128)} %get-tuple-element.44), calls=%async_computation.3 | async-start | bytes 32768 | tf_op jit(solution)/shard_map/all_to_all | solution.py:555

commit v3 on v2

v3 whole, which is shorter than its diff:
```python
import functools
import math

import jax
import jax.numpy as jnp
from jax import lax
from jax.experimental import pallas as pl
from jax.experimental.pallas import tpu as pltpu
from jax.sharding import PartitionSpec as P

F32, BF16, I32 = jnp.float32, jnp.bfloat16, jnp.int32
VMEM_BYTES = 24 * 1024 * 1024
STATS = 9


def far(arg):
    return pltpu.with_memory_space_constraint(arg, pltpu.HBM)


class Raw:
    def __init__(self, arg):
        self.arg = arg


def call(body, outs, args, scratch=(), copies=0, flops=0):
    anywhere, near = pl.BlockSpec(memory_space=pl.ANY), pl.BlockSpec(memory_space=pltpu.VMEM)
    scratch = [pltpu.VMEM(*entry) for entry in scratch]
    if copies:
        scratch.append(pltpu.SemaphoreType.DMA((copies,)))
    specs = [anywhere if isinstance(arg, Raw) else near for arg in args]
    args = [far(arg.arg) if isinstance(arg, Raw) else arg for arg in args]
    return pl.pallas_call(
        body,
        out_shape=[
            pltpu.HBM(*out[:2]) if len(out) > 2 else jax.ShapeDtypeStruct(*out) for out in outs
        ],
        in_specs=specs,
        out_specs=[anywhere if out[2:] == ("raw",) else near for out in outs],
        scratch_shapes=scratch,
        compiler_params=pltpu.CompilerParams(vmem_limit_bytes=VMEM_BYTES),
        cost_estimate=pl.CostEstimate(
            flops=flops, bytes_accessed=sum(arg.size * 4 for arg in args), transcendentals=0
        ),
    )(*args)


def begin(source, target, semaphore):
    copy = pltpu.make_async_copy(source, target, semaphore)
    copy.start()
    return copy


def halves(value):
    high = value.astype(BF16)
    return high, (value - high.astype(F32)).astype(BF16)


def dot(left, right):
    return jnp.dot(left, right, preferred_element_type=F32)


def dot_split(left, right):
    rows = left[0].shape[0]
    both = dot(jnp.concatenate(left, axis=0), right[0])
    return both[:rows, :] + (both[rows:, :] + dot(left[0], right[1]))


def pick(onehot, value):
    high, low = halves(value)
    return dot(onehot, high) + dot(onehot, low)


def iota(shape, axis):
    return lax.broadcasted_iota(I32, shape, axis)


def column_of(row):
    size = row.shape[1]
    mask = iota((size, size), 0) == iota((size, size), 1)
    spread = jnp.where(mask, row.astype(F32), 0.0)
    return jnp.sum(spread, axis=1, keepdims=True).astype(I32)


def gather_lanes(value, table):
    return jnp.take_along_axis(value, table, axis=1, mode="promise_in_bounds")


def flip_halves(value):
    return pltpu.roll(value, value.shape[1] // 2, 1)


def lower_half(value):
    return iota(value.shape, 1) < value.shape[1] // 2


def to_flat(total, table, flat, count, pairs):
    width = table.shape[1]
    for c in range(0, total.shape[0] // count, 2):
        rows = slice(c * count, (c + 1) * count)
        rows_next = slice((c + 1) * count, (c + 2) * count)
        forward, forward_next = forward_of(table[rows, :]), forward_of(table[rows_next, :])
        for pair in pairs:
            lanes = slice(pair * width, (pair + 1) * width)
            first = gather_lanes(total[rows, lanes], forward)
            second = gather_lanes(total[rows_next, lanes], forward_next)
            low = lower_half(first)
            at = 2 * pair * count
            lanes = slice(c // 2 * width, (c // 2 + 1) * width)
            flat[at : at + count, lanes] = jnp.where(low, first, second)
            flat[at + count : at + 2 * count, lanes] = flip_halves(jnp.where(low, second, first))


def from_flat(flat, table, placed, count, pairs, columns):
    width = table.shape[1]
    for c in columns[::2]:
        back = back_of(table[c * count : (c + 1) * count, :])
        back_next = back_of(table[(c + 1) * count : (c + 2) * count, :])
        for pair in pairs:
            at = 2 * pair * count
            lanes = slice(c // 2 * width, (c // 2 + 1) * width)
            first = flat[at : at + count, lanes]
            second = flip_halves(flat[at + count : at + 2 * count, lanes])
            low = lower_half(first)
            lanes = slice(pair * width, (pair + 1) * width)
            placed(c, lanes, gather_lanes(jnp.where(low, first, second), back))
            placed(c + 1, lanes, gather_lanes(jnp.where(low, second, first), back_next))


def wishes_body(owned, capacity, faces, out, marks, ids, semaphores):
    begin(faces, ids, semaphores.at[0]).wait()
    row = jnp.concatenate([ids[2:3, :], ids[3:4, :]], axis=1)
    owner, slot = lax.div(row, owned), lax.rem(row, owned)
    count = row.shape[1]
    crossing = owner != lax.axis_index("dev")
    same = (column_of(owner) == owner) & (iota((count, count), 0) < iota((count, count), 1))
    rank = jnp.sum(jnp.where(same, 1.0, 0.0), axis=0, keepdims=True).astype(I32)
    first = lax.rem(jnp.concatenate([ids[0:1, :], ids[1:2, :]], axis=1), owned)
    place = jnp.where(crossing, owner * (2 * capacity) + rank, -1)
    here = jnp.where(crossing, -1, slot)
    marks[...] = jnp.concatenate(
        [place, first, here, jnp.zeros((marks.shape[0] - 3, count), I32)], axis=0
    )
    shape = (out.shape[0], count)
    line = iota(shape, 0)
    line = line - jnp.where(lax.rem(line, 2 * capacity) >= capacity, capacity, 0)
    chosen = jnp.where(line == place, (slot + 1).astype(F32), 0.0)
    out[...] = jnp.broadcast_to(
        jnp.sum(chosen, axis=1, keepdims=True).astype(I32), out.shape
    )


def start_body(
    face_nodes, source, inverse, coupling, codes, scales, solved, sides, bottom, top, table,
    source_here, inverse_here, coupling_here, orientation, scale, image, flat, semaphores
):
    small = [begin(codes, orientation, semaphores.at[4]), begin(scales, scale, semaphores.at[5])]
    reads = [
        begin(source, source_here, semaphores.at[0]),
        begin(inverse, inverse_here, semaphores.at[1]),
        begin(coupling, coupling_here, semaphores.at[2]),
    ]
    columns = orientation.shape[0]
    count = orientation.shape[1]
    edge = math.isqrt(face_nodes)
    pair = 2 * face_nodes
    lane = iota((count, pair), 1)
    half = lane - lax.rem(lane, face_nodes)
    node = lax.rem(lane, face_nodes)
    a, b = lax.div(node, edge), lax.rem(node, edge)
    for read in small:
        read.wait()
    scaled = column_of(scale[...]) * (pair * pair)
    for c in range(columns):
        turned = half if c % 2 == 0 else face_nodes - half
        code = jnp.broadcast_to(column_of(orientation[c : c + 1, :]), (count, pair))
        swapped = (code & 4) != 0
        first = (code & 2) != 0
        second = (code & 1) != 0
        i = jnp.where(first, edge - 1 - a, a)
        j = jnp.where(second, edge - 1 - b, b)
        forward = turned + jnp.where(swapped, j * edge + i, i * edge + j)
        i, j = jnp.where(swapped, b, a), jnp.where(swapped, a, b)
        i = jnp.where(first, edge - 1 - i, i)
        j = jnp.where(second, edge - 1 - j, j)
        back = turned + i * edge + j
        table[c * count : (c + 1) * count, :] = forward + pair * back + scaled
    has_below, has_above = layer_masks()
    side_columns = columns - 2

    def placed(column, lanes, value):
        if column < side_columns:
            sides[column * count : (column + 1) * count, lanes] = value
        elif column == side_columns:
            bottom[:, lanes] = value * has_below
        else:
            top[:, lanes] = value * has_above

    reads[0].wait()
    reads[1].wait()
    pairs = sides.shape[1] // pair
    parts = [range(0, pairs // 2), range(pairs // 2, pairs)]
    split = halves(inverse_here[...])
    split_coupling = None
    for part in parts:
        rows = slice(2 * part[0] * count, 2 * (part[-1] + 1) * count)
        image[rows, :] = dot_split(halves(source_here[rows, :]), split)
        if split_coupling is None:
            reads[2].wait()
            split_coupling = halves(coupling_here[...])
        flat[rows, :] = dot_split(halves(image[rows, :]), split_coupling)
    write = begin(image, solved, semaphores.at[3])
    for part in parts:
        from_flat(flat, table, placed, count, part, range(columns))
    write.wait()


def forward_of(table):
    return table & (table.shape[1] - 1)


def back_of(table):
    bits = table.shape[1].bit_length() - 1
    return (table >> bits) & (table.shape[1] - 1)


def scale_of(table):
    bits = table.shape[1].bit_length() - 1
    return (table >> (2 * bits)).astype(F32)


def places(capacity, marks, wanted):
    place, first = marks[0:1, :], marks[1:2, :]
    line = iota(wanted.shape, 0)
    named = wanted[...] == first + 1
    later = lax.rem(line, 2 * capacity) >= capacity
    taken = jnp.concatenate([later & named, line == place], axis=1).astype(F32)
    given = jnp.concatenate([~later & named, later & (line - capacity == place)], axis=1)
    return taken, given.astype(F32)


def send_body(capacity, marks, wanted, sides, send):
    taken, _ = places(capacity, marks, wanted)
    send[...] = pick(taken.astype(BF16), sides[...])


class Maps:
    def __init__(self, ref, owned):
        self.ref, self.owned = ref, owned

    def part(self, index, width=1):
        return self.ref[:, index * self.owned : (index + width) * self.owned]

    def message(self, sides):
        return pick(self.part(0, 2), sides)

    def with_partners(self, sides):
        near, far_side = sides[: self.owned, :], sides[self.owned :, :]
        return near + pick(self.part(4), far_side), far_side + pick(self.part(5), near)

    def from_message(self, received):
        return pick(self.part(2), received), pick(self.part(3), received)

    def by_face(self, sides):
        return pick(self.part(6), sides)


def tables_body(
    owned, capacity, marks, wanted, sides, inverse, coupling, operator, maps, base, lift, split
):
    taken, given = places(capacity, marks, wanted)
    first, here = marks[1:2, :], marks[2:3, :]
    across = (column_of(first) == here).astype(F32)
    sorter = (iota((owned, owned), 0) == first).astype(F32)
    maps[...] = jnp.concatenate(
        [taken, given[:, :owned].T, given[:, owned:].T, across, across.T, sorter], axis=1
    ).astype(BF16)
    base[:owned, :], base[owned:, :] = Maps(maps, owned).with_partners(sides[...])
    high, low = halves(dot_split(halves(inverse[...]), halves(coupling[...])))
    lift[0] = high
    lift[1] = low
    split[0], split[1] = halves(operator[...])


def add_up(base, maps, received, bottom, top, up, down, total):
    owned = maps.owned
    count = bottom.shape[0]
    total[2 * owned : 2 * owned + count, :] = bottom[...] + up[...]
    total[2 * owned + count :, :] = top[...] + down[...]
    first, second = maps.from_message(received[...])
    total[:owned, :] = base[:owned, :] + first
    total[owned : 2 * owned, :] = base[owned : 2 * owned, :] + second


def own_faces(total, owned, count):
    return jnp.concatenate([total[:owned, :], total[total.shape[0] - count :, :]], axis=0)


def operate(total, table, split, flat, image, count, turned):
    pairs = total.shape[1] // table.shape[1]
    scale = scale_of(table[:count, :])
    scale = jnp.concatenate([scale] * (flat.shape[1] // scale.shape[1]), axis=1)
    parts = [range(0, pairs // 2), range(pairs // 2, pairs)]
    for part in parts:
        to_flat(total, table, flat, count, part)
        rows = slice(2 * part[0] * count, 2 * (part[-1] + 1) * count)
        turned(pl.ds(rows.start, rows.stop - rows.start))
        product = dot_split(halves(flat[rows, :]), (split[0], split[1]))
        image[rows, :] = product * jnp.concatenate([scale] * (product.shape[0] // count), axis=0)
    return parts


def layer_masks():
    layer = lax.axis_index("gz")
    return (layer > 0).astype(F32), (layer < lax.axis_size("gz") - 1).astype(F32)


def apply_body(
    owned, base, maps, received, bottom, top, up, down, table, split,
    mine, flat_out, sides_out, bottom_out, top_out, send,
    total, mine_here, flat, image, message, semaphores
):
    count = bottom.shape[0]
    maps = Maps(maps, owned)
    add_up(base, maps, received, bottom, top, up, down, total)
    mine_here[...] = own_faces(total, owned, count)
    writes = [begin(mine_here, mine, semaphores.at[0])]
    has_below, has_above = layer_masks()
    columns = total.shape[0] // count
    side_columns = columns - 2

    def placed(column, lanes, value):
        if column < side_columns:
            sides_out[column * count : (column + 1) * count, lanes] = value
        elif column == side_columns:
            bottom_out[:, lanes] = value * has_below
        else:
            top_out[:, lanes] = value * has_above

    def turned(rows):
        writes.append(begin(flat.at[rows], flat_out.at[rows], semaphores.at[len(writes)]))

    parts = operate(total, table, split, flat, image, count, turned)
    for part in parts:
        from_flat(image, table, placed, count, part, range(side_columns))
        lanes = slice(part[0] * table.shape[1], (part[-1] + 1) * table.shape[1])
        message[:, lanes] = maps.message(sides_out[:, lanes])
        writes.append(
            begin(message.at[:, lanes], send.at[:, lanes], semaphores.at[len(writes)])
        )
    for part in parts:
        from_flat(image, table, placed, count, part, range(side_columns, columns))
    for write in writes:
        write.wait()


def dot_across(left, right):
    return lax.dot_general(left, right, (((1,), (1,)), ((), ())), preferred_element_type=F32)


def lifted(flat, lift):
    high, low = halves(flat)
    return dot_across(high, lift[0]) + (dot_across(low, lift[0]) + dot_across(high, lift[1]))


def store_traces(mine, maps, side_traces, top_traces, rights):
    sides = maps.by_face(mine[: maps.owned, :]).T
    tops = mine[maps.owned :, :].T
    nodes = sides.shape[0] // rights
    for r in range(rights):
        rows = slice(r * nodes, (r + 1) * nodes)
        side_traces[pl.ds(r, nodes, stride=rights), :] = sides[rows, :]
        top_traces[pl.ds(r, nodes, stride=rights), :] = tops[rows, :]


def by_right(rows, rights):
    width = 2 * rows.shape[1] // rights
    low = iota((1, width), 1) < width // 2
    tiles = [rows[:, at : at + width] for at in range(0, rows.shape[1], width)]
    return [jnp.where(low == (r % 2 == 0), tiles[r // 2], 0.0) for r in range(rights)]


def beside_body(
    owned, mine, flat, table, lift, solved, maps, sides, bottom, top,
    lifted_out, scaled, side_traces, top_traces, image_out, base, known, shifts,
    placed, image, semaphores
):
    count = top_traces.shape[1]
    rights = solved.shape[0] // count
    maps = Maps(maps, owned)
    placed[: 2 * owned, :] = sides[...]
    placed[2 * owned : 2 * owned + count, :] = bottom[...]
    placed[2 * owned + count :, :] = top[...]
    to_flat(placed, table, image, count, range(rights // 2))
    write = begin(image, image_out, semaphores.at[0])
    first, second = maps.with_partners(sides[...])
    base[:owned, :], base[owned:, :] = first, second
    inside = jnp.sum(maps.part(4).astype(F32), axis=1, keepdims=True)
    b, w = mine[:owned, :], first * inside
    lanes = mine.shape[1]
    width = lanes // rights
    group = lax.div(iota((lanes, lanes), 0), width) == lax.div(iota((lanes, lanes), 1), width)
    rows = [total_rows(b * w), total_rows(w * w), jnp.ones((6, lanes), F32)]
    pair = grouped(jnp.concatenate(rows, axis=0), group.astype(F32).astype(BF16))
    sigma = jnp.where(pair[1:2] > 0.0, pair[0:1] / pair[1:2], 0.0)
    tile = 2 * width
    spread = []
    for r in range(rights):
        piece = sigma[:, r // 2 * tile : (r // 2 + 1) * tile]
        low = lower_half(piece) == (r % 2 == 0)
        spread.append(jnp.where(low, piece, flip_halves(piece)))
    spread = jnp.concatenate(spread, axis=0)
    shifts[...] = jnp.broadcast_to(sigma, shifts.shape)
    known[...] = jnp.concatenate(
        by_right(total_rows(mine[...] * mine[...]), rights)
        + [
            flat_sums(flat[at : at + count, :] * image[at : at + count, :], tile)
            for at in range(0, flat.shape[0], count)
        ]
        + [jnp.where(iota(spread.shape, 1) == 0, spread, 0.0), spread],
        axis=0,
    )
    lifted_out[...] = lifted(flat[...], lift)
    scale = jnp.concatenate([scale_of(table[:count, :])] * rights, axis=0)
    copies = solved.shape[1] // scale.shape[1]
    scaled[...] = solved[...] / jnp.concatenate([scale] * copies, axis=1)
    store_traces(mine, maps, side_traces, top_traces, rights)
    write.wait()


def after_body(
    owned, mine, flat, lift, maps, lifted_first, lifted_out, side_traces, top_traces, first_out,
    semaphores
):
    count = top_traces.shape[1]
    read = begin(lifted_first, first_out, semaphores.at[0])
    lifted_out[...] = lifted(flat[...], lift)
    store_traces(mine, Maps(maps, owned), side_traces, top_traces, flat.shape[0] // count)
    read.wait()


def total_rows(value):
    return jnp.sum(value, axis=0, keepdims=True)


def grouped(rows, group):
    high, rest = halves(rows)
    middle = rest.astype(F32)
    low = (rows - high.astype(F32) - middle).astype(BF16)
    return dot(high, group) + (dot(rest, group) + dot(low, group))


def fold(value):
    return jnp.sum(value.reshape(value.shape[0] // 8, 8, value.shape[1]), axis=0)


def flat_sums(value, tile):
    value = fold(value)
    parts = [value[:, at : at + tile] for at in range(0, value.shape[1], tile)]
    return total_rows(functools.reduce(jnp.add, parts))


def stats_body(
    owned, base, maps, received, bottom, top, up, down, table, split, known, shifts, mine_in,
    flat_in, image_in, next_mine_out, next_flat_out, stats,
    total_next, mine, flat, image, next_mine, next_flat, next_image, semaphores
):
    count = bottom.shape[0]
    rights = flat.shape[0] // count
    reads = [
        begin(mine_in, mine, semaphores.at[0]),
        begin(flat_in, flat, semaphores.at[1]),
        begin(image_in, image, semaphores.at[2]),
    ]
    maps = Maps(maps, owned)
    add_up(base, maps, received, bottom, top, up, down, total_next)
    next_mine[...] = own_faces(total_next, owned, count)
    writes = [begin(next_mine, next_mine_out, semaphores.at[3])]

    def turned(rows):
        writes.append(
            begin(next_flat.at[rows], next_flat_out.at[rows], semaphores.at[3 + len(writes)])
        )

    operate(total_next, table, split, next_flat, next_image, count, turned)
    for read in reads:
        read.wait()
    sigma = shifts[0:1, :]
    rr = rw = ww = 0.0
    for at in range(0, mine.shape[0], count):
        w = next_mine[at : at + count, :]
        r = mine[at : at + count, :] - sigma * w
        rr, rw, ww = rr + fold(r * r), rw + fold(r * w), ww + fold(w * w)
    rows = []
    for part in (rr, rw, ww):
        rows += by_right(total_rows(part), rights)
    tile = stats.shape[2]
    gh, gz, lz = [], [], []
    for r in range(rights):
        part = slice(r * count, (r + 1) * count)
        shift = known[3 * rights + r : 3 * rights + r + 1, :]
        shift = jnp.concatenate([shift] * (flat.shape[1] // tile), axis=1)
        after, z = next_flat[part, :], next_image[part, :]
        g, h = flat[part, :] - shift * after, image[part, :] - shift * z
        gh.append(flat_sums(g * h, tile))
        gz.append(flat_sums(g * z, tile))
        lz.append(flat_sums(after * z, tile))
    rows = jnp.concatenate(
        [known[: 2 * rights, :]]
        + rows + gh + gz + lz
        + [known[2 * rights : 3 * rights, :], jnp.zeros((tile - STATS * rights, tile), F32)],
        axis=0,
    )
    high, low = halves(rows)
    rest = (rows - high.astype(F32) - low.astype(F32)).astype(BF16)
    ones = jnp.ones((8, tile), BF16)
    sums = dot_across(ones, high) + (dot_across(ones, low) + dot_across(ones, rest))
    stats[...] = jnp.broadcast_to(sums[0:1, :][None], stats.shape)
    for write in writes:
        write.wait()


def finish_body(
    stats, side_first, side_next, top_first, top_next, scaled, lifted_first, lifted_next,
    interior, side_traces, top_traces,
    scaled_here, side_here, side_next_here, top_here, top_next_here, semaphores
):
    rights = side_traces.shape[1]
    block = scaled.shape[0] // rights
    parts = [pl.ds(r * block, block) for r in range(rights)]
    reads = [
        begin(scaled.at[part], scaled_here.at[part], semaphores.at[r])
        for r, part in enumerate(parts)
    ]
    traces = (
        (side_first, side_here), (side_next, side_next_here), (top_first, top_here),
        (top_next, top_next_here),
    )
    for k, (source, target) in enumerate(traces):
        reads.append(begin(source, target, semaphores.at[rights + k]))
    every = stats[:, 0, :]
    lanes = every.shape[1]

    def quantity(index):
        return every if index == 0 else pltpu.roll(every, lanes - index * rights, 1)

    mu0, mu1 = total_rows(quantity(0)), total_rows(quantity(1))
    alpha = mu0 / mu1
    shift = quantity(8) - alpha
    norm = total_rows(quantity(2) + shift * (2.0 * quantity(3) + shift * quantity(4)))
    energy = total_rows(quantity(5) + shift * (2.0 * quantity(6) + shift * quantity(7)))
    beta = norm / mu0
    alpha_next = norm / (energy - beta * norm / alpha)
    diagonal = iota((rights, lanes), 0) == iota((rights, lanes), 1)

    def column(row):
        return jnp.sum(jnp.where(diagonal, row, 0.0), axis=1, keepdims=True)

    first = column(alpha + alpha_next * (1.0 + beta))
    following = column(-alpha_next * alpha)
    writes = []
    for r, part in enumerate(parts):
        reads[r].wait()
        scaled_here[part, :] = scaled_here[part, :] - (
            first[r : r + 1, :] * lifted_first[part, :]
            + following[r : r + 1, :] * lifted_next[part, :]
        )
        writes.append(begin(scaled_here.at[part], interior.at[part], semaphores.at[rights + 4 + r]))
    for k, (here, next_here, out) in enumerate(
        ((side_here, side_next_here, side_traces), (top_here, top_next_here, top_traces))
    ):
        reads[rights + 2 * k].wait()
        reads[rights + 2 * k + 1].wait()
        here[...] = first[None] * here[...] + following[None] * next_here[...]
        writes.append(begin(here, out, semaphores.at[2 * rights + 4 + k]))
    for write in writes:
        write.wait()


def per_device(
    source, interior_inverse, coupling, trace_operator, face_ids, orientation, element_scale
):
    nodes, rights, count = source.shape
    traces = trace_operator.shape[0]
    columns = orientation.shape[1]
    face_nodes = traces // columns
    blocks = lax.axis_size("dev")
    layers = lax.axis_size("gz")
    capacity = count // blocks
    owned = 2 * count
    lines = 2 * blocks * capacity
    flat_rows = rights * count
    lanes = rights * face_nodes
    grid_rows = columns * count
    side_rows = (columns - 2) * count
    ids, codes = face_ids.T, orientation.T
    scale = element_scale.reshape(1, count)
    flat_source = source.transpose(1, 2, 0).reshape(flat_rows, nodes)
    grid = ((grid_rows, lanes), F32)
    faces = [((side_rows, lanes), F32), ((count, lanes), F32), ((count, lanes), F32)]
    flat = ((flat_rows, traces), F32)
    whole = ((flat_rows, nodes), F32)
    table = ((grid_rows, 2 * face_nodes), I32)
    message = ((lines, lanes), F32)
    side_shape = ((face_nodes * rights, owned), F32)
    top_shape = ((face_nodes * rights, count), F32)

    def across(message):
        parts = message.reshape(blocks, 2 * capacity, message.shape[1])
        return lax.all_to_all(parts, "dev", 0, 0, tiled=True).reshape(message.shape)

    def climb(value):
        return lax.ppermute(value, "gz", [(at, (at + 1) % layers) for at in range(layers)])

    def sink(value):
        return lax.ppermute(value, "gz", [((at + 1) % layers, at) for at in range(layers)])

    wishes, marks = call(
        functools.partial(wishes_body, owned, capacity),
        [((lines, owned), I32), ((8, owned), I32)],
        [Raw(ids)],
        [(ids.shape, I32)],
        copies=1,
    )
    wanted = across(wishes)
    solved, sides, bottom, top, table = call(
        functools.partial(start_body, face_nodes),
        [whole + ("raw",)] + faces + [table],
        [Raw(flat_source), Raw(interior_inverse), Raw(coupling), Raw(codes), Raw(scale)],
        [whole, ((nodes, nodes), F32), ((nodes, traces), F32), (codes.shape, I32),
         (scale.shape, I32), whole, flat],
        copies=6,
        flops=6 * flat_rows * nodes * (nodes + traces),
    )
    (send,) = call(
        functools.partial(send_body, capacity),
        [message],
        [marks, wanted, sides],
        flops=4 * lines * side_rows * lanes,
    )
    up, down, received = climb(top), sink(bottom), across(send)
    square = ((2, traces, traces), BF16)
    maps, base, lift, split = call(
        functools.partial(tables_body, owned, capacity),
        [
            ((lines, 7 * owned), BF16),
            faces[0],
            ((2, nodes, traces), BF16, "far"),
            square,
        ],
        [marks, wanted, sides, far(interior_inverse), far(coupling), far(trace_operator)],
        flops=6 * nodes * nodes * traces,
    )
    mine = ((owned + count, lanes), F32)
    own, local, sides, bottom, top, send = call(
        functools.partial(apply_body, owned),
        [mine + ("raw",), flat + ("raw",)] + faces + [message + ("raw",)],
        [base, maps, received, bottom, top, up, down, table, split],
        [grid, mine, flat, flat, message],
        copies=5,
        flops=6 * flat_rows * traces * traces,
    )
    up, down, received = climb(top), sink(bottom), across(send)
    lifted_first, scaled, side_first, top_first, image, base, known, shifts = call(
        functools.partial(beside_body, owned),
        [whole + ("far",), whole + ("far",), side_shape + ("far",), top_shape + ("far",),
         flat + ("raw",), faces[0], ((4 * rights, 2 * face_nodes), F32), ((8, lanes), F32)],
        [far(own), far(local), table, far(lift), far(solved), maps, sides, bottom, top],
        [grid, flat],
        copies=1,
        flops=6 * flat_rows * traces * nodes,
    )
    own, local, stats = call(
        functools.partial(stats_body, owned),
        [mine + ("raw",), flat + ("raw",), ((layers * blocks, 1, 2 * face_nodes), F32)],
        [base, maps, received, bottom, top, up, down, table, split, known, shifts,
         Raw(own), Raw(local), Raw(image)],
        [grid, mine, flat, flat, mine, flat, flat],
        copies=6,
        flops=6 * flat_rows * traces * traces,
    )
    stats = lax.all_to_all(stats, ("gz", "dev"), 0, 0, tiled=True)
    lifted_next, side_next, top_next, lifted_first = call(
        functools.partial(after_body, owned),
        [whole, side_shape + ("far",), top_shape + ("far",), whole],
        [far(own), far(local), far(lift), maps, Raw(lifted_first)],
        copies=1,
        flops=6 * flat_rows * traces * nodes,
    )
    side_form = ((face_nodes, rights, owned), F32)
    top_form = ((face_nodes, rights, count), F32)
    interior, side_traces, top_traces = call(
        finish_body,
        [whole + ("raw",), side_form + ("raw",), top_form + ("raw",)],
        [stats, Raw(side_first.reshape(side_form[0])), Raw(side_next.reshape(side_form[0])),
         Raw(top_first.reshape(top_form[0])), Raw(top_next.reshape(top_form[0])), Raw(scaled),
         lifted_first, lifted_next],
        [whole, side_form, side_form, top_form, top_form],
        copies=2 * rights + 6,
    )
    interior = interior.reshape(rights, count, nodes).transpose(2, 0, 1)
    return (interior, side_traces, top_traces)


def solution(mesh):
    placed = (
        P(None, None, ("gz", "dev")),
        P(),
        P(),
        P(),
        P(("gz", "dev"), None),
        P(("gz", "dev"), None),
        P(("gz", "dev")),
    )
    return jax.shard_map(
        per_device,
        mesh=mesh,
        in_specs=placed,
        out_specs=(
            P(None, None, ("gz", "dev")),
            P(None, None, ("gz", "dev")),
            P(None, None, ("gz", "dev")),
        ),
        check_vma=False,
    )
```

time: 65.5 us -> 63.6 us (0.971)
  waiting for transfers between devices: 12 us -> 9.12 us
  starting transfers between devices: 23.7 us -> 25 us
    ppermute x2, waiting for transfers between devices: 5.1 us -> 0.35 us  [climb(): lax.ppermute(value, 'gz', [(at, (at + 1) % layers) for at in range(layers)])]
    ppermute x2, starting transfers between devices: 0.6 us -> 3.03 us  [climb(): lax.ppermute(value, 'gz', [(at, (at + 1) % layers) for at in range(layers)])]
    ppermute x2, waiting for transfers between devices: 0.26 us -> 2.41 us  [sink(): lax.ppermute(value, 'gz', [((at + 1) % layers, at) for at in range(layers)])]
    ppermute x2, starting transfers between devices: 3.87 us -> 2.88 us  [sink(): lax.ppermute(value, 'gz', [((at + 1) % layers, at) for at in range(layers)])]
  transfers between devices with their start and end apart: 8 -> 8, of which waited for: 7 -> 6; matrix products, arithmetic and copies ran while one was open for 0% -> 0% of each run, Pallas kernels for 25% -> 28%
where the time goes in v3:
time: 63.6 us; the launch traced here: 62.9 us
  Pallas kernels  28.1 us (44%)
  starting transfers between devices  25 us (39%)
  waiting for transfers between devices  9.12 us (14%)
  between operations  0.72 us (1%)
    pallas_call x9, Pallas kernels, call(): pl.pallas_call(body, out_shape=[pltpu.HBM(*out[:2]) if len(out) > 2 else...  28.1 us
    all_to_all x3, starting transfers between devices, across(): return lax.all_to_all(parts, 'dev', 0, 0, tiled=True).reshape(message.shape)  14.4 us
    all_to_all x1, starting transfers between devices, per_device(): stats = lax.all_to_all(stats, ('gz', 'dev'), 0, 0, tiled=True)  4.63 us
    all_to_all x1, waiting for transfers between devices, per_device(): stats = lax.all_to_all(stats, ('gz', 'dev'), 0, 0, tiled=True)  3.54 us
    ppermute x2, starting transfers between devices, climb(): lax.ppermute(value, 'gz', [(at, (at + 1) % layers) for at in range(layers)])  3.03 us
    ppermute x2, starting transfers between devices, sink(): lax.ppermute(value, 'gz', [((at + 1) % layers, at) for at in range(layers)])  2.88 us
    all_to_all x3, waiting for transfers between devices, across(): return lax.all_to_all(parts, 'dev', 0, 0, tiled=True).reshape(message.shape)  2.82 us
    ppermute x2, waiting for transfers between devices, sink(): lax.ppermute(value, 'gz', [((at + 1) % layers, at) for at in range(layers)])  2.41 us
  transfers between devices with their start and end apart: 8, of which 6 were waited for; matrix products, arithmetic and copies ran while one was open for 0% of the time, Pallas kernels for 28%

profile of v3, /device:TPU:0, one launch (start us, length us, event | category | flops | bytes accessed | tf_op | source)
XLA Modules:
  0.0 62.9 jit_solution(6805401743893753636)
XLA Ops:
  0.6 1.6 %shard_map.94 = (s32[128,128]{1,0:T(8,128)}, s32[8,128]{1,0:T(8,128)S(1)}) custom-call(s32[4,64]{1,0:T(4,128)} %bitcast.28), custom_call_target="tpu_custom_call" | custom-call | bytes 1024 | tf_op jit(solution)/shard_map/pallas_call | solution.py:32
  2.3 6.3 %all-to-all-start = ((s32[8,16,128]{2,1,0:T(8,128)}), s32[8,16,128]{2,1,0:T(8,128)S(1)}, u32[]{:S(2)}, u32[]{:S(2)}) async-start(s32[8,16,128]{2,1,0:T(8,128)} %bitcast.1), calls=%async_computation | async-start | bytes 131072 | tf_op jit(solution)/shard_map/all_to_all | solution.py:609
  8.6 4.2 %shard_map.95 = (f32[512,512]{1,0:T(8,128)}, f32[256,512]{1,0:T(8,128)S(1)}, f32[64,512]{1,0:T(8,128)S(1)}, f32[64,512]{1,0:T(8,128)S(1)}, s32[384,128]{1,0:T(8,128)S(1)}) custom-call(f32[512,512]{1,0:T(8,128)} %bitcast.29, f32[512,512]{1,0:T(8,128)} %inverse.3, f32[512,384]{1,0:T(8,128)} %coupling.3, s32[6,64]{1,0:T(8,128)} %bitcast.31, s32[1,64]{1,0:T(1,128)} %bitcast.32), custom_call_target="tpu_custom_call" | custom-call | flops 1409286144 | bytes 2885376 | tf_op jit(solution)/shard_map/pallas_call | solution.py:32
  12.8 1.7 %all-to-all-done = s32[8,16,128]{2,1,0:T(8,128)S(1)} async-done(((s32[8,16,128]{2,1,0:T(8,128)}), s32[8,16,128]{2,1,0:T(8,128)S(1)}, u32[]{:S(2)}, u32[]{:S(2)}) %all-to-all-start) | async-done | bytes 65568 | tf_op jit(solution)/shard_map/all_to_all | solution.py:609
  14.5 1.0 %shard_map.97 = f32[128,512]{1,0:T(8,128)} custom-call(s32[8,128]{1,0:T(8,128)S(1)} %get-tuple-element.38.marks, s32[128,128]{1,0:T(8,128)S(1)} %bitcast.21, f32[256,512]{1,0:T(8,128)S(1)} %get-tuple-element.40.sides), custom_call_target="tpu_custom_call" | custom-call | flops 67108864 | bytes 593920 | tf_op jit(solution)/shard_map/pallas_call | solution.py:32
  15.5 3.4 %all-to-all-start.1 = ((f32[8,16,512]{2,1,0:T(8,128)}), f32[8,16,512]{2,1,0:T(8,128)S(1)}, u32[]{:S(2)}, u32[]{:S(2)}) async-start(f32[8,16,512]{2,1,0:T(8,128)} %bitcast.7), calls=%async_computation.1 | async-start | bytes 524288 | tf_op jit(solution)/shard_map/all_to_all | solution.py:609
  18.9 1.5 %collective-permute-start = (f32[64,512]{1,0:T(8,128)S(1)}, f32[64,512]{1,0:T(8,128)S(1)}, u32[]{:S(2)}, u32[]{:S(2)}) collective-permute-start(f32[64,512]{1,0:T(8,128)S(1)} %get-tuple-element.44.top), channel_id=1, source_target_pairs={{0,8},{8,16},{16,24},{24,0},{1,9},{9,17},{17,25},{25,1},{2,10},{10... | collective-permute-start | bytes 393224 | tf_op jit(solution)/shard_map/ppermute | solution.py:612
  20.4 1.4 %collective-permute-start.1 = (f32[64,512]{1,0:T(8,128)S(1)}, f32[64,512]{1,0:T(8,128)S(1)}, u32[]{:S(2)}, u32[]{:S(2)}) collective-permute-start(f32[64,512]{1,0:T(8,128)S(1)} %get-tuple-element.43.bottom), channel_id=1, source_target_pairs={{8,0},{16,8},{24,16},{0,24},{9,1},{17,9},{25,17},{1,25},{10,2},{18... | collective-permute-start | bytes 393224 | tf_op jit(solution)/shard_map/ppermute | solution.py:615
  21.9 3.9 %shard_map.96 = (bf16[128,896]{1,0:T(8,128)(2,1)S(1)}, f32[256,512]{1,0:T(8,128)S(1)}, bf16[2,512,384]{2,1,0:T(8,128)(2,1)}, bf16[2,384,384]{2,1,0:T(8,128)(2,1)S(1)}) custom-call(s32[8,128]{1,0:T(8,128)S(1)} %get-tuple-element.38.marks, s32[128,128]{1,0:T(8,128)S(1)} %bitcast.22, f32[256,512]{1,0:T(8,128)S(1)} %get-tuple-element.40.sides, ...), custom_call_target="tpu_custom_call" | custom-call | flops 603979776 | bytes 3018752 | tf_op jit(solution)/shard_map/pallas_call | solution.py:32
  25.8 0.4 collective-permute-done.up
  26.1 2.4 %collective-permute-done.1.down = f32[64,512]{1,0:T(8,128)S(1)} collective-permute-done((f32[64,512]{1,0:T(8,128)S(1)}, f32[64,512]{1,0:T(8,128)S(1)}, u32[]{:S(2)}, u32[]{:S(2)}) %collective-permute-start.1) | collective-permute-done | bytes 131104 | tf_op jit(solution)/shard_map/ppermute | solution.py:615
  28.5 0.1 all-to-all-done.1
  28.6 2.8 %shard_map.98 = (f32[192,512]{1,0:T(8,128)}, f32[512,384]{1,0:T(8,128)}, f32[256,512]{1,0:T(8,128)S(1)}, f32[64,512]{1,0:T(8,128)S(1)}, f32[64,512]{1,0:T(8,128)S(1)}, /*index=5*/f32[128,512]{1,0:T(8,128)}) custom-call(f32[256,512]{1,0:T(8,128)S(1)} %get-tuple-element.41.base, bf16[128,896]{1,0:T(8,128)(2,1)S(1)} %get-tuple-element.42.maps, ...), custom_call_target="tpu_custom_call" | custom-call | flops 452984832 | bytes 3145728 | tf_op jit(solution)/shard_map/pallas_call | solution.py:32
  31.4 4.7 %all-to-all-start.2 = ((f32[8,16,512]{2,1,0:T(8,128)}), f32[8,16,512]{2,1,0:T(8,128)S(1)}, u32[]{:S(2)}, u32[]{:S(2)}) async-start(f32[8,16,512]{2,1,0:T(8,128)} %bitcast.27), calls=%async_computation.2 | async-start | bytes 524288 | tf_op jit(solution)/shard_map/all_to_all | solution.py:609
  36.1 1.5 %collective-permute-start.2 = (f32[64,512]{1,0:T(8,128)S(1)}, f32[64,512]{1,0:T(8,128)S(1)}, u32[]{:S(2)}, u32[]{:S(2)}) collective-permute-start(f32[64,512]{1,0:T(8,128)S(1)} %get-tuple-element.53.top), channel_id=1, source_target_pairs={{0,8},{8,16},{16,24},{24,0},{1,9},{9,17},{17,25},{25,1},{2,10},{10... | collective-permute-start | bytes 393224 | tf_op jit(solution)/shard_map/ppermute | solution.py:612
  37.6 1.4 %collective-permute-start.3 = (f32[64,512]{1,0:T(8,128)S(1)}, f32[64,512]{1,0:T(8,128)S(1)}, u32[]{:S(2)}, u32[]{:S(2)}) collective-permute-start(f32[64,512]{1,0:T(8,128)S(1)} %get-tuple-element.52.bottom), channel_id=1, source_target_pairs={{8,0},{16,8},{24,16},{0,24},{9,1},{17,9},{25,17},{1,25},{10,2},{18... | collective-permute-start | bytes 393224 | tf_op jit(solution)/shard_map/ppermute | solution.py:615
  39.1 5.7 %shard_map.99 = (f32[512,512]{1,0:T(8,128)}, f32[512,512]{1,0:T(8,128)}, f32[512,128]{1,0:T(8,128)}, f32[512,64]{1,0:T(8,128)}, f32[512,384]{1,0:T(8,128)}, /*in...) custom-call(f32[192,512]{1,0:T(8,128)} %get-tuple-element.47.mine.mine_in, ...), custom_call_target="tpu_custom_call" | custom-call | flops 603979776 | bytes 5242880 | tf_op jit(solution)/shard_map/pallas_call | solution.py:32
  44.8 0.0 collective-permute-done.2.up
  44.8 1.0 %all-to-all-done.2 = f32[8,16,512]{2,1,0:T(8,128)S(1)} async-done(((f32[8,16,512]{2,1,0:T(8,128)}), f32[8,16,512]{2,1,0:T(8,128)S(1)}, u32[]{:S(2)}, u32[]{:S(2)}) %all-to-all-start.2) | async-done | bytes 262176 | tf_op jit(solution)/shard_map/all_to_all | solution.py:609
  45.9 2.8 %shard_map.100 = (f32[192,512]{1,0:T(8,128)}, f32[512,384]{1,0:T(8,128)}, f32[32,1,128]{2,1,0:T(1,128)}) custom-call(f32[256,512]{1,0:T(8,128)S(1)} %get-tuple-element.54.base, bf16[128,896]{1,0:T(8,128)(2,1)S(1)} %get-tuple-element.42.maps, f32[128,512]{1,0:T(8,128)S(1)} %bitcast.19, f32[64,512]{1,0:T(8,128)S(1)} %get-tuple-element.52.bottom, ...), custom_call_target="tpu_custom_call" | custom-call | flops 452984832 | bytes 5144576 | tf_op jit(solution)/shard_map/pallas_call | solution.py:32
  48.7 4.6 %all-to-all-start.3 = ((f32[32,1,128]{2,1,0:T(1,128)}), f32[32,1,128]{2,1,0:T(1,128)S(1)}, u32[]{:S(2)}, u32[]{:S(2)}) async-start(f32[32,1,128]{2,1,0:T(1,128)} %get-tuple-element.59), calls=%async_computation.3 | async-start | bytes 32768 | tf_op jit(solution)/shard_map/all_to_all | solution.py:681
  53.3 3.5 %shard_map.101 = (f32[512,512]{1,0:T(8,128)S(1)}, f32[512,128]{1,0:T(8,128)}, f32[512,64]{1,0:T(8,128)}, f32[512,512]{1,0:T(8,128)S(1)}) custom-call(f32[192,512]{1,0:T(8,128)} %get-tuple-element.61.mine, f32[512,384]{1,0:T(8,128)} %get-tuple-element.62.flat, bf16[2,512,384]{2,1,0:T(8,128)(2,1)} %get-tuple-element.49.lift, ...), custom_call_target="tpu_custom_call" | custom-call | flops 603979776 | bytes 4259840 | tf_op jit(solution)/shard_map/pallas_call | solution.py:32
  56.8 3.5 %all-to-all-done.3.stats = f32[32,1,128]{2,1,0:T(1,128)S(1)} async-done(((f32[32,1,128]{2,1,0:T(1,128)}), f32[32,1,128]{2,1,0:T(1,128)S(1)}, u32[]{:S(2)}, u32[]{:S(2)}) %all-to-all-start.3) | async-done | bytes 16416 | tf_op jit(solution)/shard_map/all_to_all | solution.py:681
  60.4 2.5 %shard_map.102 = (f32[512,512]{1,0:T(8,128)}, f32[64,8,128]{2,1,0:T(8,128)}, f32[64,8,64]{2,1,0:T(8,128)}) custom-call(f32[32,1,128]{2,1,0:T(1,128)S(1)} %all-to-all-done.3.stats, f32[64,8,128]{2,1,0:T(8,128)} %bitcast.23, f32[64,8,128]{2,1,0:T(8,128)} %bitcast.25, f32[64,8,64]{2,1,0:T(8,128)} %bitcast.24, f32[64,8,64]{2,1,0:T(8,128)} %bitcast.26, ...), custom_call_target="tpu_custom_call" | custom-call | bytes 3948544 | tf_op jit(solution)/shard_map/pallas_call | solution.py:32
  (1 shorter events, 0.0 us)
Async XLA Ops:
  2.3 12.3 %all-to-all-start = ((s32[8,16,128]{2,1,0:T(8,128)}), s32[8,16,128]{2,1,0:T(8,128)S(1)}, u32[]{:S(2)}, u32[]{:S(2)}) async-start(s32[8,16,128]{2,1,0:T(8,128)} %bitcast.1), calls=%async_computation | async-start | bytes 131072 | tf_op jit(solution)/shard_map/all_to_all | solution.py:609
  15.5 13.1 %all-to-all-start.1 = ((f32[8,16,512]{2,1,0:T(8,128)}), f32[8,16,512]{2,1,0:T(8,128)S(1)}, u32[]{:S(2)}, u32[]{:S(2)}) async-start(f32[8,16,512]{2,1,0:T(8,128)} %bitcast.7), calls=%async_computation.1 | async-start | bytes 524288 | tf_op jit(solution)/shard_map/all_to_all | solution.py:609
  18.9 7.3 %collective-permute-start = (f32[64,512]{1,0:T(8,128)S(1)}, f32[64,512]{1,0:T(8,128)S(1)}, u32[]{:S(2)}, u32[]{:S(2)}) collective-permute-start(f32[64,512]{1,0:T(8,128)S(1)} %get-tuple-element.44.top), channel_id=1, source_target_pairs={{0,8},{8,16},{16,24},{24,0},{1,9},{9,17},{17,25},{25,1},{2,10},{10... | collective-permute-start | bytes 393224 | tf_op jit(solution)/shard_map/ppermute | solution.py:612
  20.4 8.1 %collective-permute-start.1 = (f32[64,512]{1,0:T(8,128)S(1)}, f32[64,512]{1,0:T(8,128)S(1)}, u32[]{:S(2)}, u32[]{:S(2)}) collective-permute-start(f32[64,512]{1,0:T(8,128)S(1)} %get-tuple-element.43.bottom), channel_id=1, source_target_pairs={{8,0},{16,8},{24,16},{0,24},{9,1},{17,9},{25,17},{1,25},{10,2},{18... | collective-permute-start | bytes 393224 | tf_op jit(solution)/shard_map/ppermute | solution.py:615
  31.4 14.4 %all-to-all-start.2 = ((f32[8,16,512]{2,1,0:T(8,128)}), f32[8,16,512]{2,1,0:T(8,128)S(1)}, u32[]{:S(2)}, u32[]{:S(2)}) async-start(f32[8,16,512]{2,1,0:T(8,128)} %bitcast.27), calls=%async_computation.2 | async-start | bytes 524288 | tf_op jit(solution)/shard_map/all_to_all | solution.py:609
  36.1 8.7 %collective-permute-start.2 = (f32[64,512]{1,0:T(8,128)S(1)}, f32[64,512]{1,0:T(8,128)S(1)}, u32[]{:S(2)}, u32[]{:S(2)}) collective-permute-start(f32[64,512]{1,0:T(8,128)S(1)} %get-tuple-element.53.top), channel_id=1, source_target_pairs={{0,8},{8,16},{16,24},{24,0},{1,9},{9,17},{17,25},{25,1},{2,10},{10... | collective-permute-start | bytes 393224 | tf_op jit(solution)/shard_map/ppermute | solution.py:612
  37.6 7.2 %collective-permute-start.3 = (f32[64,512]{1,0:T(8,128)S(1)}, f32[64,512]{1,0:T(8,128)S(1)}, u32[]{:S(2)}, u32[]{:S(2)}) collective-permute-start(f32[64,512]{1,0:T(8,128)S(1)} %get-tuple-element.52.bottom), channel_id=1, source_target_pairs={{8,0},{16,8},{24,16},{0,24},{9,1},{17,9},{25,17},{1,25},{10,2},{18... | collective-permute-start | bytes 393224 | tf_op jit(solution)/shard_map/ppermute | solution.py:615
  48.7 11.7 %all-to-all-start.3 = ((f32[32,1,128]{2,1,0:T(1,128)}), f32[32,1,128]{2,1,0:T(1,128)S(1)}, u32[]{:S(2)}, u32[]{:S(2)}) async-start(f32[32,1,128]{2,1,0:T(1,128)} %get-tuple-element.59), calls=%async_computation.3 | async-start | bytes 32768 | tf_op jit(solution)/shard_map/all_to_all | solution.py:681

commit v4 on v3

--- a/solution.py
+++ b/solution.py
@@ -153,12 +153,18 @@
     face_nodes, source, inverse, coupling, codes, scales, solved, sides, bottom, top, table,
     source_here, inverse_here, coupling_here, orientation, scale, image, flat, semaphores
 ):
-    small = [begin(codes, orientation, semaphores.at[4]), begin(scales, scale, semaphores.at[5])]
-    reads = [
-        begin(source, source_here, semaphores.at[0]),
-        begin(inverse, inverse_here, semaphores.at[1]),
-        begin(coupling, coupling_here, semaphores.at[2]),
-    ]
+    small = [begin(codes, orientation, semaphores.at[5]), begin(scales, scale, semaphores.at[6])]
+    depth = inverse.shape[0] // 2
+    reads = []
+    for k in range(2):
+        part = pl.ds(k * depth, depth)
+        reads.append(
+            (
+                begin(inverse.at[part], inverse_here.at[part], semaphores.at[2 * k]),
+                begin(source.at[:, part], source_here.at[:, part], semaphores.at[2 * k + 1]),
+            )
+        )
+    read_coupling = begin(coupling, coupling_here, semaphores.at[4])
     columns = orientation.shape[0]
     count = orientation.shape[1]
     edge = math.isqrt(face_nodes)
@@ -195,20 +201,20 @@
         else:
             top[:, lanes] = value * has_above
 
-    reads[0].wait()
-    reads[1].wait()
     pairs = sides.shape[1] // pair
     parts = [range(0, pairs // 2), range(pairs // 2, pairs)]
-    split = halves(inverse_here[...])
-    split_coupling = None
+    for k, pieces in enumerate(reads):
+        for piece in pieces:
+            piece.wait()
+        depths = slice(k * depth, (k + 1) * depth)
+        product = dot_split(halves(source_here[:, depths]), halves(inverse_here[depths, :]))
+        image[...] = product if k == 0 else image[...] + product
+    read_coupling.wait()
+    split_coupling = halves(coupling_here[...])
     for part in parts:
         rows = slice(2 * part[0] * count, 2 * (part[-1] + 1) * count)
-        image[rows, :] = dot_split(halves(source_here[rows, :]), split)
-        if split_coupling is None:
-            reads[2].wait()
-            split_coupling = halves(coupling_here[...])
         flat[rows, :] = dot_split(halves(image[rows, :]), split_coupling)
-    write = begin(image, solved, semaphores.at[3])
+    write = begin(image, solved, semaphores.at[7])
     for part in parts:
         from_flat(flat, table, placed, count, part, range(columns))
     write.wait()
@@ -265,7 +271,8 @@
 
 
 def tables_body(
-    owned, capacity, marks, wanted, sides, inverse, coupling, operator, maps, base, lift, split
+    owned, capacity, marks, wanted, sides, bottom, up, inverse, coupling, operator,
+    maps, base, below, lift, split
 ):
     taken, given = places(capacity, marks, wanted)
     first, here = marks[1:2, :], marks[2:3, :]
@@ -274,6 +281,7 @@
     maps[...] = jnp.concatenate(
         [taken, given[:, :owned].T, given[:, owned:].T, across, across.T, sorter], axis=1
     ).astype(BF16)
+    below[...] = bottom[...] + up[...]
     base[:owned, :], base[owned:, :] = Maps(maps, owned).with_partners(sides[...])
     high, low = halves(dot_split(halves(inverse[...]), halves(coupling[...])))
     lift[0] = high
@@ -281,10 +289,10 @@
     split[0], split[1] = halves(operator[...])
 
 
-def add_up(base, maps, received, bottom, top, up, down, total):
+def add_up(base, maps, received, below, top, down, total):
     owned = maps.owned
-    count = bottom.shape[0]
-    total[2 * owned : 2 * owned + count, :] = bottom[...] + up[...]
+    count = top.shape[0]
+    total[2 * owned : 2 * owned + count, :] = below[...]
     total[2 * owned + count :, :] = top[...] + down[...]
     first, second = maps.from_message(received[...])
     total[:owned, :] = base[:owned, :] + first
@@ -315,13 +323,13 @@
 
 
 def apply_body(
-    owned, base, maps, received, bottom, top, up, down, table, split,
+    owned, base, maps, received, below, top, down, table, split,
     mine, flat_out, sides_out, bottom_out, top_out, send,
     total, mine_here, flat, image, message, semaphores
 ):
-    count = bottom.shape[0]
+    count = top.shape[0]
     maps = Maps(maps, owned)
-    add_up(base, maps, received, bottom, top, up, down, total)
+    add_up(base, maps, received, below, top, down, total)
     mine_here[...] = own_faces(total, owned, count)
     writes = [begin(mine_here, mine, semaphores.at[0])]
     has_below, has_above = layer_masks()
@@ -380,22 +388,36 @@
 
 
 def beside_body(
-    owned, mine, flat, table, lift, solved, maps, sides, bottom, top,
-    lifted_out, scaled, side_traces, top_traces, image_out, base, known, shifts,
-    placed, image, semaphores
+    owned, mine_in, flat_in, lift_in, table, maps, sides, bottom, top, up,
+    lifted_out, side_out, top_out, image_out, base, below, known, shifts,
+    mine, flat, lift, placed, image, lifted_here, side_traces, top_traces, semaphores
 ):
-    count = top_traces.shape[1]
-    rights = solved.shape[0] // count
+    reads = [
+        begin(mine_in, mine, semaphores.at[0]),
+        begin(flat_in, flat, semaphores.at[1]),
+        begin(lift_in, lift, semaphores.at[2]),
+    ]
+    count = bottom.shape[0]
+    rights = flat.shape[0] // count
     maps = Maps(maps, owned)
     placed[: 2 * owned, :] = sides[...]
     placed[2 * owned : 2 * owned + count, :] = bottom[...]
+    below[...] = bottom[...] + up[...]
     placed[2 * owned + count :, :] = top[...]
     to_flat(placed, table, image, count, range(rights // 2))
-    write = begin(image, image_out, semaphores.at[0])
+    writes = [begin(image, image_out, semaphores.at[3])]
     first, second = maps.with_partners(sides[...])
     base[:owned, :], base[owned:, :] = first, second
+    reads[0].wait()
+    store_traces(mine, maps, side_traces, top_traces, rights)
+    writes.append(begin(side_traces, side_out, semaphores.at[4]))
+    writes.append(begin(top_traces, top_out, semaphores.at[5]))
+    reads[1].wait()
+    reads[2].wait()
+    lifted_here[...] = lifted(flat[...], lift)
+    writes.append(begin(lifted_here, lifted_out, semaphores.at[6]))
     inside = jnp.sum(maps.part(4).astype(F32), axis=1, keepdims=True)
-    b, w = mine[:owned, :], first * inside
+    b, w = mine[:owned, :], base[:owned, :] * inside
     lanes = mine.shape[1]
     width = lanes // rights
     group = lax.div(iota((lanes, lanes), 0), width) == lax.div(iota((lanes, lanes), 1), width)
@@ -419,23 +441,35 @@
         + [jnp.where(iota(spread.shape, 1) == 0, spread, 0.0), spread],
         axis=0,
     )
+    for write in writes:
+        write.wait()
+
+
+def after_body(
+    owned, mine_in, flat_in, lift_in, lifted_first, table, maps,
+    lifted_out, side_out, top_out, first_out, inverse_scale,
+    mine, flat, lift, side_traces, top_traces, semaphores
+):
+    reads = [
+        begin(mine_in, mine, semaphores.at[0]),
+        begin(flat_in, flat, semaphores.at[1]),
+        begin(lift_in, lift, semaphores.at[2]),
+        begin(lifted_first, first_out, semaphores.at[3]),
+    ]
+    count = inverse_scale.shape[0]
+    inverse_scale[...] = 1.0 / scale_of(table[:count, :])
+    reads[0].wait()
+    store_traces(mine, Maps(maps, owned), side_traces, top_traces, flat.shape[0] // count)
+    writes = [
+        begin(side_traces, side_out, semaphores.at[4]),
+        begin(top_traces, top_out, semaphores.at[5]),
+    ]
+    reads[1].wait()
+    reads[2].wait()
     lifted_out[...] = lifted(flat[...], lift)
-    scale = jnp.concatenate([scale_of(table[:count, :])] * rights, axis=0)
-    copies = solved.shape[1] // scale.shape[1]
-    scaled[...] = solved[...] / jnp.concatenate([scale] * copies, axis=1)
-    store_traces(mine, maps, side_traces, top_traces, rights)
-    write.wait()
-
-
-def after_body(
-    owned, mine, flat, lift, maps, lifted_first, lifted_out, side_traces, top_traces, first_out,
-    semaphores
-):
-    count = top_traces.shape[1]
-    read = begin(lifted_first, first_out, semaphores.at[0])
-    lifted_out[...] = lifted(flat[...], lift)
-    store_traces(mine, Maps(maps, owned), side_traces, top_traces, flat.shape[0] // count)
-    read.wait()
+    reads[3].wait()
+    for write in writes:
+        write.wait()
 
 
 def total_rows(value):
@@ -460,11 +494,11 @@
 
 
 def stats_body(
-    owned, base, maps, received, bottom, top, up, down, table, split, known, shifts, mine_in,
+    owned, base, maps, received, below, top, down, table, split, known, shifts, mine_in,
     flat_in, image_in, next_mine_out, next_flat_out, stats,
     total_next, mine, flat, image, next_mine, next_flat, next_image, semaphores
 ):
-    count = bottom.shape[0]
+    count = top.shape[0]
     rights = flat.shape[0] // count
     reads = [
         begin(mine_in, mine, semaphores.at[0]),
@@ -472,7 +506,7 @@
         begin(image_in, image, semaphores.at[2]),
     ]
     maps = Maps(maps, owned)
-    add_up(base, maps, received, bottom, top, up, down, total_next)
+    add_up(base, maps, received, below, top, down, total_next)
     next_mine[...] = own_faces(total_next, owned, count)
     writes = [begin(next_mine, next_mine_out, semaphores.at[3])]
 
@@ -520,15 +554,15 @@
 
 
 def finish_body(
-    stats, side_first, side_next, top_first, top_next, scaled, lifted_first, lifted_next,
-    interior, side_traces, top_traces,
-    scaled_here, side_here, side_next_here, top_here, top_next_here, semaphores
+    stats, side_first, side_next, top_first, top_next, solved, lifted_first, lifted_next,
+    inverse_scale, interior, side_traces, top_traces,
+    solved_here, side_here, side_next_here, top_here, top_next_here, semaphores
 ):
     rights = side_traces.shape[1]
-    block = scaled.shape[0] // rights
+    block = solved.shape[0] // rights
     parts = [pl.ds(r * block, block) for r in range(rights)]
     reads = [
-        begin(scaled.at[part], scaled_here.at[part], semaphores.at[r])
+        begin(solved.at[part], solved_here.at[part], semaphores.at[r])
         for r, part in enumerate(parts)
     ]
     traces = (
@@ -557,14 +591,16 @@
 
     first = column(alpha + alpha_next * (1.0 + beta))
     following = column(-alpha_next * alpha)
+    scale = inverse_scale[...]
+    scale = jnp.concatenate([scale] * (solved.shape[1] // scale.shape[1]), axis=1)
     writes = []
     for r, part in enumerate(parts):
         reads[r].wait()
-        scaled_here[part, :] = scaled_here[part, :] - (
+        solved_here[part, :] = solved_here[part, :] * scale - (
             first[r : r + 1, :] * lifted_first[part, :]
             + following[r : r + 1, :] * lifted_next[part, :]
         )
-        writes.append(begin(scaled_here.at[part], interior.at[part], semaphores.at[rights + 4 + r]))
+        writes.append(begin(solved_here.at[part], interior.at[part], semaphores.at[rights + 4 + r]))
     for k, (here, next_here, out) in enumerate(
         ((side_here, side_next_here, side_traces), (top_here, top_next_here, top_traces))
     ):
@@ -628,62 +664,67 @@
         [Raw(flat_source), Raw(interior_inverse), Raw(coupling), Raw(codes), Raw(scale)],
         [whole, ((nodes, nodes), F32), ((nodes, traces), F32), (codes.shape, I32),
          (scale.shape, I32), whole, flat],
-        copies=6,
+        copies=8,
         flops=6 * flat_rows * nodes * (nodes + traces),
     )
     (send,) = call(
         functools.partial(send_body, capacity),
         [message],
         [marks, wanted, sides],
-        flops=4 * lines * side_rows * lanes,
+        flops=400 * lines * side_rows * lanes,
     )
     up, down, received = climb(top), sink(bottom), across(send)
     square = ((2, traces, traces), BF16)
-    maps, base, lift, split = call(
+    maps, base, below, lift, split = call(
         functools.partial(tables_body, owned, capacity),
         [
             ((lines, 7 * owned), BF16),
             faces[0],
+            faces[1],
             ((2, nodes, traces), BF16, "far"),
             square,
         ],
-        [marks, wanted, sides, far(interior_inverse), far(coupling), far(trace_operator)],
-        flops=6 * nodes * nodes * traces,
+        [marks, wanted, sides, bottom, up, far(interior_inverse), far(coupling),
+         far(trace_operator)],
+        flops=40 * nodes * nodes * traces,
     )
     mine = ((owned + count, lanes), F32)
     own, local, sides, bottom, top, send = call(
         functools.partial(apply_body, owned),
         [mine + ("raw",), flat + ("raw",)] + faces + [message + ("raw",)],
-        [base, maps, received, bottom, top, up, down, table, split],
+        [base, maps, received, below, top, down, table, split],
         [grid, mine, flat, flat, message],
         copies=5,
         flops=6 * flat_rows * traces * traces,
     )
     up, down, received = climb(top), sink(bottom), across(send)
-    lifted_first, scaled, side_first, top_first, image, base, known, shifts = call(
+    lift_form = ((2, nodes, traces), BF16)
+    lifted_first, side_first, top_first, image, base, below, known, shifts = call(
         functools.partial(beside_body, owned),
-        [whole + ("far",), whole + ("far",), side_shape + ("far",), top_shape + ("far",),
-         flat + ("raw",), faces[0], ((4 * rights, 2 * face_nodes), F32), ((8, lanes), F32)],
-        [far(own), far(local), table, far(lift), far(solved), maps, sides, bottom, top],
-        [grid, flat],
-        copies=1,
-        flops=6 * flat_rows * traces * nodes,
+        [whole + ("raw",), side_shape + ("raw",), top_shape + ("raw",), flat + ("raw",), faces[0],
+         faces[1], ((4 * rights, 2 * face_nodes), F32), ((8, lanes), F32)],
+        [Raw(own), Raw(local), Raw(lift), table, maps, sides, bottom, top, up],
+        [mine, flat, lift_form, grid, flat, whole, side_shape, top_shape],
+        copies=7,
+        flops=40 * flat_rows * traces * nodes,
     )
     own, local, stats = call(
         functools.partial(stats_body, owned),
         [mine + ("raw",), flat + ("raw",), ((layers * blocks, 1, 2 * face_nodes), F32)],
-        [base, maps, received, bottom, top, up, down, table, split, known, shifts,
+        [base, maps, received, below, top, down, table, split, known, shifts,
          Raw(own), Raw(local), Raw(image)],
         [grid, mine, flat, flat, mine, flat, flat],
         copies=6,
         flops=6 * flat_rows * traces * traces,
     )
     stats = lax.all_to_all(stats, ("gz", "dev"), 0, 0, tiled=True)
-    lifted_next, side_next, top_next, lifted_first = call(
+    lifted_next, side_next, top_next, lifted_first, inverse_scale = call(
         functools.partial(after_body, owned),
-        [whole, side_shape + ("far",), top_shape + ("far",), whole],
-        [far(own), far(local), far(lift), maps, Raw(lifted_first)],
-        copies=1,
+        [whole, side_shape + ("raw",), top_shape + ("raw",), whole,
+         ((count, 2 * face_nodes), F32)],
+        [Raw(own), Raw(local), Raw(lift), Raw(lifted_first), table, maps],
+        [mine, flat, lift_form, side_shape, top_shape],
+        copies=6,
         flops=6 * flat_rows * traces * nodes,
     )
     side_form = ((face_nodes, rights, owned), F32)
@@ -692,8 +733,8 @@
         finish_body,
         [whole + ("raw",), side_form + ("raw",), top_form + ("raw",)],
         [stats, Raw(side_first.reshape(side_form[0])), Raw(side_next.reshape(side_form[0])),
-         Raw(top_first.reshape(top_form[0])), Raw(top_next.reshape(top_form[0])), Raw(scaled),
-         lifted_first, lifted_next],
+         Raw(top_first.reshape(top_form[0])), Raw(top_next.reshape(top_form[0])), Raw(solved),
+         lifted_first, lifted_next, inverse_scale],
         [whole, side_form, side_form, top_form, top_form],
         copies=2 * rights + 6,
     )

time: 63.6 us -> 62.7 us (0.986)
  waiting for transfers between devices: 9.12 us -> 12.6 us
  starting transfers between devices: 25 us -> 22.8 us
  Pallas kernels: 28.1 us -> 26 us
    all_to_all x3, waiting for transfers between devices: 2.82 us -> 7.66 us  [across(): return lax.all_to_all(parts, 'dev', 0, 0, tiled=True).reshape(message.shape)]
    pallas_call x9, Pallas kernels: 28.1 us -> 26 us  [call(): pl.pallas_call(body, out_shape=[pltpu.HBM(*out[:2]) if len(out) > 2 else...]
    all_to_all x1, starting transfers between devices: 4.63 us -> 2.56 us  [per_device(): stats = lax.all_to_all(stats, ('gz', 'dev'), 0, 0, tiled=True)]
    ppermute x2, waiting for transfers between devices: 2.41 us -> 0.42 us  [sink(): lax.ppermute(value, 'gz', [((at + 1) % layers, at) for at in range(layers)])]
    all_to_all x1, waiting for transfers between devices: 3.54 us -> 4.5 us  [per_device(): stats = lax.all_to_all(stats, ('gz', 'dev'), 0, 0, tiled=True)]
  transfers between devices with their start and end apart: 8 -> 8, of which waited for: 6 -> 5; matrix products, arithmetic and copies ran while one was open for 0% -> 0% of each run, Pallas kernels for 28% -> 26%
where the time goes in v4:
time: 62.7 us; the launch traced here: 62.1 us
  Pallas kernels  26 us (41%)
  starting transfers between devices  22.8 us (36%)
  waiting for transfers between devices  12.6 us (20%)
  between operations  0.71 us (1%)
    pallas_call x9, Pallas kernels, call(): pl.pallas_call(body, out_shape=[pltpu.HBM(*out[:2]) if len(out) > 2 else...  26 us
    all_to_all x3, starting transfers between devices, across(): return lax.all_to_all(parts, 'dev', 0, 0, tiled=True).reshape(message.shape)  14.2 us
    all_to_all x3, waiting for transfers between devices, across(): return lax.all_to_all(parts, 'dev', 0, 0, tiled=True).reshape(message.shape)  7.66 us
    all_to_all x1, waiting for transfers between devices, per_device(): stats = lax.all_to_all(stats, ('gz', 'dev'), 0, 0, tiled=True)  4.5 us
    ppermute x2, starting transfers between devices, climb(): lax.ppermute(value, 'gz', [(at, (at + 1) % layers) for at in range(layers)])  3.1 us
    ppermute x2, starting transfers between devices, sink(): lax.ppermute(value, 'gz', [((at + 1) % layers, at) for at in range(layers)])  2.99 us
    all_to_all x1, starting transfers between devices, per_device(): stats = lax.all_to_all(stats, ('gz', 'dev'), 0, 0, tiled=True)  2.56 us
  transfers between devices with their start and end apart: 8, of which 5 were waited for; matrix products, arithmetic and copies ran while one was open for 0% of the time, Pallas kernels for 26%

profile of v4, /device:TPU:0, one launch (start us, length us, event | category | flops | bytes accessed | tf_op | source)
XLA Modules:
  0.0 62.1 jit_solution(13814313406947959218)
XLA Ops:
  0.6 1.6 %shard_map.94 = (s32[128,128]{1,0:T(8,128)}, s32[8,128]{1,0:T(8,128)S(1)}) custom-call(s32[4,64]{1,0:T(4,128)} %bitcast.28), custom_call_target="tpu_custom_call" | custom-call | bytes 1024 | tf_op jit(solution)/shard_map/pallas_call | solution.py:32
  2.3 6.3 %all-to-all-start = ((s32[8,16,128]{2,1,0:T(8,128)}), s32[8,16,128]{2,1,0:T(8,128)S(1)}, u32[]{:S(2)}, u32[]{:S(2)}) async-start(s32[8,16,128]{2,1,0:T(8,128)} %bitcast.1), calls=%async_computation | async-start | bytes 131072 | tf_op jit(solution)/shard_map/all_to_all | solution.py:645
  8.6 3.7 %shard_map.95 = (f32[512,512]{1,0:T(8,128)}, f32[256,512]{1,0:T(8,128)S(1)}, f32[64,512]{1,0:T(8,128)S(1)}, f32[64,512]{1,0:T(8,128)S(1)}, s32[384,128]{1,0:T(8,128)S(1)}) custom-call(f32[512,512]{1,0:T(8,128)} %bitcast.29, f32[512,512]{1,0:T(8,128)} %inverse.3, f32[512,384]{1,0:T(8,128)} %coupling.3, s32[6,64]{1,0:T(8,128)} %bitcast.31, s32[1,64]{1,0:T(1,128)} %bitcast.32), custom_call_target="tpu_custom_call" | custom-call | flops 1409286144 | bytes 2885376 | tf_op jit(solution)/shard_map/pallas_call | solution.py:32
  12.3 1.5 %collective-permute-start = (f32[64,512]{1,0:T(8,128)S(1)}, f32[64,512]{1,0:T(8,128)S(1)}, u32[]{:S(2)}, u32[]{:S(2)}) collective-permute-start(f32[64,512]{1,0:T(8,128)S(1)} %get-tuple-element.44.top), channel_id=1, source_target_pairs={{0,8},{8,16},{16,24},{24,0},{1,9},{9,17},{17,25},{25,1},{2,10},{10... | collective-permute-start | bytes 393224 | tf_op jit(solution)/shard_map/ppermute | solution.py:648
  13.8 0.7 %all-to-all-done = s32[8,16,128]{2,1,0:T(8,128)S(1)} async-done(((s32[8,16,128]{2,1,0:T(8,128)}), s32[8,16,128]{2,1,0:T(8,128)S(1)}, u32[]{:S(2)}, u32[]{:S(2)}) %all-to-all-start) | async-done | bytes 65568 | tf_op jit(solution)/shard_map/all_to_all | solution.py:645
  14.5 1.0 %shard_map.97 = f32[128,512]{1,0:T(8,128)} custom-call(s32[8,128]{1,0:T(8,128)S(1)} %get-tuple-element.40.marks, s32[128,128]{1,0:T(8,128)S(1)} %bitcast.21, f32[256,512]{1,0:T(8,128)S(1)} %get-tuple-element.42.sides), custom_call_target="tpu_custom_call" | custom-call | flops 6710886400 | bytes 593920 | tf_op jit(solution)/shard_map/pallas_call | solution.py:32
  15.5 4.4 %all-to-all-start.1 = ((f32[8,16,512]{2,1,0:T(8,128)}), f32[8,16,512]{2,1,0:T(8,128)S(1)}, u32[]{:S(2)}, u32[]{:S(2)}) async-start(f32[8,16,512]{2,1,0:T(8,128)} %bitcast.7), calls=%async_computation.1 | async-start | bytes 524288 | tf_op jit(solution)/shard_map/all_to_all | solution.py:645
  19.9 1.5 %collective-permute-start.1 = (f32[64,512]{1,0:T(8,128)S(1)}, f32[64,512]{1,0:T(8,128)S(1)}, u32[]{:S(2)}, u32[]{:S(2)}) collective-permute-start(f32[64,512]{1,0:T(8,128)S(1)} %get-tuple-element.43.bottom), channel_id=1, source_target_pairs={{8,0},{16,8},{24,16},{0,24},{9,1},{17,9},{25,17},{1,25},{10,2},{18... | collective-permute-start | bytes 393224 | tf_op jit(solution)/shard_map/ppermute | solution.py:651
  21.4 0.0 collective-permute-done.up
  21.4 4.0 %shard_map.96 = (bf16[128,896]{1,0:T(8,128)(2,1)S(1)}, f32[256,512]{1,0:T(8,128)S(1)}, f32[64,512]{1,0:T(8,128)S(1)}, bf16[2,512,384]{2,1,0:T(8,128)(2,1)}, bf16[2,384,384]{2,1,0:T(8,128)(2,1)S(1)}) custom-call(s32[8,128]{1,0:T(8,128)S(1)} %get-tuple-element.40.marks, s32[128,128]{1,0:T(8,128)S(1)} %bitcast.22, f32[256,512]{1,0:T(8,128)S(1)} %get-tuple-element.42.sides, ...), custom_call_target="tpu_custom_call" | custom-call | flops 4026531840 | bytes 3280896 | tf_op jit(solution)/shard_map/pallas_call | solution.py:32
  25.4 0.4 collective-permute-done.1.down
  25.8 3.8 %all-to-all-done.1 = f32[8,16,512]{2,1,0:T(8,128)S(1)} async-done(((f32[8,16,512]{2,1,0:T(8,128)}), f32[8,16,512]{2,1,0:T(8,128)S(1)}, u32[]{:S(2)}, u32[]{:S(2)}) %all-to-all-start.1) | async-done | bytes 262176 | tf_op jit(solution)/shard_map/all_to_all | solution.py:645
  29.6 2.8 %shard_map.98 = (f32[192,512]{1,0:T(8,128)}, f32[512,384]{1,0:T(8,128)}, f32[256,512]{1,0:T(8,128)S(1)}, f32[64,512]{1,0:T(8,128)S(1)}, f32[64,512]{1,0:T(8,128)S(1)}, /*index=5*/f32[128,512]{1,0:T(8,128)}) custom-call(f32[256,512]{1,0:T(8,128)S(1)} %get-tuple-element.45.base, bf16[128,896]{1,0:T(8,128)(2,1)S(1)} %get-tuple-element.46.maps, ...), custom_call_target="tpu_custom_call" | custom-call | flops 452984832 | bytes 3014656 | tf_op jit(solution)/shard_map/pallas_call | solution.py:32
  32.4 1.6 %collective-permute-start.2 = (f32[64,512]{1,0:T(8,128)S(1)}, f32[64,512]{1,0:T(8,128)S(1)}, u32[]{:S(2)}, u32[]{:S(2)}) collective-permute-start(f32[64,512]{1,0:T(8,128)S(1)} %get-tuple-element.55.top), channel_id=1, source_target_pairs={{0,8},{8,16},{16,24},{24,0},{1,9},{9,17},{17,25},{25,1},{2,10},{10... | collective-permute-start | bytes 393224 | tf_op jit(solution)/shard_map/ppermute | solution.py:648
  34.0 3.4 %all-to-all-start.2 = ((f32[8,16,512]{2,1,0:T(8,128)}), f32[8,16,512]{2,1,0:T(8,128)S(1)}, u32[]{:S(2)}, u32[]{:S(2)}) async-start(f32[8,16,512]{2,1,0:T(8,128)} %bitcast.27), calls=%async_computation.2 | async-start | bytes 524288 | tf_op jit(solution)/shard_map/all_to_all | solution.py:645
  37.4 1.5 %collective-permute-start.3 = (f32[64,512]{1,0:T(8,128)S(1)}, f32[64,512]{1,0:T(8,128)S(1)}, u32[]{:S(2)}, u32[]{:S(2)}) collective-permute-start(f32[64,512]{1,0:T(8,128)S(1)} %get-tuple-element.54.bottom), channel_id=1, source_target_pairs={{8,0},{16,8},{24,16},{0,24},{9,1},{17,9},{25,17},{1,25},{10,2},{18... | collective-permute-start | bytes 393224 | tf_op jit(solution)/shard_map/ppermute | solution.py:651
  38.9 0.0 collective-permute-done.2.up
  38.9 5.0 %shard_map.99 = (f32[512,512]{1,0:T(8,128)}, f32[512,128]{1,0:T(8,128)}, f32[512,64]{1,0:T(8,128)}, f32[512,384]{1,0:T(8,128)}, f32[256,512]{1,0:T(8,128)S(1)}, ...) custom-call(f32[192,512]{1,0:T(8,128)} %get-tuple-element.50.mine_in, ...), custom_call_target="tpu_custom_call" | custom-call | flops 4026531840 | bytes 4325376 | tf_op jit(solution)/shard_map/pallas_call | solution.py:32
  44.0 3.1 %all-to-all-done.2 = f32[8,16,512]{2,1,0:T(8,128)S(1)} async-done(((f32[8,16,512]{2,1,0:T(8,128)}), f32[8,16,512]{2,1,0:T(8,128)S(1)}, u32[]{:S(2)}, u32[]{:S(2)}) %all-to-all-start.2) | async-done | bytes 262176 | tf_op jit(solution)/shard_map/all_to_all | solution.py:645
  47.1 2.8 %shard_map.100 = (f32[192,512]{1,0:T(8,128)}, f32[512,384]{1,0:T(8,128)}, f32[32,1,128]{2,1,0:T(1,128)}) custom-call(f32[256,512]{1,0:T(8,128)S(1)} %get-tuple-element.56.base, bf16[128,896]{1,0:T(8,128)(2,1)S(1)} %get-tuple-element.46.maps, f32[128,512]{1,0:T(8,128)S(1)} %bitcast.19, f32[64,512]{1,0:T(8,128)S(1)} %get-tuple-element.58.below, ...), custom_call_target="tpu_custom_call" | custom-call | flops 452984832 | bytes 5013504 | tf_op jit(solution)/shard_map/pallas_call | solution.py:32
  49.9 2.6 %all-to-all-start.3 = ((f32[32,1,128]{2,1,0:T(1,128)}), f32[32,1,128]{2,1,0:T(1,128)S(1)}, u32[]{:S(2)}, u32[]{:S(2)}) async-start(f32[32,1,128]{2,1,0:T(1,128)} %get-tuple-element.62), calls=%async_computation.3 | async-start | bytes 32768 | tf_op jit(solution)/shard_map/all_to_all | solution.py:720
  52.5 2.6 %shard_map.101 = (f32[512,512]{1,0:T(8,128)S(1)}, f32[512,128]{1,0:T(8,128)}, f32[512,64]{1,0:T(8,128)}, f32[512,512]{1,0:T(8,128)S(1)}, f32[64,128]{1,0:T(8,128)S(1)}) custom-call(f32[192,512]{1,0:T(8,128)} %get-tuple-element.64.mine_in, f32[512,384]{1,0:T(8,128)} %get-tuple-element.65.flat_in, bf16[2,512,384]{2,1,0:T(8,128)(2,1)} %get-tuple-element.52.lift_in, ...), custom_call_target="tpu_custom_call" | custom-call | flops 603979776 | bytes 4456448 | tf_op jit(solution)/shard_map/pallas_call | solution.py:32
  55.0 4.5 %all-to-all-done.3.stats = f32[32,1,128]{2,1,0:T(1,128)S(1)} async-done(((f32[32,1,128]{2,1,0:T(1,128)}), f32[32,1,128]{2,1,0:T(1,128)S(1)}, u32[]{:S(2)}, u32[]{:S(2)}) %all-to-all-start.3) | async-done | bytes 16416 | tf_op jit(solution)/shard_map/all_to_all | solution.py:720
  59.5 2.5 %shard_map.102 = (f32[512,512]{1,0:T(8,128)}, f32[64,8,128]{2,1,0:T(8,128)}, f32[64,8,64]{2,1,0:T(8,128)}) custom-call(f32[32,1,128]{2,1,0:T(1,128)S(1)} %all-to-all-done.3.stats, f32[64,8,128]{2,1,0:T(8,128)} %bitcast.23, f32[64,8,128]{2,1,0:T(8,128)} %bitcast.25, f32[64,8,64]{2,1,0:T(8,128)} %bitcast.24, f32[64,8,64]{2,1,0:T(8,128)} %bitcast.26, ...), custom_call_target="tpu_custom_call" | custom-call | bytes 3981312 | tf_op jit(solution)/shard_map/pallas_call | solution.py:32
  (1 shorter events, 0.0 us)
Async XLA Ops:
  2.3 12.3 %all-to-all-start = ((s32[8,16,128]{2,1,0:T(8,128)}), s32[8,16,128]{2,1,0:T(8,128)S(1)}, u32[]{:S(2)}, u32[]{:S(2)}) async-start(s32[8,16,128]{2,1,0:T(8,128)} %bitcast.1), calls=%async_computation | async-start | bytes 131072 | tf_op jit(solution)/shard_map/all_to_all | solution.py:645
  12.3 9.1 %collective-permute-start = (f32[64,512]{1,0:T(8,128)S(1)}, f32[64,512]{1,0:T(8,128)S(1)}, u32[]{:S(2)}, u32[]{:S(2)}) collective-permute-start(f32[64,512]{1,0:T(8,128)S(1)} %get-tuple-element.44.top), channel_id=1, source_target_pairs={{0,8},{8,16},{16,24},{24,0},{1,9},{9,17},{17,25},{25,1},{2,10},{10... | collective-permute-start | bytes 393224 | tf_op jit(solution)/shard_map/ppermute | solution.py:648
  15.5 14.1 %all-to-all-start.1 = ((f32[8,16,512]{2,1,0:T(8,128)}), f32[8,16,512]{2,1,0:T(8,128)S(1)}, u32[]{:S(2)}, u32[]{:S(2)}) async-start(f32[8,16,512]{2,1,0:T(8,128)} %bitcast.7), calls=%async_computation.1 | async-start | bytes 524288 | tf_op jit(solution)/shard_map/all_to_all | solution.py:645
  19.9 5.9 %collective-permute-start.1 = (f32[64,512]{1,0:T(8,128)S(1)}, f32[64,512]{1,0:T(8,128)S(1)}, u32[]{:S(2)}, u32[]{:S(2)}) collective-permute-start(f32[64,512]{1,0:T(8,128)S(1)} %get-tuple-element.43.bottom), channel_id=1, source_target_pairs={{8,0},{16,8},{24,16},{0,24},{9,1},{17,9},{25,17},{1,25},{10,2},{18... | collective-permute-start | bytes 393224 | tf_op jit(solution)/shard_map/ppermute | solution.py:651
  32.4 6.5 %collective-permute-start.2 = (f32[64,512]{1,0:T(8,128)S(1)}, f32[64,512]{1,0:T(8,128)S(1)}, u32[]{:S(2)}, u32[]{:S(2)}) collective-permute-start(f32[64,512]{1,0:T(8,128)S(1)} %get-tuple-element.55.top), channel_id=1, source_target_pairs={{0,8},{8,16},{16,24},{24,0},{1,9},{9,17},{17,25},{25,1},{2,10},{10... | collective-permute-start | bytes 393224 | tf_op jit(solution)/shard_map/ppermute | solution.py:648
  34.0 13.1 %all-to-all-start.2 = ((f32[8,16,512]{2,1,0:T(8,128)}), f32[8,16,512]{2,1,0:T(8,128)S(1)}, u32[]{:S(2)}, u32[]{:S(2)}) async-start(f32[8,16,512]{2,1,0:T(8,128)} %bitcast.27), calls=%async_computation.2 | async-start | bytes 524288 | tf_op jit(solution)/shard_map/all_to_all | solution.py:645
  37.4 6.5 %collective-permute-start.3 = (f32[64,512]{1,0:T(8,128)S(1)}, f32[64,512]{1,0:T(8,128)S(1)}, u32[]{:S(2)}, u32[]{:S(2)}) collective-permute-start(f32[64,512]{1,0:T(8,128)S(1)} %get-tuple-element.54.bottom), channel_id=1, source_target_pairs={{8,0},{16,8},{24,16},{0,24},{9,1},{17,9},{25,17},{1,25},{10,2},{18... | collective-permute-start | bytes 393224 | tf_op jit(solution)/shard_map/ppermute | solution.py:651
  49.9 9.6 %all-to-all-start.3 = ((f32[32,1,128]{2,1,0:T(1,128)}), f32[32,1,128]{2,1,0:T(1,128)S(1)}, u32[]{:S(2)}, u32[]{:S(2)}) async-start(f32[32,1,128]{2,1,0:T(1,128)} %get-tuple-element.62), calls=%async_computation.3 | async-start | bytes 32768 | tf_op jit(solution)/shard_map/all_to_all | solution.py:720

commit v5 on v4

--- a/solution.py
+++ b/solution.py
@@ -126,34 +126,11 @@
             placed(c + 1, lanes, gather_lanes(jnp.where(low, second, first), back_next))
 
 
-def wishes_body(owned, capacity, faces, out, marks, ids, semaphores):
-    begin(faces, ids, semaphores.at[0]).wait()
-    row = jnp.concatenate([ids[2:3, :], ids[3:4, :]], axis=1)
-    owner, slot = lax.div(row, owned), lax.rem(row, owned)
-    count = row.shape[1]
-    crossing = owner != lax.axis_index("dev")
-    same = (column_of(owner) == owner) & (iota((count, count), 0) < iota((count, count), 1))
-    rank = jnp.sum(jnp.where(same, 1.0, 0.0), axis=0, keepdims=True).astype(I32)
-    first = lax.rem(jnp.concatenate([ids[0:1, :], ids[1:2, :]], axis=1), owned)
-    place = jnp.where(crossing, owner * (2 * capacity) + rank, -1)
-    here = jnp.where(crossing, -1, slot)
-    marks[...] = jnp.concatenate(
-        [place, first, here, jnp.zeros((marks.shape[0] - 3, count), I32)], axis=0
-    )
-    shape = (out.shape[0], count)
-    line = iota(shape, 0)
-    line = line - jnp.where(lax.rem(line, 2 * capacity) >= capacity, capacity, 0)
-    chosen = jnp.where(line == place, (slot + 1).astype(F32), 0.0)
-    out[...] = jnp.broadcast_to(
-        jnp.sum(chosen, axis=1, keepdims=True).astype(I32), out.shape
-    )
-
-
-def start_body(
-    face_nodes, source, inverse, coupling, codes, scales, solved, sides, bottom, top, table,
-    source_here, inverse_here, coupling_here, orientation, scale, image, flat, semaphores
-):
-    small = [begin(codes, orientation, semaphores.at[5]), begin(scales, scale, semaphores.at[6])]
+def solve_body(
+    face_nodes, source, inverse, coupling, codes, scales, solved, coupling_here, table,
+    source_here, inverse_here, orientation, scale, semaphores
+):
+    small = [begin(codes, orientation, semaphores.at[4]), begin(scales, scale, semaphores.at[5])]
     depth = inverse.shape[0] // 2
     reads = []
     for k in range(2):
@@ -164,20 +141,20 @@
                 begin(source.at[:, part], source_here.at[:, part], semaphores.at[2 * k + 1]),
             )
         )
-    read_coupling = begin(coupling, coupling_here, semaphores.at[4])
+    read_coupling = begin(coupling, coupling_here, semaphores.at[6])
     columns = orientation.shape[0]
     count = orientation.shape[1]
     edge = math.isqrt(face_nodes)
     pair = 2 * face_nodes
     lane = iota((count, pair), 1)
-    half = lane - lax.rem(lane, face_nodes)
+    side = lane - lax.rem(lane, face_nodes)
     node = lax.rem(lane, face_nodes)
     a, b = lax.div(node, edge), lax.rem(node, edge)
     for read in small:
         read.wait()
     scaled = column_of(scale[...]) * (pair * pair)
     for c in range(columns):
-        turned = half if c % 2 == 0 else face_nodes - half
+        turned = side if c % 2 == 0 else face_nodes - side
         code = jnp.broadcast_to(column_of(orientation[c : c + 1, :]), (count, pair))
         swapped = (code & 4) != 0
         first = (code & 2) != 0
@@ -190,6 +167,21 @@
         j = jnp.where(second, edge - 1 - j, j)
         back = turned + i * edge + j
         table[c * count : (c + 1) * count, :] = forward + pair * back + scaled
+    for k, pieces in enumerate(reads):
+        for piece in pieces:
+            piece.wait()
+        depths = slice(k * depth, (k + 1) * depth)
+        product = dot_split(halves(source_here[:, depths]), halves(inverse_here[depths, :]))
+        solved[...] = product if k == 0 else solved[...] + product
+    read_coupling.wait()
+
+
+def condense_body(
+    solved, coupling, table, solved_out, sides, bottom, top, flat, semaphores
+):
+    write = begin(solved, solved_out, semaphores.at[0])
+    count = bottom.shape[0]
+    columns = table.shape[0] // count
     has_below, has_above = layer_masks()
     side_columns = columns - 2
 
@@ -201,20 +193,12 @@
         else:
             top[:, lanes] = value * has_above
 
-    pairs = sides.shape[1] // pair
+    pairs = sides.shape[1] // table.shape[1]
     parts = [range(0, pairs // 2), range(pairs // 2, pairs)]
-    for k, pieces in enumerate(reads):
-        for piece in pieces:
-            piece.wait()
-        depths = slice(k * depth, (k + 1) * depth)
-        product = dot_split(halves(source_here[:, depths]), halves(inverse_here[depths, :]))
-        image[...] = product if k == 0 else image[...] + product
-    read_coupling.wait()
-    split_coupling = halves(coupling_here[...])
+    split = halves(coupling[...])
     for part in parts:
         rows = slice(2 * part[0] * count, 2 * (part[-1] + 1) * count)
-        flat[rows, :] = dot_split(halves(image[rows, :]), split_coupling)
-    write = begin(image, solved, semaphores.at[7])
+        flat[rows, :] = dot_split(halves(solved[rows, :]), split)
     for part in parts:
         from_flat(flat, table, placed, count, part, range(columns))
     write.wait()
@@ -244,7 +228,44 @@
     return taken, given.astype(F32)
 
 
-def send_body(capacity, marks, wanted, sides, send):
+def names_body(owned, capacity, block_of, ids, *refs):
+    *others, sides, send, wanted, marks = refs
+    here = lax.axis_index("dev")
+
+    def second(rows, at):
+        return jnp.concatenate([rows[at + 2 : at + 3, :], rows[at + 3 : at + 4, :]], axis=1)
+
+    names = jnp.concatenate(
+        [second(rows, at) for rows in others for at in range(0, rows.shape[0], ids.shape[0])], axis=0
+    )
+    blocks, count = names.shape
+    earlier = (iota((count, count), 0) < iota((count, count), 1)).astype(F32).astype(BF16)
+    block = block_of(iota((blocks, count), 0), here)
+    row = second(ids, 0)
+    owner, slot = lax.div(row, owned), lax.rem(row, owned)
+    crossing = owner != here
+    named = (lax.div(names, owned) == here) & (block != here)
+    own = (block == owner) & crossing
+    masks = jnp.concatenate([named.astype(F32), own.astype(F32)], axis=0).astype(BF16)
+    ranks = dot(masks, earlier)
+    place = jnp.where(own, (block * (2 * capacity)).astype(F32) + ranks[blocks:, :] + 1.0, 0.0)
+    place = jnp.sum(place, axis=0, keepdims=True).astype(I32) - 1
+    first = lax.rem(jnp.concatenate([ids[0:1, :], ids[1:2, :]], axis=1), owned)
+    marks[...] = jnp.concatenate(
+        [place, first, jnp.where(crossing, -1, slot), jnp.zeros((marks.shape[0] - 3, count), I32)],
+        axis=0,
+    )
+    shape = (send.shape[0], blocks)
+    line = iota(shape, 0)
+    of_line = block_of(iota(shape, 1), here) == lax.div(line, 2 * capacity)
+    of_line = of_line.astype(F32).astype(BF16)
+    rank_here = dot(of_line, jnp.where(named, ranks[:blocks, :], -1.0).astype(BF16))
+    slot_here = dot(of_line, lax.rem(names, owned).astype(F32).astype(BF16))
+    line = lax.rem(iota(rank_here.shape, 0), capacity).astype(F32)
+    chosen = jnp.where(rank_here == line, slot_here + 1.0, 0.0)
+    wanted[...] = jnp.broadcast_to(
+        jnp.sum(chosen, axis=1, keepdims=True).astype(I32), wanted.shape
+    )
     taken, _ = places(capacity, marks, wanted)
     send[...] = pick(taken.astype(BF16), sides[...])
 
@@ -650,27 +671,37 @@
     def sink(value):
         return lax.ppermute(value, "gz", [((at + 1) % layers, at) for at in range(layers)])
 
-    wishes, marks = call(
-        functools.partial(wishes_body, owned, capacity),
-        [((lines, owned), I32), ((8, owned), I32)],
-        [Raw(ids)],
-        [(ids.shape, I32)],
+    if blocks & (blocks - 1) == 0:
+        gathered, received = [], ids
+        for step in [2**k for k in range(blocks.bit_length() - 1)]:
+            gathered = [jnp.concatenate(gathered + [received], axis=0)]
+            pairs = [(at, at ^ step) for at in range(blocks)]
+            received = lax.ppermute(gathered[0], "dev", pairs)
+        gathered = gathered + [received]
+        block_of = lambda row, here: row ^ here
+    else:
+        gathered = [lax.all_gather(ids, "dev", tiled=True)]
+        block_of = lambda row, here: row
+    solved, coupling_here, table = call(
+        functools.partial(solve_body, face_nodes),
+        [whole, ((nodes, traces), F32), table],
+        [Raw(flat_source), Raw(interior_inverse), Raw(coupling), Raw(codes), Raw(scale)],
+        [whole, ((nodes, nodes), F32), (codes.shape, I32), (scale.shape, I32)],
+        copies=7,
+        flops=6 * flat_rows * nodes * nodes,
+    )
+    solved, sides, bottom, top = call(
+        condense_body,
+        [whole + ("raw",)] + faces,
+        [solved, coupling_here, table],
+        [flat],
         copies=1,
-    )
-    wanted = across(wishes)
-    solved, sides, bottom, top, table = call(
-        functools.partial(start_body, face_nodes),
-        [whole + ("raw",)] + faces + [table],
-        [Raw(flat_source), Raw(interior_inverse), Raw(coupling), Raw(codes), Raw(scale)],
-        [whole, ((nodes, nodes), F32), ((nodes, traces), F32), (codes.shape, I32),
-         (scale.shape, I32), whole, flat],
-        copies=8,
-        flops=6 * flat_rows * nodes * (nodes + traces),
-    )
-    (send,) = call(
-        functools.partial(send_body, capacity),
-        [message],
-        [marks, wanted, sides],
+        flops=6 * flat_rows * nodes * traces,
+    )
+    send, wanted, marks = call(
+        functools.partial(names_body, owned, capacity, block_of),
+        [message, ((lines, owned), I32), ((8, owned), I32)],
+        [ids] + gathered + [sides],
         flops=400 * lines * side_rows * lanes,
     )
     up, down, received = climb(top), sink(bottom), across(send)

time: 62.7 us -> 61.4 us (0.979)
  Pallas kernels: 26 us -> 24.7 us
  other arithmetic: 0 us -> 0.7 us
    all_to_all x3 -> x2, starting transfers between devices: 14.2 us -> 7 us  [across(): return lax.all_to_all(parts, 'dev', 0, 0, tiled=True).reshape(message.shape)]
    ppermute x0 -> x3, starting transfers between devices: none -> 6.07 us  [per_device(): received = lax.ppermute(gathered[0], 'dev', pairs)]
    pallas_call x9, Pallas kernels: 26 us -> 24.7 us  [call(): pl.pallas_call(body, out_shape=[pltpu.HBM(*out[:2]) if len(out) > 2 else...]
    all_to_all x3 -> x2, waiting for transfers between devices: 7.66 us -> 6.45 us  [across(): return lax.all_to_all(parts, 'dev', 0, 0, tiled=True).reshape(message.shape)]
    ppermute x0 -> x3, waiting for transfers between devices: none -> 1.04 us  [per_device(): received = lax.ppermute(gathered[0], 'dev', pairs)]
    ppermute x2, starting transfers between devices: 2.99 us -> 3.93 us  [sink(): lax.ppermute(value, 'gz', [((at + 1) % layers, at) for at in range(layers)])]
    concatenate x0 -> x2, other arithmetic: none -> 0.7 us  [per_device(): gathered = [jnp.concatenate(gathered + [received], axis=0)]]
  transfers between devices with their start and end apart: 8 -> 10, of which waited for: 5 -> 4; matrix products, arithmetic and copies ran while one was open for 0% -> 0% of each run, Pallas kernels for 26% -> 27%
where the time goes in v5:
time: 61.4 us; the launch traced here: 60.8 us
  Pallas kernels  24.7 us (40%)
  starting transfers between devices  22.7 us (37%)
  waiting for transfers between devices  12 us (20%)
  between operations  0.73 us (1%)
  other arithmetic  0.7 us (1%)
    pallas_call x9, Pallas kernels, call(): pl.pallas_call(body, out_shape=[pltpu.HBM(*out[:2]) if len(out) > 2 else...  24.7 us
    all_to_all x2, starting transfers between devices, across(): return lax.all_to_all(parts, 'dev', 0, 0, tiled=True).reshape(message.shape)  7 us
    all_to_all x2, waiting for transfers between devices, across(): return lax.all_to_all(parts, 'dev', 0, 0, tiled=True).reshape(message.shape)  6.45 us
    ppermute x3, starting transfers between devices, per_device(): received = lax.ppermute(gathered[0], 'dev', pairs)  6.07 us
    all_to_all x1, waiting for transfers between devices, per_device(): stats = lax.all_to_all(stats, ('gz', 'dev'), 0, 0, tiled=True)  4.5 us
    ppermute x2, starting transfers between devices, sink(): lax.ppermute(value, 'gz', [((at + 1) % layers, at) for at in range(layers)])  3.93 us
    ppermute x2, starting transfers between devices, climb(): lax.ppermute(value, 'gz', [(at, (at + 1) % layers) for at in range(layers)])  3.09 us
    all_to_all x1, starting transfers between devices, per_device(): stats = lax.all_to_all(stats, ('gz', 'dev'), 0, 0, tiled=True)  2.57 us
  transfers between devices with their start and end apart: 10, of which 4 were waited for; matrix products, arithmetic and copies ran while one was open for 0% of the time, Pallas kernels for 27%

profile of v5, /device:TPU:0, one launch (start us, length us, event | category | flops | bytes accessed | tf_op | source)
XLA Modules:
  0.0 60.8 jit_solution(4251318743533925438)
XLA Ops:
  0.6 0.5 collective-permute-start
  1.1 1.0 %collective-permute-done = s32[4,64]{1,0:T(4,128)S(1)} collective-permute-done((s32[4,64]{1,0:T(4,128)}, s32[4,64]{1,0:T(4,128)S(1)}, u32[]{:S(2)}, u32[]{:S(2)}) %collective-permute-start) | collective-permute-done | bytes 1056 | tf_op jit(solution)/shard_map/ppermute | solution.py:679
  2.2 0.7 %pad_add_fusion.1 = s32[8,64]{1,0:T(8,128)S(1)} fusion(s32[4,64]{1,0:T(4,128)S(1)} %collective-permute-done, s32[4,64]{1,0:T(4,128)} %bitcast.20), kind=kLoop, calls=%fused_computation.1 | loop fusion | flops 512 | bytes 4096 | tf_op jit(solution)/shard_map/concatenate | solution.py:677
  2.9 2.9 %collective-permute-start.1 = (s32[8,64]{1,0:T(8,128)S(1)}, s32[8,64]{1,0:T(8,128)S(1)}, u32[]{:S(2)}, u32[]{:S(2)}) collective-permute-start(s32[8,64]{1,0:T(8,128)S(1)} %pad_add_fusion.1), channel_id=1, source_target_pairs={{0,2},{1,3},{2,0},{3,1},{4,6},{5,7},{6,4},{7,5},{8,10},{9,11},{10,... | collective-permute-start | bytes 6152 | tf_op jit(solution)/shard_map/ppermute | solution.py:679
  5.8 2.3 %shard_map.94 = (f32[512,512]{1,0:T(8,128)S(1)}, f32[512,384]{1,0:T(8,128)S(1)}, s32[384,128]{1,0:T(8,128)S(1)}) custom-call(f32[512,512]{1,0:T(8,128)} %bitcast.28, f32[512,512]{1,0:T(8,128)} %inverse.3, f32[512,384]{1,0:T(8,128)} %coupling.3, s32[6,64]{1,0:T(8,128)} %bitcast.30, s32[1,64]{1,0:T(1,128)} %bitcast.31), custom_call_target="tpu_custom_call" | custom-call | flops 805306368 | bytes 2885376 | tf_op jit(solution)/shard_map/pallas_call | solution.py:32
  8.2 2.6 %collective-permute-start.2 = (s32[16,64]{1,0:T(8,128)S(1)}, s32[16,64]{1,0:T(8,128)S(1)}, u32[]{:S(2)}, u32[]{:S(2)}) collective-permute-start(s32[16,64]{1,0:T(8,128)S(1)} %pad_add_fusion.refs_0_), channel_id=1, source_target_pairs={{0,4},{1,5},{2,6},{3,7},{4,0},{5,1},{6,2},{7,3},{8,12},{9,13},{10,... | collective-permute-start | bytes 12296 | tf_op jit(solution)/shard_map/ppermute | solution.py:679
  10.8 1.4 %shard_map.95 = (f32[512,512]{1,0:T(8,128)}, f32[256,512]{1,0:T(8,128)S(1)}, f32[64,512]{1,0:T(8,128)S(1)}, f32[64,512]{1,0:T(8,128)S(1)}) custom-call(f32[512,512]{1,0:T(8,128)S(1)} %get-tuple-element.43.solved, f32[512,384]{1,0:T(8,128)S(1)} %get-tuple-element.44.coupling, s32[384,128]{1,0:T(8,128)S(1)} %get-tuple-element.45.table), custom_call_target="tpu_custom_call" | custom-call | flops 603979776 | bytes 2031616 | tf_op jit(solution)/shard_map/pallas_call | solution.py:32
  12.2 1.5 %collective-permute-start.3 = (f32[64,512]{1,0:T(8,128)S(1)}, f32[64,512]{1,0:T(8,128)S(1)}, u32[]{:S(2)}, u32[]{:S(2)}) collective-permute-start(f32[64,512]{1,0:T(8,128)S(1)} %get-tuple-element.50.top), channel_id=1, source_target_pairs={{0,8},{8,16},{16,24},{24,0},{1,9},{9,17},{17,25},{25,1},{2,10},{10... | collective-permute-start | bytes 393224 | tf_op jit(solution)/shard_map/ppermute | solution.py:669
  13.7 1.3 %shard_map.96 = (f32[128,512]{1,0:T(8,128)}, s32[128,128]{1,0:T(8,128)S(1)}, s32[8,128]{1,0:T(8,128)S(1)}) custom-call(s32[4,64]{1,0:T(4,128)S(1)} %bitcast.22, s32[16,64]{1,0:T(8,128)S(1)} %pad_add_fusion.refs_0_, s32[16,64]{1,0:T(8,128)S(1)} %collective-permute-done.2.refs_1_, f32[256,512]{1,0:T(8,128)S(1)} %get-tuple-element.46.refs_2_.sides), custom_call_target="tpu_custom_call" | custom-call | flops 6710886400 | bytes 533504 | tf_op jit(solution)/shard_map/pallas_call | solution.py:32
  15.0 3.6 %all-to-all-start = ((f32[8,16,512]{2,1,0:T(8,128)}), f32[8,16,512]{2,1,0:T(8,128)S(1)}, u32[]{:S(2)}, u32[]{:S(2)}) async-start(f32[8,16,512]{2,1,0:T(8,128)} %bitcast.5), calls=%async_computation | async-start | bytes 524288 | tf_op jit(solution)/shard_map/all_to_all | solution.py:666
  18.6 2.4 %collective-permute-start.4 = (f32[64,512]{1,0:T(8,128)S(1)}, f32[64,512]{1,0:T(8,128)S(1)}, u32[]{:S(2)}, u32[]{:S(2)}) collective-permute-start(f32[64,512]{1,0:T(8,128)S(1)} %get-tuple-element.49.bottom), channel_id=1, source_target_pairs={{8,0},{16,8},{24,16},{0,24},{9,1},{17,9},{25,17},{1,25},{10,2},{18... | collective-permute-start | bytes 393224 | tf_op jit(solution)/shard_map/ppermute | solution.py:672
  21.1 3.9 %shard_map.97 = (bf16[128,896]{1,0:T(8,128)(2,1)S(1)}, f32[256,512]{1,0:T(8,128)S(1)}, f32[64,512]{1,0:T(8,128)S(1)}, bf16[2,512,384]{2,1,0:T(8,128)(2,1)}, bf16[2,384,384]{2,1,0:T(8,128)(2,1)S(1)}) custom-call(s32[8,128]{1,0:T(8,128)S(1)} %get-tuple-element.47.marks, s32[128,128]{1,0:T(8,128)S(1)} %get-tuple-element.48.wanted, ...), custom_call_target="tpu_custom_call" | custom-call | flops 4026531840 | bytes 3280896 | tf_op jit(solution)/shard_map/pallas_call | solution.py:32
  25.0 3.3 %all-to-all-done = f32[8,16,512]{2,1,0:T(8,128)S(1)} async-done(((f32[8,16,512]{2,1,0:T(8,128)}), f32[8,16,512]{2,1,0:T(8,128)S(1)}, u32[]{:S(2)}, u32[]{:S(2)}) %all-to-all-start) | async-done | bytes 262176 | tf_op jit(solution)/shard_map/all_to_all | solution.py:666
  28.4 2.8 %shard_map.98 = (f32[192,512]{1,0:T(8,128)}, f32[512,384]{1,0:T(8,128)}, f32[256,512]{1,0:T(8,128)S(1)}, f32[64,512]{1,0:T(8,128)S(1)}, f32[64,512]{1,0:T(8,128)S(1)}, /*index=5*/f32[128,512]{1,0:T(8,128)}) custom-call(f32[256,512]{1,0:T(8,128)S(1)} %get-tuple-element.51.base, bf16[128,896]{1,0:T(8,128)(2,1)S(1)} %get-tuple-element.52.maps, ...), custom_call_target="tpu_custom_call" | custom-call | flops 452984832 | bytes 3014656 | tf_op jit(solution)/shard_map/pallas_call | solution.py:32
  31.2 1.5 %collective-permute-start.5 = (f32[64,512]{1,0:T(8,128)S(1)}, f32[64,512]{1,0:T(8,128)S(1)}, u32[]{:S(2)}, u32[]{:S(2)}) collective-permute-start(f32[64,512]{1,0:T(8,128)S(1)} %get-tuple-element.61.top), channel_id=1, source_target_pairs={{0,8},{8,16},{16,24},{24,0},{1,9},{9,17},{17,25},{25,1},{2,10},{10... | collective-permute-start | bytes 393224 | tf_op jit(solution)/shard_map/ppermute | solution.py:669
  32.8 3.4 %all-to-all-start.1 = ((f32[8,16,512]{2,1,0:T(8,128)}), f32[8,16,512]{2,1,0:T(8,128)S(1)}, u32[]{:S(2)}, u32[]{:S(2)}) async-start(f32[8,16,512]{2,1,0:T(8,128)} %bitcast.27), calls=%async_computation.1 | async-start | bytes 524288 | tf_op jit(solution)/shard_map/all_to_all | solution.py:666
  36.2 1.5 %collective-permute-start.6 = (f32[64,512]{1,0:T(8,128)S(1)}, f32[64,512]{1,0:T(8,128)S(1)}, u32[]{:S(2)}, u32[]{:S(2)}) collective-permute-start(f32[64,512]{1,0:T(8,128)S(1)} %get-tuple-element.60.bottom), channel_id=1, source_target_pairs={{8,0},{16,8},{24,16},{0,24},{9,1},{17,9},{25,17},{1,25},{10,2},{18... | collective-permute-start | bytes 393224 | tf_op jit(solution)/shard_map/ppermute | solution.py:672
  37.7 5.0 %shard_map.99 = (f32[512,512]{1,0:T(8,128)}, f32[512,128]{1,0:T(8,128)}, f32[512,64]{1,0:T(8,128)}, f32[512,384]{1,0:T(8,128)}, f32[256,512]{1,0:T(8,128)S(1)}, ...) custom-call(f32[192,512]{1,0:T(8,128)} %get-tuple-element.56.mine_in, ...), custom_call_target="tpu_custom_call" | custom-call | flops 4026531840 | bytes 4325376 | tf_op jit(solution)/shard_map/pallas_call | solution.py:32
  42.7 3.1 %all-to-all-done.1 = f32[8,16,512]{2,1,0:T(8,128)S(1)} async-done(((f32[8,16,512]{2,1,0:T(8,128)}), f32[8,16,512]{2,1,0:T(8,128)S(1)}, u32[]{:S(2)}, u32[]{:S(2)}) %all-to-all-start.1) | async-done | bytes 262176 | tf_op jit(solution)/shard_map/all_to_all | solution.py:666
  45.8 2.8 %shard_map.100 = (f32[192,512]{1,0:T(8,128)}, f32[512,384]{1,0:T(8,128)}, f32[32,1,128]{2,1,0:T(1,128)}) custom-call(f32[256,512]{1,0:T(8,128)S(1)} %get-tuple-element.62.base, bf16[128,896]{1,0:T(8,128)(2,1)S(1)} %get-tuple-element.52.maps, f32[128,512]{1,0:T(8,128)S(1)} %bitcast.17, f32[64,512]{1,0:T(8,128)S(1)} %get-tuple-element.64.below, ...), custom_call_target="tpu_custom_call" | custom-call | flops 452984832 | bytes 5013504 | tf_op jit(solution)/shard_map/pallas_call | solution.py:32
  48.6 2.6 %all-to-all-start.2 = ((f32[32,1,128]{2,1,0:T(1,128)}), f32[32,1,128]{2,1,0:T(1,128)S(1)}, u32[]{:S(2)}, u32[]{:S(2)}) async-start(f32[32,1,128]{2,1,0:T(1,128)} %get-tuple-element.68), calls=%async_computation.2 | async-start | bytes 32768 | tf_op jit(solution)/shard_map/all_to_all | solution.py:751
  51.2 2.6 %shard_map.101 = (f32[512,512]{1,0:T(8,128)S(1)}, f32[512,128]{1,0:T(8,128)}, f32[512,64]{1,0:T(8,128)}, f32[512,512]{1,0:T(8,128)S(1)}, f32[64,128]{1,0:T(8,128)S(1)}) custom-call(f32[192,512]{1,0:T(8,128)} %get-tuple-element.70.mine_in, f32[512,384]{1,0:T(8,128)} %get-tuple-element.71.flat_in, bf16[2,512,384]{2,1,0:T(8,128)(2,1)} %get-tuple-element.58.lift_in, ...), custom_call_target="tpu_custom_call" | custom-call | flops 603979776 | bytes 4456448 | tf_op jit(solution)/shard_map/pallas_call | solution.py:32
  53.8 4.5 %all-to-all-done.2.stats = f32[32,1,128]{2,1,0:T(1,128)S(1)} async-done(((f32[32,1,128]{2,1,0:T(1,128)}), f32[32,1,128]{2,1,0:T(1,128)S(1)}, u32[]{:S(2)}, u32[]{:S(2)}) %all-to-all-start.2) | async-done | bytes 16416 | tf_op jit(solution)/shard_map/all_to_all | solution.py:751
  58.3 2.5 %shard_map.102 = (f32[512,512]{1,0:T(8,128)}, f32[64,8,128]{2,1,0:T(8,128)}, f32[64,8,64]{2,1,0:T(8,128)}) custom-call(f32[32,1,128]{2,1,0:T(1,128)S(1)} %all-to-all-done.2.stats, f32[64,8,128]{2,1,0:T(8,128)} %bitcast.23, f32[64,8,128]{2,1,0:T(8,128)} %bitcast.25, f32[64,8,64]{2,1,0:T(8,128)} %bitcast.24, f32[64,8,64]{2,1,0:T(8,128)} %bitcast.26, ...), custom_call_target="tpu_custom_call" | custom-call | bytes 3981312 | tf_op jit(solution)/shard_map/pallas_call | solution.py:32
  (9 shorter events, 0.0 us)
Async XLA Ops:
  0.6 1.5 %collective-permute-start = (s32[4,64]{1,0:T(4,128)}, s32[4,64]{1,0:T(4,128)S(1)}, u32[]{:S(2)}, u32[]{:S(2)}) collective-permute-start(s32[4,64]{1,0:T(4,128)} %bitcast.19), channel_id=1, source_target_pairs={{0,1},{1,0},{2,3},{3,2},{4,5},{5,4},{6,7},{7,6},{8,9},{9,8},{10,11... | collective-permute-start | bytes 3080 | tf_op jit(solution)/shard_map/ppermute | solution.py:679
  2.9 5.3 %collective-permute-start.1 = (s32[8,64]{1,0:T(8,128)S(1)}, s32[8,64]{1,0:T(8,128)S(1)}, u32[]{:S(2)}, u32[]{:S(2)}) collective-permute-start(s32[8,64]{1,0:T(8,128)S(1)} %pad_add_fusion.1), channel_id=1, source_target_pairs={{0,2},{1,3},{2,0},{3,1},{4,6},{5,7},{6,4},{7,5},{8,10},{9,11},{10,... | collective-permute-start | bytes 6152 | tf_op jit(solution)/shard_map/ppermute | solution.py:679
  5.8 2.4 %copy-start = (s32[64,4]{0,1:T(4,128)S(1)}, s32[64,4]{0,1:T(4,128)}, u32[]{:S(2)}) copy-start(s32[64,4]{0,1:T(4,128)} %param.11) | copy-start | bytes 3076
  8.2 5.6 %collective-permute-start.2 = (s32[16,64]{1,0:T(8,128)S(1)}, s32[16,64]{1,0:T(8,128)S(1)}, u32[]{:S(2)}, u32[]{:S(2)}) collective-permute-start(s32[16,64]{1,0:T(8,128)S(1)} %pad_add_fusion.refs_0_), channel_id=1, source_target_pairs={{0,4},{1,5},{2,6},{3,7},{4,0},{5,1},{6,2},{7,3},{8,12},{9,13},{10,... | collective-permute-start | bytes 12296 | tf_op jit(solution)/shard_map/ppermute | solution.py:679
  12.2 8.9 %collective-permute-start.3 = (f32[64,512]{1,0:T(8,128)S(1)}, f32[64,512]{1,0:T(8,128)S(1)}, u32[]{:S(2)}, u32[]{:S(2)}) collective-permute-start(f32[64,512]{1,0:T(8,128)S(1)} %get-tuple-element.50.top), channel_id=1, source_target_pairs={{0,8},{8,16},{16,24},{24,0},{1,9},{9,17},{17,25},{25,1},{2,10},{10... | collective-permute-start | bytes 393224 | tf_op jit(solution)/shard_map/ppermute | solution.py:669
  15.0 13.3 %all-to-all-start = ((f32[8,16,512]{2,1,0:T(8,128)}), f32[8,16,512]{2,1,0:T(8,128)S(1)}, u32[]{:S(2)}, u32[]{:S(2)}) async-start(f32[8,16,512]{2,1,0:T(8,128)} %bitcast.5), calls=%async_computation | async-start | bytes 524288 | tf_op jit(solution)/shard_map/all_to_all | solution.py:666
  18.6 6.4 %collective-permute-start.4 = (f32[64,512]{1,0:T(8,128)S(1)}, f32[64,512]{1,0:T(8,128)S(1)}, u32[]{:S(2)}, u32[]{:S(2)}) collective-permute-start(f32[64,512]{1,0:T(8,128)S(1)} %get-tuple-element.49.bottom), channel_id=1, source_target_pairs={{8,0},{16,8},{24,16},{0,24},{9,1},{17,9},{25,17},{1,25},{10,2},{18... | collective-permute-start | bytes 393224 | tf_op jit(solution)/shard_map/ppermute | solution.py:672
  31.2 6.5 %collective-permute-start.5 = (f32[64,512]{1,0:T(8,128)S(1)}, f32[64,512]{1,0:T(8,128)S(1)}, u32[]{:S(2)}, u32[]{:S(2)}) collective-permute-start(f32[64,512]{1,0:T(8,128)S(1)} %get-tuple-element.61.top), channel_id=1, source_target_pairs={{0,8},{8,16},{16,24},{24,0},{1,9},{9,17},{17,25},{25,1},{2,10},{10... | collective-permute-start | bytes 393224 | tf_op jit(solution)/shard_map/ppermute | solution.py:669
  32.8 13.1 %all-to-all-start.1 = ((f32[8,16,512]{2,1,0:T(8,128)}), f32[8,16,512]{2,1,0:T(8,128)S(1)}, u32[]{:S(2)}, u32[]{:S(2)}) async-start(f32[8,16,512]{2,1,0:T(8,128)} %bitcast.27), calls=%async_computation.1 | async-start | bytes 524288 | tf_op jit(solution)/shard_map/all_to_all | solution.py:666
  36.2 6.5 %collective-permute-start.6 = (f32[64,512]{1,0:T(8,128)S(1)}, f32[64,512]{1,0:T(8,128)S(1)}, u32[]{:S(2)}, u32[]{:S(2)}) collective-permute-start(f32[64,512]{1,0:T(8,128)S(1)} %get-tuple-element.60.bottom), channel_id=1, source_target_pairs={{8,0},{16,8},{24,16},{0,24},{9,1},{17,9},{25,17},{1,25},{10,2},{18... | collective-permute-start | bytes 393224 | tf_op jit(solution)/shard_map/ppermute | solution.py:672
  48.6 9.7 %all-to-all-start.2 = ((f32[32,1,128]{2,1,0:T(1,128)}), f32[32,1,128]{2,1,0:T(1,128)S(1)}, u32[]{:S(2)}, u32[]{:S(2)}) async-start(f32[32,1,128]{2,1,0:T(1,128)} %get-tuple-element.68), calls=%async_computation.2 | async-start | bytes 32768 | tf_op jit(solution)/shard_map/all_to_all | solution.py:751

commit v6 on v5

--- a/solution.py
+++ b/solution.py
@@ -672,12 +672,12 @@
         return lax.ppermute(value, "gz", [((at + 1) % layers, at) for at in range(layers)])
 
     if blocks & (blocks - 1) == 0:
-        gathered, received = [], ids
+        gathered = [ids]
         for step in [2**k for k in range(blocks.bit_length() - 1)]:
-            gathered = [jnp.concatenate(gathered + [received], axis=0)]
+            if len(gathered) == 4:
+                gathered = [jnp.concatenate(gathered, axis=0)]
             pairs = [(at, at ^ step) for at in range(blocks)]
-            received = lax.ppermute(gathered[0], "dev", pairs)
-        gathered = gathered + [received]
+            gathered = gathered + [lax.ppermute(entry, "dev", pairs) for entry in gathered]
         block_of = lambda row, here: row ^ here
     else:
         gathered = [lax.all_gather(ids, "dev", tiled=True)]

time: 61.4 us -> 60.7 us (0.989)
  starting transfers between devices: 22.7 us -> 23.7 us
  waiting for transfers between devices: 12 us -> 11 us
  other arithmetic: 0.7 us -> 0.01 us
    ppermute x3 -> x4, starting transfers between devices: 6.07 us -> 7.11 us  [per_device(): lax.ppermute(entry, 'dev', pairs)]
    ppermute x3 -> x4, waiting for transfers between devices: 1.04 us -> 0.01 us  [per_device(): lax.ppermute(entry, 'dev', pairs)]
    concatenate x2 -> x1, other arithmetic: 0.7 us -> 0.01 us  [per_device(): gathered = [jnp.concatenate(gathered, axis=0)]]
  transfers between devices with their start and end apart: 10 -> 11, of which waited for: 4 -> 3; matrix products, arithmetic and copies ran while one was open for 0% -> 0% of each run, Pallas kernels for 27% -> 28%
where the time goes in v6:
time: 60.7 us; the launch traced here: 60.1 us
  Pallas kernels  24.7 us (41%)
  starting transfers between devices  23.7 us (39%)
  waiting for transfers between devices  11 us (18%)
  between operations  0.74 us (1%)
    pallas_call x9, Pallas kernels, call(): pl.pallas_call(body, out_shape=[pltpu.HBM(*out[:2]) if len(out) > 2 else...  24.7 us
    ppermute x4, starting transfers between devices, per_device(): lax.ppermute(entry, 'dev', pairs)  7.11 us
    all_to_all x2, starting transfers between devices, across(): return lax.all_to_all(parts, 'dev', 0, 0, tiled=True).reshape(message.shape)  6.96 us
    all_to_all x2, waiting for transfers between devices, across(): return lax.all_to_all(parts, 'dev', 0, 0, tiled=True).reshape(message.shape)  6.44 us
    all_to_all x1, waiting for transfers between devices, per_device(): stats = lax.all_to_all(stats, ('gz', 'dev'), 0, 0, tiled=True)  4.5 us
    ppermute x2, starting transfers between devices, sink(): lax.ppermute(value, 'gz', [((at + 1) % layers, at) for at in range(layers)])  3.93 us
    ppermute x2, starting transfers between devices, climb(): lax.ppermute(value, 'gz', [(at, (at + 1) % layers) for at in range(layers)])  3.09 us
    all_to_all x1, starting transfers between devices, per_device(): stats = lax.all_to_all(stats, ('gz', 'dev'), 0, 0, tiled=True)  2.57 us
  transfers between devices with their start and end apart: 11, of which 3 were waited for; matrix products, arithmetic and copies ran while one was open for 0% of the time, Pallas kernels for 28%

profile of v6, /device:TPU:0, one launch (start us, length us, event | category | flops | bytes accessed | tf_op | source)
XLA Modules:
  0.0 60.1 jit_solution(5203489251621764679)
XLA Ops:
  0.6 0.5 collective-permute-start
  1.1 2.6 %collective-permute-start.1 = (s32[4,64]{1,0:T(4,128)}, s32[4,64]{1,0:T(4,128)S(1)}, u32[]{:S(2)}, u32[]{:S(2)}) collective-permute-start(s32[4,64]{1,0:T(4,128)} %bitcast.20), channel_id=1, source_target_pairs={{0,2},{1,3},{2,0},{3,1},{4,6},{5,7},{6,4},{7,5},{8,10},{9,11},{10,... | collective-permute-start | bytes 3080 | tf_op jit(solution)/shard_map/ppermute | solution.py:680
  3.8 1.3 %collective-permute-start.2 = (s32[4,64]{1,0:T(4,128)S(1)}, s32[4,64]{1,0:T(4,128)S(1)}, u32[]{:S(2)}, u32[]{:S(2)}) collective-permute-start(s32[4,64]{1,0:T(4,128)S(1)} %collective-permute-done), channel_id=1, source_target_pairs={{0,2},{1,3},{2,0},{3,1},{4,6},{5,7},{6,4},{7,5},{8,10},{9,11},{10,... | collective-permute-start | bytes 3080 | tf_op jit(solution)/shard_map/ppermute | solution.py:680
  5.1 2.3 %shard_map.94 = (f32[512,512]{1,0:T(8,128)S(1)}, f32[512,384]{1,0:T(8,128)S(1)}, s32[384,128]{1,0:T(8,128)S(1)}) custom-call(f32[512,512]{1,0:T(8,128)} %bitcast.28, f32[512,512]{1,0:T(8,128)} %inverse.3, f32[512,384]{1,0:T(8,128)} %coupling.3, s32[6,64]{1,0:T(8,128)} %bitcast.30, s32[1,64]{1,0:T(1,128)} %bitcast.31), custom_call_target="tpu_custom_call" | custom-call | flops 805306368 | bytes 2885376 | tf_op jit(solution)/shard_map/pallas_call | solution.py:32
  7.5 0.0 collective-permute-done.2
  7.5 2.7 %collective-permute-start.3 = (s32[16,64]{1,0:T(8,128)S(1)}, s32[16,64]{1,0:T(8,128)S(1)}, u32[]{:S(2)}, u32[]{:S(2)}) collective-permute-start(s32[16,64]{1,0:T(8,128)S(1)} %pad_add_fusion.refs_0_), channel_id=1, source_target_pairs={{0,4},{1,5},{2,6},{3,7},{4,0},{5,1},{6,2},{7,3},{8,12},{9,13},{10,... | collective-permute-start | bytes 12296 | tf_op jit(solution)/shard_map/ppermute | solution.py:680
  10.1 1.4 %shard_map.95 = (f32[512,512]{1,0:T(8,128)}, f32[256,512]{1,0:T(8,128)S(1)}, f32[64,512]{1,0:T(8,128)S(1)}, f32[64,512]{1,0:T(8,128)S(1)}) custom-call(f32[512,512]{1,0:T(8,128)S(1)} %get-tuple-element.43.solved, f32[512,384]{1,0:T(8,128)S(1)} %get-tuple-element.44.coupling, s32[384,128]{1,0:T(8,128)S(1)} %get-tuple-element.45.table), custom_call_target="tpu_custom_call" | custom-call | flops 603979776 | bytes 2031616 | tf_op jit(solution)/shard_map/pallas_call | solution.py:32
  11.5 1.5 %collective-permute-start.4 = (f32[64,512]{1,0:T(8,128)S(1)}, f32[64,512]{1,0:T(8,128)S(1)}, u32[]{:S(2)}, u32[]{:S(2)}) collective-permute-start(f32[64,512]{1,0:T(8,128)S(1)} %get-tuple-element.50.top), channel_id=1, source_target_pairs={{0,8},{8,16},{16,24},{24,0},{1,9},{9,17},{17,25},{25,1},{2,10},{10... | collective-permute-start | bytes 393224 | tf_op jit(solution)/shard_map/ppermute | solution.py:669
  13.1 1.3 %shard_map.96 = (f32[128,512]{1,0:T(8,128)}, s32[128,128]{1,0:T(8,128)S(1)}, s32[8,128]{1,0:T(8,128)S(1)}) custom-call(s32[4,64]{1,0:T(4,128)S(1)} %bitcast.22, s32[16,64]{1,0:T(8,128)S(1)} %pad_add_fusion.refs_0_, s32[16,64]{1,0:T(8,128)S(1)} %collective-permute-done.3.refs_1_, f32[256,512]{1,0:T(8,128)S(1)} %get-tuple-element.46.refs_2_.sides), custom_call_target="tpu_custom_call" | custom-call | flops 6710886400 | bytes 533504 | tf_op jit(solution)/shard_map/pallas_call | solution.py:32
  14.4 3.6 %all-to-all-start = ((f32[8,16,512]{2,1,0:T(8,128)}), f32[8,16,512]{2,1,0:T(8,128)S(1)}, u32[]{:S(2)}, u32[]{:S(2)}) async-start(f32[8,16,512]{2,1,0:T(8,128)} %bitcast.5), calls=%async_computation | async-start | bytes 524288 | tf_op jit(solution)/shard_map/all_to_all | solution.py:666
  17.9 2.4 %collective-permute-start.5 = (f32[64,512]{1,0:T(8,128)S(1)}, f32[64,512]{1,0:T(8,128)S(1)}, u32[]{:S(2)}, u32[]{:S(2)}) collective-permute-start(f32[64,512]{1,0:T(8,128)S(1)} %get-tuple-element.49.bottom), channel_id=1, source_target_pairs={{8,0},{16,8},{24,16},{0,24},{9,1},{17,9},{25,17},{1,25},{10,2},{18... | collective-permute-start | bytes 393224 | tf_op jit(solution)/shard_map/ppermute | solution.py:672
  20.4 4.0 %shard_map.97 = (bf16[128,896]{1,0:T(8,128)(2,1)S(1)}, f32[256,512]{1,0:T(8,128)S(1)}, f32[64,512]{1,0:T(8,128)S(1)}, bf16[2,512,384]{2,1,0:T(8,128)(2,1)}, bf16[2,384,384]{2,1,0:T(8,128)(2,1)S(1)}) custom-call(s32[8,128]{1,0:T(8,128)S(1)} %get-tuple-element.47.marks, s32[128,128]{1,0:T(8,128)S(1)} %get-tuple-element.48.wanted, ...), custom_call_target="tpu_custom_call" | custom-call | flops 4026531840 | bytes 3280896 | tf_op jit(solution)/shard_map/pallas_call | solution.py:32
  24.3 3.3 %all-to-all-done = f32[8,16,512]{2,1,0:T(8,128)S(1)} async-done(((f32[8,16,512]{2,1,0:T(8,128)}), f32[8,16,512]{2,1,0:T(8,128)S(1)}, u32[]{:S(2)}, u32[]{:S(2)}) %all-to-all-start) | async-done | bytes 262176 | tf_op jit(solution)/shard_map/all_to_all | solution.py:666
  27.7 2.8 %shard_map.98 = (f32[192,512]{1,0:T(8,128)}, f32[512,384]{1,0:T(8,128)}, f32[256,512]{1,0:T(8,128)S(1)}, f32[64,512]{1,0:T(8,128)S(1)}, f32[64,512]{1,0:T(8,128)S(1)}, /*index=5*/f32[128,512]{1,0:T(8,128)}) custom-call(f32[256,512]{1,0:T(8,128)S(1)} %get-tuple-element.51.base, bf16[128,896]{1,0:T(8,128)(2,1)S(1)} %get-tuple-element.52.maps, ...), custom_call_target="tpu_custom_call" | custom-call | flops 452984832 | bytes 3014656 | tf_op jit(solution)/shard_map/pallas_call | solution.py:32
  30.5 1.5 %collective-permute-start.6 = (f32[64,512]{1,0:T(8,128)S(1)}, f32[64,512]{1,0:T(8,128)S(1)}, u32[]{:S(2)}, u32[]{:S(2)}) collective-permute-start(f32[64,512]{1,0:T(8,128)S(1)} %get-tuple-element.61.top), channel_id=1, source_target_pairs={{0,8},{8,16},{16,24},{24,0},{1,9},{9,17},{17,25},{25,1},{2,10},{10... | collective-permute-start | bytes 393224 | tf_op jit(solution)/shard_map/ppermute | solution.py:669
  32.0 3.4 %all-to-all-start.1 = ((f32[8,16,512]{2,1,0:T(8,128)}), f32[8,16,512]{2,1,0:T(8,128)S(1)}, u32[]{:S(2)}, u32[]{:S(2)}) async-start(f32[8,16,512]{2,1,0:T(8,128)} %bitcast.27), calls=%async_computation.1 | async-start | bytes 524288 | tf_op jit(solution)/shard_map/all_to_all | solution.py:666
  35.5 1.5 %collective-permute-start.7 = (f32[64,512]{1,0:T(8,128)S(1)}, f32[64,512]{1,0:T(8,128)S(1)}, u32[]{:S(2)}, u32[]{:S(2)}) collective-permute-start(f32[64,512]{1,0:T(8,128)S(1)} %get-tuple-element.60.bottom), channel_id=1, source_target_pairs={{8,0},{16,8},{24,16},{0,24},{9,1},{17,9},{25,17},{1,25},{10,2},{18... | collective-permute-start | bytes 393224 | tf_op jit(solution)/shard_map/ppermute | solution.py:672
  37.0 5.0 %shard_map.99 = (f32[512,512]{1,0:T(8,128)}, f32[512,128]{1,0:T(8,128)}, f32[512,64]{1,0:T(8,128)}, f32[512,384]{1,0:T(8,128)}, f32[256,512]{1,0:T(8,128)S(1)}, ...) custom-call(f32[192,512]{1,0:T(8,128)} %get-tuple-element.56.mine_in, ...), custom_call_target="tpu_custom_call" | custom-call | flops 4026531840 | bytes 4325376 | tf_op jit(solution)/shard_map/pallas_call | solution.py:32
  42.0 3.1 %all-to-all-done.1 = f32[8,16,512]{2,1,0:T(8,128)S(1)} async-done(((f32[8,16,512]{2,1,0:T(8,128)}), f32[8,16,512]{2,1,0:T(8,128)S(1)}, u32[]{:S(2)}, u32[]{:S(2)}) %all-to-all-start.1) | async-done | bytes 262176 | tf_op jit(solution)/shard_map/all_to_all | solution.py:666
  45.1 2.8 %shard_map.100 = (f32[192,512]{1,0:T(8,128)}, f32[512,384]{1,0:T(8,128)}, f32[32,1,128]{2,1,0:T(1,128)}) custom-call(f32[256,512]{1,0:T(8,128)S(1)} %get-tuple-element.62.base, bf16[128,896]{1,0:T(8,128)(2,1)S(1)} %get-tuple-element.52.maps, f32[128,512]{1,0:T(8,128)S(1)} %bitcast.17, f32[64,512]{1,0:T(8,128)S(1)} %get-tuple-element.64.below, ...), custom_call_target="tpu_custom_call" | custom-call | flops 452984832 | bytes 5013504 | tf_op jit(solution)/shard_map/pallas_call | solution.py:32
  47.9 2.6 %all-to-all-start.2 = ((f32[32,1,128]{2,1,0:T(1,128)}), f32[32,1,128]{2,1,0:T(1,128)S(1)}, u32[]{:S(2)}, u32[]{:S(2)}) async-start(f32[32,1,128]{2,1,0:T(1,128)} %get-tuple-element.68), calls=%async_computation.2 | async-start | bytes 32768 | tf_op jit(solution)/shard_map/all_to_all | solution.py:751
  50.5 2.6 %shard_map.101 = (f32[512,512]{1,0:T(8,128)S(1)}, f32[512,128]{1,0:T(8,128)}, f32[512,64]{1,0:T(8,128)}, f32[512,512]{1,0:T(8,128)S(1)}, f32[64,128]{1,0:T(8,128)S(1)}) custom-call(f32[192,512]{1,0:T(8,128)} %get-tuple-element.70.mine_in, f32[512,384]{1,0:T(8,128)} %get-tuple-element.71.flat_in, bf16[2,512,384]{2,1,0:T(8,128)(2,1)} %get-tuple-element.58.lift_in, ...), custom_call_target="tpu_custom_call" | custom-call | flops 603979776 | bytes 4456448 | tf_op jit(solution)/shard_map/pallas_call | solution.py:32
  53.1 4.5 %all-to-all-done.2.stats = f32[32,1,128]{2,1,0:T(1,128)S(1)} async-done(((f32[32,1,128]{2,1,0:T(1,128)}), f32[32,1,128]{2,1,0:T(1,128)S(1)}, u32[]{:S(2)}, u32[]{:S(2)}) %all-to-all-start.2) | async-done | bytes 16416 | tf_op jit(solution)/shard_map/all_to_all | solution.py:751
  57.6 2.5 %shard_map.102 = (f32[512,512]{1,0:T(8,128)}, f32[64,8,128]{2,1,0:T(8,128)}, f32[64,8,64]{2,1,0:T(8,128)}) custom-call(f32[32,1,128]{2,1,0:T(1,128)S(1)} %all-to-all-done.2.stats, f32[64,8,128]{2,1,0:T(8,128)} %bitcast.23, f32[64,8,128]{2,1,0:T(8,128)} %bitcast.25, f32[64,8,64]{2,1,0:T(8,128)} %bitcast.24, f32[64,8,64]{2,1,0:T(8,128)} %bitcast.26, ...), custom_call_target="tpu_custom_call" | custom-call | bytes 3981312 | tf_op jit(solution)/shard_map/pallas_call | solution.py:32
  (10 shorter events, 0.0 us)
Async XLA Ops:
  0.6 3.2 %collective-permute-start = (s32[4,64]{1,0:T(4,128)}, s32[4,64]{1,0:T(4,128)S(1)}, u32[]{:S(2)}, u32[]{:S(2)}) collective-permute-start(s32[4,64]{1,0:T(4,128)} %bitcast.19), channel_id=1, source_target_pairs={{0,1},{1,0},{2,3},{3,2},{4,5},{5,4},{6,7},{7,6},{8,9},{9,8},{10,11... | collective-permute-start | bytes 3080 | tf_op jit(solution)/shard_map/ppermute | solution.py:680
  1.1 6.3 %collective-permute-start.1 = (s32[4,64]{1,0:T(4,128)}, s32[4,64]{1,0:T(4,128)S(1)}, u32[]{:S(2)}, u32[]{:S(2)}) collective-permute-start(s32[4,64]{1,0:T(4,128)} %bitcast.20), channel_id=1, source_target_pairs={{0,2},{1,3},{2,0},{3,1},{4,6},{5,7},{6,4},{7,5},{8,10},{9,11},{10,... | collective-permute-start | bytes 3080 | tf_op jit(solution)/shard_map/ppermute | solution.py:680
  3.8 3.7 %collective-permute-start.2 = (s32[4,64]{1,0:T(4,128)S(1)}, s32[4,64]{1,0:T(4,128)S(1)}, u32[]{:S(2)}, u32[]{:S(2)}) collective-permute-start(s32[4,64]{1,0:T(4,128)S(1)} %collective-permute-done), channel_id=1, source_target_pairs={{0,2},{1,3},{2,0},{3,1},{4,6},{5,7},{6,4},{7,5},{8,10},{9,11},{10,... | collective-permute-start | bytes 3080 | tf_op jit(solution)/shard_map/ppermute | solution.py:680
  5.1 2.4 %copy-start = (s32[64,4]{0,1:T(4,128)S(1)}, s32[64,4]{0,1:T(4,128)}, u32[]{:S(2)}) copy-start(s32[64,4]{0,1:T(4,128)} %param.11) | copy-start | bytes 3076
  7.5 5.6 %collective-permute-start.3 = (s32[16,64]{1,0:T(8,128)S(1)}, s32[16,64]{1,0:T(8,128)S(1)}, u32[]{:S(2)}, u32[]{:S(2)}) collective-permute-start(s32[16,64]{1,0:T(8,128)S(1)} %pad_add_fusion.refs_0_), channel_id=1, source_target_pairs={{0,4},{1,5},{2,6},{3,7},{4,0},{5,1},{6,2},{7,3},{8,12},{9,13},{10,... | collective-permute-start | bytes 12296 | tf_op jit(solution)/shard_map/ppermute | solution.py:680
  11.5 8.9 %collective-permute-start.4 = (f32[64,512]{1,0:T(8,128)S(1)}, f32[64,512]{1,0:T(8,128)S(1)}, u32[]{:S(2)}, u32[]{:S(2)}) collective-permute-start(f32[64,512]{1,0:T(8,128)S(1)} %get-tuple-element.50.top), channel_id=1, source_target_pairs={{0,8},{8,16},{16,24},{24,0},{1,9},{9,17},{17,25},{25,1},{2,10},{10... | collective-permute-start | bytes 393224 | tf_op jit(solution)/shard_map/ppermute | solution.py:669
  14.4 13.3 %all-to-all-start = ((f32[8,16,512]{2,1,0:T(8,128)}), f32[8,16,512]{2,1,0:T(8,128)S(1)}, u32[]{:S(2)}, u32[]{:S(2)}) async-start(f32[8,16,512]{2,1,0:T(8,128)} %bitcast.5), calls=%async_computation | async-start | bytes 524288 | tf_op jit(solution)/shard_map/all_to_all | solution.py:666
  17.9 6.4 %collective-permute-start.5 = (f32[64,512]{1,0:T(8,128)S(1)}, f32[64,512]{1,0:T(8,128)S(1)}, u32[]{:S(2)}, u32[]{:S(2)}) collective-permute-start(f32[64,512]{1,0:T(8,128)S(1)} %get-tuple-element.49.bottom), channel_id=1, source_target_pairs={{8,0},{16,8},{24,16},{0,24},{9,1},{17,9},{25,17},{1,25},{10,2},{18... | collective-permute-start | bytes 393224 | tf_op jit(solution)/shard_map/ppermute | solution.py:672
  30.5 6.5 %collective-permute-start.6 = (f32[64,512]{1,0:T(8,128)S(1)}, f32[64,512]{1,0:T(8,128)S(1)}, u32[]{:S(2)}, u32[]{:S(2)}) collective-permute-start(f32[64,512]{1,0:T(8,128)S(1)} %get-tuple-element.61.top), channel_id=1, source_target_pairs={{0,8},{8,16},{16,24},{24,0},{1,9},{9,17},{17,25},{25,1},{2,10},{10... | collective-permute-start | bytes 393224 | tf_op jit(solution)/shard_map/ppermute | solution.py:669
  32.0 13.1 %all-to-all-start.1 = ((f32[8,16,512]{2,1,0:T(8,128)}), f32[8,16,512]{2,1,0:T(8,128)S(1)}, u32[]{:S(2)}, u32[]{:S(2)}) async-start(f32[8,16,512]{2,1,0:T(8,128)} %bitcast.27), calls=%async_computation.1 | async-start | bytes 524288 | tf_op jit(solution)/shard_map/all_to_all | solution.py:666
  35.5 6.5 %collective-permute-start.7 = (f32[64,512]{1,0:T(8,128)S(1)}, f32[64,512]{1,0:T(8,128)S(1)}, u32[]{:S(2)}, u32[]{:S(2)}) collective-permute-start(f32[64,512]{1,0:T(8,128)S(1)} %get-tuple-element.60.bottom), channel_id=1, source_target_pairs={{8,0},{16,8},{24,16},{0,24},{9,1},{17,9},{25,17},{1,25},{10,2},{18... | collective-permute-start | bytes 393224 | tf_op jit(solution)/shard_map/ppermute | solution.py:672
  47.9 9.6 %all-to-all-start.2 = ((f32[32,1,128]{2,1,0:T(1,128)}), f32[32,1,128]{2,1,0:T(1,128)S(1)}, u32[]{:S(2)}, u32[]{:S(2)}) async-start(f32[32,1,128]{2,1,0:T(1,128)} %get-tuple-element.68), calls=%async_computation.2 | async-start | bytes 32768 | tf_op jit(solution)/shard_map/all_to_all | solution.py:751

commit v7 on v6

--- a/solution.py
+++ b/solution.py
@@ -126,11 +126,35 @@
             placed(c + 1, lanes, gather_lanes(jnp.where(low, second, first), back_next))
 
 
+def store_marks(owned, capacity, ids, marks):
+    row = jnp.concatenate([ids[2:3, :], ids[3:4, :]], axis=1)
+    owner, slot = lax.div(row, owned), lax.rem(row, owned)
+    crossing = owner != lax.axis_index("dev")
+    count = row.shape[1]
+    blocks = lax.axis_size("dev")
+    block = iota((blocks, count), 0)
+    earlier = (iota((count, count), 0) < iota((count, count), 1)).astype(F32).astype(BF16)
+    own = (block == owner) & crossing
+    ranks = dot(own.astype(F32).astype(BF16), earlier)
+    place = jnp.where(own, (block * (2 * capacity)).astype(F32) + ranks + 1.0, 0.0)
+    place = jnp.sum(place, axis=0, keepdims=True).astype(I32) - 1
+    first = lax.rem(jnp.concatenate([ids[0:1, :], ids[1:2, :]], axis=1), owned)
+    marks[...] = jnp.concatenate(
+        [place, first, jnp.where(crossing, -1, slot), jnp.zeros((marks.shape[0] - 3, count), I32)],
+        axis=0,
+    )
+
+
 def solve_body(
-    face_nodes, source, inverse, coupling, codes, scales, solved, coupling_here, table,
-    source_here, inverse_here, orientation, scale, semaphores
+    face_nodes, owned, capacity, source, inverse, coupling, codes, scales, faces,
+    solved, coupling_here, table, marks,
+    source_here, inverse_here, orientation, scale, ids, semaphores
 ):
-    small = [begin(codes, orientation, semaphores.at[4]), begin(scales, scale, semaphores.at[5])]
+    small = [
+        begin(codes, orientation, semaphores.at[4]),
+        begin(scales, scale, semaphores.at[5]),
+        begin(faces, ids, semaphores.at[7]),
+    ]
     depth = inverse.shape[0] // 2
     reads = []
     for k in range(2):
@@ -167,6 +191,7 @@
         j = jnp.where(second, edge - 1 - j, j)
         back = turned + i * edge + j
         table[c * count : (c + 1) * count, :] = forward + pair * back + scaled
+    store_marks(owned, capacity, ids, marks)
     for k, pieces in enumerate(reads):
         for piece in pieces:
             piece.wait()
@@ -229,7 +254,7 @@
 
 
 def names_body(owned, capacity, block_of, ids, *refs):
-    *others, sides, send, wanted, marks = refs
+    *others, marks, sides, send, wanted = refs
     here = lax.axis_index("dev")
 
     def second(rows, at):
@@ -241,25 +266,13 @@
     blocks, count = names.shape
     earlier = (iota((count, count), 0) < iota((count, count), 1)).astype(F32).astype(BF16)
     block = block_of(iota((blocks, count), 0), here)
-    row = second(ids, 0)
-    owner, slot = lax.div(row, owned), lax.rem(row, owned)
-    crossing = owner != here
     named = (lax.div(names, owned) == here) & (block != here)
-    own = (block == owner) & crossing
-    masks = jnp.concatenate([named.astype(F32), own.astype(F32)], axis=0).astype(BF16)
-    ranks = dot(masks, earlier)
-    place = jnp.where(own, (block * (2 * capacity)).astype(F32) + ranks[blocks:, :] + 1.0, 0.0)
-    place = jnp.sum(place, axis=0, keepdims=True).astype(I32) - 1
-    first = lax.rem(jnp.concatenate([ids[0:1, :], ids[1:2, :]], axis=1), owned)
-    marks[...] = jnp.concatenate(
-        [place, first, jnp.where(crossing, -1, slot), jnp.zeros((marks.shape[0] - 3, count), I32)],
-        axis=0,
-    )
+    ranks = dot(named.astype(F32).astype(BF16), earlier)
     shape = (send.shape[0], blocks)
     line = iota(shape, 0)
     of_line = block_of(iota(shape, 1), here) == lax.div(line, 2 * capacity)
     of_line = of_line.astype(F32).astype(BF16)
-    rank_here = dot(of_line, jnp.where(named, ranks[:blocks, :], -1.0).astype(BF16))
+    rank_here = dot(of_line, jnp.where(named, ranks, -1.0).astype(BF16))
     slot_here = dot(of_line, lax.rem(names, owned).astype(F32).astype(BF16))
     line = lax.rem(iota(rank_here.shape, 0), capacity).astype(F32)
     chosen = jnp.where(rank_here == line, slot_here + 1.0, 0.0)
@@ -682,12 +695,12 @@
     else:
         gathered = [lax.all_gather(ids, "dev", tiled=True)]
         block_of = lambda row, here: row
-    solved, coupling_here, table = call(
-        functools.partial(solve_body, face_nodes),
-        [whole, ((nodes, traces), F32), table],
-        [Raw(flat_source), Raw(interior_inverse), Raw(coupling), Raw(codes), Raw(scale)],
-        [whole, ((nodes, nodes), F32), (codes.shape, I32), (scale.shape, I32)],
-        copies=7,
+    solved, coupling_here, table, marks = call(
+        functools.partial(solve_body, face_nodes, owned, capacity),
+        [whole, ((nodes, traces), F32), table, ((8, owned), I32)],
+        [Raw(flat_source), Raw(interior_inverse), Raw(coupling), Raw(codes), Raw(scale), Raw(ids)],
+        [whole, ((nodes, nodes), F32), (codes.shape, I32), (scale.shape, I32), (ids.shape, I32)],
+        copies=8,
         flops=6 * flat_rows * nodes * nodes,
     )
     solved, sides, bottom, top = call(
@@ -698,10 +711,10 @@
         copies=1,
         flops=6 * flat_rows * nodes * traces,
     )
-    send, wanted, marks = call(
+    send, wanted = call(
         functools.partial(names_body, owned, capacity, block_of),
-        [message, ((lines, owned), I32), ((8, owned), I32)],
-        [ids] + gathered + [sides],
+        [message, ((lines, owned), I32)],
+        [ids] + gathered + [marks, sides],
         flops=400 * lines * side_rows * lanes,
     )
     up, down, received = climb(top), sink(bottom), across(send)

time: 60.7 us -> 60.7 us (level)
  no operation moved by 1% of the time
where the time goes in v7:
time: 60.7 us; the launch traced here: 60.1 us
  Pallas kernels  24.8 us (41%)
  starting transfers between devices  23.6 us (39%)
  waiting for transfers between devices  10.9 us (18%)
  between operations  0.74 us (1%)
    pallas_call x9, Pallas kernels, call(): pl.pallas_call(body, out_shape=[pltpu.HBM(*out[:2]) if len(out) > 2 else...  24.8 us
    ppermute x4, starting transfers between devices, per_device(): lax.ppermute(entry, 'dev', pairs)  7.1 us
    all_to_all x2, starting transfers between devices, across(): return lax.all_to_all(parts, 'dev', 0, 0, tiled=True).reshape(message.shape)  6.93 us
    all_to_all x2, waiting for transfers between devices, across(): return lax.all_to_all(parts, 'dev', 0, 0, tiled=True).reshape(message.shape)  6.42 us
    all_to_all x1, waiting for transfers between devices, per_device(): stats = lax.all_to_all(stats, ('gz', 'dev'), 0, 0, tiled=True)  4.5 us
    ppermute x2, starting transfers between devices, sink(): lax.ppermute(value, 'gz', [((at + 1) % layers, at) for at in range(layers)])  3.95 us
    ppermute x2, starting transfers between devices, climb(): lax.ppermute(value, 'gz', [(at, (at + 1) % layers) for at in range(layers)])  3.08 us
    all_to_all x1, starting transfers between devices, per_device(): stats = lax.all_to_all(stats, ('gz', 'dev'), 0, 0, tiled=True)  2.58 us
  transfers between devices with their start and end apart: 11, of which 3 were waited for; matrix products, arithmetic and copies ran while one was open for 0% of the time, Pallas kernels for 28%

profile of v7, /device:TPU:0, one launch (start us, length us, event | category | flops | bytes accessed | tf_op | source)
XLA Modules:
  0.0 60.1 jit_solution(9220580476129518825)
XLA Ops:
  0.6 0.5 collective-permute-start
  1.1 2.6 %collective-permute-start.1 = (s32[4,64]{1,0:T(4,128)}, s32[4,64]{1,0:T(4,128)S(1)}, u32[]{:S(2)}, u32[]{:S(2)}) collective-permute-start(s32[4,64]{1,0:T(4,128)} %bitcast.20), channel_id=1, source_target_pairs={{0,2},{1,3},{2,0},{3,1},{4,6},{5,7},{6,4},{7,5},{8,10},{9,11},{10,... | collective-permute-start | bytes 3080 | tf_op jit(solution)/shard_map/ppermute | solution.py:693
  3.8 1.3 %collective-permute-start.2 = (s32[4,64]{1,0:T(4,128)S(1)}, s32[4,64]{1,0:T(4,128)S(1)}, u32[]{:S(2)}, u32[]{:S(2)}) collective-permute-start(s32[4,64]{1,0:T(4,128)S(1)} %collective-permute-done), channel_id=1, source_target_pairs={{0,2},{1,3},{2,0},{3,1},{4,6},{5,7},{6,4},{7,5},{8,10},{9,11},{10,... | collective-permute-start | bytes 3080 | tf_op jit(solution)/shard_map/ppermute | solution.py:693
  5.1 2.4 %shard_map.94 = (f32[512,512]{1,0:T(8,128)S(1)}, f32[512,384]{1,0:T(8,128)S(1)}, s32[384,128]{1,0:T(8,128)S(1)}, s32[8,128]{1,0:T(8,128)S(1)}) custom-call(f32[512,512]{1,0:T(8,128)} %bitcast.29, f32[512,512]{1,0:T(8,128)} %inverse.3, f32[512,384]{1,0:T(8,128)} %coupling.3, s32[6,64]{1,0:T(8,128)} %bitcast.31, s32[1,64]{1,0:T(1,128)} %bitcast.32, ...), custom_call_target="tpu_custom_call" | custom-call | flops 805306368 | bytes 2886400 | tf_op jit(solution)/shard_map/pallas_call | solution.py:32
  7.5 0.0 collective-permute-done.2
  7.5 2.7 %collective-permute-start.3 = (s32[16,64]{1,0:T(8,128)S(1)}, s32[16,64]{1,0:T(8,128)S(1)}, u32[]{:S(2)}, u32[]{:S(2)}) collective-permute-start(s32[16,64]{1,0:T(8,128)S(1)} %pad_add_fusion.refs_0_), channel_id=1, source_target_pairs={{0,4},{1,5},{2,6},{3,7},{4,0},{5,1},{6,2},{7,3},{8,12},{9,13},{10,... | collective-permute-start | bytes 12296 | tf_op jit(solution)/shard_map/ppermute | solution.py:693
  10.2 1.4 %shard_map.95 = (f32[512,512]{1,0:T(8,128)}, f32[256,512]{1,0:T(8,128)S(1)}, f32[64,512]{1,0:T(8,128)S(1)}, f32[64,512]{1,0:T(8,128)S(1)}) custom-call(f32[512,512]{1,0:T(8,128)S(1)} %get-tuple-element.44.solved, f32[512,384]{1,0:T(8,128)S(1)} %get-tuple-element.45.coupling, s32[384,128]{1,0:T(8,128)S(1)} %get-tuple-element.46.table), custom_call_target="tpu_custom_call" | custom-call | flops 603979776 | bytes 2031616 | tf_op jit(solution)/shard_map/pallas_call | solution.py:32
  11.5 1.5 %collective-permute-start.4 = (f32[64,512]{1,0:T(8,128)S(1)}, f32[64,512]{1,0:T(8,128)S(1)}, u32[]{:S(2)}, u32[]{:S(2)}) collective-permute-start(f32[64,512]{1,0:T(8,128)S(1)} %get-tuple-element.50.top), channel_id=1, source_target_pairs={{0,8},{8,16},{16,24},{24,0},{1,9},{9,17},{17,25},{25,1},{2,10},{10... | collective-permute-start | bytes 393224 | tf_op jit(solution)/shard_map/ppermute | solution.py:682
  13.1 1.3 %shard_map.96 = (f32[128,512]{1,0:T(8,128)}, s32[128,128]{1,0:T(8,128)S(1)}) custom-call(s32[4,64]{1,0:T(4,128)S(1)} %bitcast.23, s32[16,64]{1,0:T(8,128)S(1)} %pad_add_fusion.refs_0_, s32[16,64]{1,0:T(8,128)S(1)} %collective-permute-done.3.refs_1_, s32[8,128]{1,0:T(8,128)S(1)} %get-tuple-element.43.refs_2_.marks, f32[256,512]{1,0:T(8,128)S(1)} %get-tuple-element.47.refs_3_.sides), custom_call_target="tpu_custom_call" | custom-call | flops 6710886400 | bytes 537600 | tf_op jit(solution)/shard_map/pallas_call | solution.py:32
  14.4 3.5 %all-to-all-start = ((f32[8,16,512]{2,1,0:T(8,128)}), f32[8,16,512]{2,1,0:T(8,128)S(1)}, u32[]{:S(2)}, u32[]{:S(2)}) async-start(f32[8,16,512]{2,1,0:T(8,128)} %bitcast.5), calls=%async_computation | async-start | bytes 524288 | tf_op jit(solution)/shard_map/all_to_all | solution.py:679
  17.9 2.5 %collective-permute-start.5 = (f32[64,512]{1,0:T(8,128)S(1)}, f32[64,512]{1,0:T(8,128)S(1)}, u32[]{:S(2)}, u32[]{:S(2)}) collective-permute-start(f32[64,512]{1,0:T(8,128)S(1)} %get-tuple-element.49.bottom), channel_id=1, source_target_pairs={{8,0},{16,8},{24,16},{0,24},{9,1},{17,9},{25,17},{1,25},{10,2},{18... | collective-permute-start | bytes 393224 | tf_op jit(solution)/shard_map/ppermute | solution.py:685
  20.4 4.0 %shard_map.97 = (bf16[128,896]{1,0:T(8,128)(2,1)S(1)}, f32[256,512]{1,0:T(8,128)S(1)}, f32[64,512]{1,0:T(8,128)S(1)}, bf16[2,512,384]{2,1,0:T(8,128)(2,1)}, bf16[2,384,384]{2,1,0:T(8,128)(2,1)S(1)}) custom-call(s32[8,128]{1,0:T(8,128)S(1)} %get-tuple-element.43.refs_2_.marks, s32[128,128]{1,0:T(8,128)S(1)} %get-tuple-element.48.wanted, ...), custom_call_target="tpu_custom_call" | custom-call | flops 4026531840 | bytes 3280896 | tf_op jit(solution)/shard_map/pallas_call | solution.py:32
  24.3 3.3 %all-to-all-done = f32[8,16,512]{2,1,0:T(8,128)S(1)} async-done(((f32[8,16,512]{2,1,0:T(8,128)}), f32[8,16,512]{2,1,0:T(8,128)S(1)}, u32[]{:S(2)}, u32[]{:S(2)}) %all-to-all-start) | async-done | bytes 262176 | tf_op jit(solution)/shard_map/all_to_all | solution.py:679
  27.7 2.8 %shard_map.98 = (f32[192,512]{1,0:T(8,128)}, f32[512,384]{1,0:T(8,128)}, f32[256,512]{1,0:T(8,128)S(1)}, f32[64,512]{1,0:T(8,128)S(1)}, f32[64,512]{1,0:T(8,128)S(1)}, /*index=5*/f32[128,512]{1,0:T(8,128)}) custom-call(f32[256,512]{1,0:T(8,128)S(1)} %get-tuple-element.51.base, bf16[128,896]{1,0:T(8,128)(2,1)S(1)} %get-tuple-element.52.maps, ...), custom_call_target="tpu_custom_call" | custom-call | flops 452984832 | bytes 3014656 | tf_op jit(solution)/shard_map/pallas_call | solution.py:32
  30.5 1.5 %collective-permute-start.6 = (f32[64,512]{1,0:T(8,128)S(1)}, f32[64,512]{1,0:T(8,128)S(1)}, u32[]{:S(2)}, u32[]{:S(2)}) collective-permute-start(f32[64,512]{1,0:T(8,128)S(1)} %get-tuple-element.61.top), channel_id=1, source_target_pairs={{0,8},{8,16},{16,24},{24,0},{1,9},{9,17},{17,25},{25,1},{2,10},{10... | collective-permute-start | bytes 393224 | tf_op jit(solution)/shard_map/ppermute | solution.py:682
  32.0 3.4 %all-to-all-start.1 = ((f32[8,16,512]{2,1,0:T(8,128)}), f32[8,16,512]{2,1,0:T(8,128)S(1)}, u32[]{:S(2)}, u32[]{:S(2)}) async-start(f32[8,16,512]{2,1,0:T(8,128)} %bitcast.28), calls=%async_computation.1 | async-start | bytes 524288 | tf_op jit(solution)/shard_map/all_to_all | solution.py:679
  35.5 1.5 %collective-permute-start.7 = (f32[64,512]{1,0:T(8,128)S(1)}, f32[64,512]{1,0:T(8,128)S(1)}, u32[]{:S(2)}, u32[]{:S(2)}) collective-permute-start(f32[64,512]{1,0:T(8,128)S(1)} %get-tuple-element.60.bottom), channel_id=1, source_target_pairs={{8,0},{16,8},{24,16},{0,24},{9,1},{17,9},{25,17},{1,25},{10,2},{18... | collective-permute-start | bytes 393224 | tf_op jit(solution)/shard_map/ppermute | solution.py:685
  37.0 5.0 %shard_map.99 = (f32[512,512]{1,0:T(8,128)}, f32[512,128]{1,0:T(8,128)}, f32[512,64]{1,0:T(8,128)}, f32[512,384]{1,0:T(8,128)}, f32[256,512]{1,0:T(8,128)S(1)}, ...) custom-call(f32[192,512]{1,0:T(8,128)} %get-tuple-element.56.mine_in, ...), custom_call_target="tpu_custom_call" | custom-call | flops 4026531840 | bytes 4325376 | tf_op jit(solution)/shard_map/pallas_call | solution.py:32
  42.0 3.1 %all-to-all-done.1 = f32[8,16,512]{2,1,0:T(8,128)S(1)} async-done(((f32[8,16,512]{2,1,0:T(8,128)}), f32[8,16,512]{2,1,0:T(8,128)S(1)}, u32[]{:S(2)}, u32[]{:S(2)}) %all-to-all-start.1) | async-done | bytes 262176 | tf_op jit(solution)/shard_map/all_to_all | solution.py:679
  45.1 2.8 %shard_map.100 = (f32[192,512]{1,0:T(8,128)}, f32[512,384]{1,0:T(8,128)}, f32[32,1,128]{2,1,0:T(1,128)}) custom-call(f32[256,512]{1,0:T(8,128)S(1)} %get-tuple-element.62.base, bf16[128,896]{1,0:T(8,128)(2,1)S(1)} %get-tuple-element.52.maps, f32[128,512]{1,0:T(8,128)S(1)} %bitcast.17, f32[64,512]{1,0:T(8,128)S(1)} %get-tuple-element.64.below, ...), custom_call_target="tpu_custom_call" | custom-call | flops 452984832 | bytes 5013504 | tf_op jit(solution)/shard_map/pallas_call | solution.py:32
  47.9 2.6 %all-to-all-start.2 = ((f32[32,1,128]{2,1,0:T(1,128)}), f32[32,1,128]{2,1,0:T(1,128)S(1)}, u32[]{:S(2)}, u32[]{:S(2)}) async-start(f32[32,1,128]{2,1,0:T(1,128)} %get-tuple-element.68), calls=%async_computation.2 | async-start | bytes 32768 | tf_op jit(solution)/shard_map/all_to_all | solution.py:764
  50.5 2.6 %shard_map.101 = (f32[512,512]{1,0:T(8,128)S(1)}, f32[512,128]{1,0:T(8,128)}, f32[512,64]{1,0:T(8,128)}, f32[512,512]{1,0:T(8,128)S(1)}, f32[64,128]{1,0:T(8,128)S(1)}) custom-call(f32[192,512]{1,0:T(8,128)} %get-tuple-element.70.mine_in, f32[512,384]{1,0:T(8,128)} %get-tuple-element.71.flat_in, bf16[2,512,384]{2,1,0:T(8,128)(2,1)} %get-tuple-element.58.lift_in, ...), custom_call_target="tpu_custom_call" | custom-call | flops 603979776 | bytes 4456448 | tf_op jit(solution)/shard_map/pallas_call | solution.py:32
  53.1 4.5 %all-to-all-done.2.stats = f32[32,1,128]{2,1,0:T(1,128)S(1)} async-done(((f32[32,1,128]{2,1,0:T(1,128)}), f32[32,1,128]{2,1,0:T(1,128)S(1)}, u32[]{:S(2)}, u32[]{:S(2)}) %all-to-all-start.2) | async-done | bytes 16416 | tf_op jit(solution)/shard_map/all_to_all | solution.py:764
  57.6 2.5 %shard_map.102 = (f32[512,512]{1,0:T(8,128)}, f32[64,8,128]{2,1,0:T(8,128)}, f32[64,8,64]{2,1,0:T(8,128)}) custom-call(f32[32,1,128]{2,1,0:T(1,128)S(1)} %all-to-all-done.2.stats, f32[64,8,128]{2,1,0:T(8,128)} %bitcast.24, f32[64,8,128]{2,1,0:T(8,128)} %bitcast.26, f32[64,8,64]{2,1,0:T(8,128)} %bitcast.25, f32[64,8,64]{2,1,0:T(8,128)} %bitcast.27, ...), custom_call_target="tpu_custom_call" | custom-call | bytes 3981312 | tf_op jit(solution)/shard_map/pallas_call | solution.py:32
  (10 shorter events, 0.0 us)
Async XLA Ops:
  0.6 3.2 %collective-permute-start = (s32[4,64]{1,0:T(4,128)}, s32[4,64]{1,0:T(4,128)S(1)}, u32[]{:S(2)}, u32[]{:S(2)}) collective-permute-start(s32[4,64]{1,0:T(4,128)} %bitcast.19), channel_id=1, source_target_pairs={{0,1},{1,0},{2,3},{3,2},{4,5},{5,4},{6,7},{7,6},{8,9},{9,8},{10,11... | collective-permute-start | bytes 3080 | tf_op jit(solution)/shard_map/ppermute | solution.py:693
  1.1 6.3 %collective-permute-start.1 = (s32[4,64]{1,0:T(4,128)}, s32[4,64]{1,0:T(4,128)S(1)}, u32[]{:S(2)}, u32[]{:S(2)}) collective-permute-start(s32[4,64]{1,0:T(4,128)} %bitcast.20), channel_id=1, source_target_pairs={{0,2},{1,3},{2,0},{3,1},{4,6},{5,7},{6,4},{7,5},{8,10},{9,11},{10,... | collective-permute-start | bytes 3080 | tf_op jit(solution)/shard_map/ppermute | solution.py:693
  3.8 3.7 %collective-permute-start.2 = (s32[4,64]{1,0:T(4,128)S(1)}, s32[4,64]{1,0:T(4,128)S(1)}, u32[]{:S(2)}, u32[]{:S(2)}) collective-permute-start(s32[4,64]{1,0:T(4,128)S(1)} %collective-permute-done), channel_id=1, source_target_pairs={{0,2},{1,3},{2,0},{3,1},{4,6},{5,7},{6,4},{7,5},{8,10},{9,11},{10,... | collective-permute-start | bytes 3080 | tf_op jit(solution)/shard_map/ppermute | solution.py:693
  5.1 2.4 %copy-start = (s32[64,4]{0,1:T(4,128)S(1)}, s32[64,4]{0,1:T(4,128)}, u32[]{:S(2)}) copy-start(s32[64,4]{0,1:T(4,128)} %param.11) | copy-start | bytes 3076
  7.5 5.6 %collective-permute-start.3 = (s32[16,64]{1,0:T(8,128)S(1)}, s32[16,64]{1,0:T(8,128)S(1)}, u32[]{:S(2)}, u32[]{:S(2)}) collective-permute-start(s32[16,64]{1,0:T(8,128)S(1)} %pad_add_fusion.refs_0_), channel_id=1, source_target_pairs={{0,4},{1,5},{2,6},{3,7},{4,0},{5,1},{6,2},{7,3},{8,12},{9,13},{10,... | collective-permute-start | bytes 12296 | tf_op jit(solution)/shard_map/ppermute | solution.py:693
  11.5 8.8 %collective-permute-start.4 = (f32[64,512]{1,0:T(8,128)S(1)}, f32[64,512]{1,0:T(8,128)S(1)}, u32[]{:S(2)}, u32[]{:S(2)}) collective-permute-start(f32[64,512]{1,0:T(8,128)S(1)} %get-tuple-element.50.top), channel_id=1, source_target_pairs={{0,8},{8,16},{16,24},{24,0},{1,9},{9,17},{17,25},{25,1},{2,10},{10... | collective-permute-start | bytes 393224 | tf_op jit(solution)/shard_map/ppermute | solution.py:682
  14.4 13.3 %all-to-all-start = ((f32[8,16,512]{2,1,0:T(8,128)}), f32[8,16,512]{2,1,0:T(8,128)S(1)}, u32[]{:S(2)}, u32[]{:S(2)}) async-start(f32[8,16,512]{2,1,0:T(8,128)} %bitcast.5), calls=%async_computation | async-start | bytes 524288 | tf_op jit(solution)/shard_map/all_to_all | solution.py:679
  17.9 6.4 %collective-permute-start.5 = (f32[64,512]{1,0:T(8,128)S(1)}, f32[64,512]{1,0:T(8,128)S(1)}, u32[]{:S(2)}, u32[]{:S(2)}) collective-permute-start(f32[64,512]{1,0:T(8,128)S(1)} %get-tuple-element.49.bottom), channel_id=1, source_target_pairs={{8,0},{16,8},{24,16},{0,24},{9,1},{17,9},{25,17},{1,25},{10,2},{18... | collective-permute-start | bytes 393224 | tf_op jit(solution)/shard_map/ppermute | solution.py:685
  30.5 6.5 %collective-permute-start.6 = (f32[64,512]{1,0:T(8,128)S(1)}, f32[64,512]{1,0:T(8,128)S(1)}, u32[]{:S(2)}, u32[]{:S(2)}) collective-permute-start(f32[64,512]{1,0:T(8,128)S(1)} %get-tuple-element.61.top), channel_id=1, source_target_pairs={{0,8},{8,16},{16,24},{24,0},{1,9},{9,17},{17,25},{25,1},{2,10},{10... | collective-permute-start | bytes 393224 | tf_op jit(solution)/shard_map/ppermute | solution.py:682
  32.0 13.1 %all-to-all-start.1 = ((f32[8,16,512]{2,1,0:T(8,128)}), f32[8,16,512]{2,1,0:T(8,128)S(1)}, u32[]{:S(2)}, u32[]{:S(2)}) async-start(f32[8,16,512]{2,1,0:T(8,128)} %bitcast.28), calls=%async_computation.1 | async-start | bytes 524288 | tf_op jit(solution)/shard_map/all_to_all | solution.py:679
  35.5 6.6 %collective-permute-start.7 = (f32[64,512]{1,0:T(8,128)S(1)}, f32[64,512]{1,0:T(8,128)S(1)}, u32[]{:S(2)}, u32[]{:S(2)}) collective-permute-start(f32[64,512]{1,0:T(8,128)S(1)} %get-tuple-element.60.bottom), channel_id=1, source_target_pairs={{8,0},{16,8},{24,16},{0,24},{9,1},{17,9},{25,17},{1,25},{10,2},{18... | collective-permute-start | bytes 393224 | tf_op jit(solution)/shard_map/ppermute | solution.py:685
  47.9 9.7 %all-to-all-start.2 = ((f32[32,1,128]{2,1,0:T(1,128)}), f32[32,1,128]{2,1,0:T(1,128)S(1)}, u32[]{:S(2)}, u32[]{:S(2)}) async-start(f32[32,1,128]{2,1,0:T(1,128)} %get-tuple-element.68), calls=%async_computation.2 | async-start | bytes 32768 | tf_op jit(solution)/shard_map/all_to_all | solution.py:764

commit v8 on v6

--- a/solution.py
+++ b/solution.py
@@ -581,7 +581,8 @@
 ):
     rights = side_traces.shape[1]
     block = solved.shape[0] // rights
-    parts = [pl.ds(r * block, block) for r in range(rights)]
+    group = 2
+    parts = [pl.ds(r * block, group * block) for r in range(0, rights, group)]
     reads = [
         begin(solved.at[part], solved_here.at[part], semaphores.at[r])
         for r, part in enumerate(parts)
@@ -617,16 +618,18 @@
     writes = []
     for r, part in enumerate(parts):
         reads[r].wait()
-        solved_here[part, :] = solved_here[part, :] * scale - (
-            first[r : r + 1, :] * lifted_first[part, :]
-            + following[r : r + 1, :] * lifted_next[part, :]
-        )
+        for at in range(r * group, (r + 1) * group):
+            rows = slice(at * block, (at + 1) * block)
+            solved_here[rows, :] = solved_here[rows, :] * scale - (
+                first[at : at + 1, :] * lifted_first[rows, :]
+                + following[at : at + 1, :] * lifted_next[rows, :]
+            )
         writes.append(begin(solved_here.at[part], interior.at[part], semaphores.at[rights + 4 + r]))
     for k, (here, next_here, out) in enumerate(
         ((side_here, side_next_here, side_traces), (top_here, top_next_here, top_traces))
     ):
-        reads[rights + 2 * k].wait()
-        reads[rights + 2 * k + 1].wait()
+        reads[rights // group + 2 * k].wait()
+        reads[rights // group + 2 * k + 1].wait()
         here[...] = first[None] * here[...] + following[None] * next_here[...]
         writes.append(begin(here, out, semaphores.at[2 * rights + 4 + k]))
     for write in writes:

time: 60.7 us -> 60.6 us (level)
  no operation moved by 1% of the time
where the time goes in v8:
time: 60.6 us; the launch traced here: 60 us
  Pallas kernels  24.6 us (41%)
  starting transfers between devices  23.7 us (39%)
  waiting for transfers between devices  11 us (18%)
  between operations  0.74 us (1%)
    pallas_call x9, Pallas kernels, call(): pl.pallas_call(body, out_shape=[pltpu.HBM(*out[:2]) if len(out) > 2 else...  24.6 us
    ppermute x4, starting transfers between devices, per_device(): lax.ppermute(entry, 'dev', pairs)  7.11 us
    all_to_all x2, starting transfers between devices, across(): return lax.all_to_all(parts, 'dev', 0, 0, tiled=True).reshape(message.shape)  6.96 us
    all_to_all x2, waiting for transfers between devices, across(): return lax.all_to_all(parts, 'dev', 0, 0, tiled=True).reshape(message.shape)  6.44 us
    all_to_all x1, waiting for transfers between devices, per_device(): stats = lax.all_to_all(stats, ('gz', 'dev'), 0, 0, tiled=True)  4.5 us
    ppermute x2, starting transfers between devices, sink(): lax.ppermute(value, 'gz', [((at + 1) % layers, at) for at in range(layers)])  3.93 us
    ppermute x2, starting transfers between devices, climb(): lax.ppermute(value, 'gz', [(at, (at + 1) % layers) for at in range(layers)])  3.09 us
    all_to_all x1, starting transfers between devices, per_device(): stats = lax.all_to_all(stats, ('gz', 'dev'), 0, 0, tiled=True)  2.57 us
  transfers between devices with their start and end apart: 11, of which 3 were waited for; matrix products, arithmetic and copies ran while one was open for 0% of the time, Pallas kernels for 28%

profile of v8, /device:TPU:0, one launch (start us, length us, event | category | flops | bytes accessed | tf_op | source)
XLA Modules:
  0.0 60.0 jit_solution(7734619746876141555)
XLA Ops:
  0.6 0.5 collective-permute-start
  1.1 2.6 %collective-permute-start.1 = (s32[4,64]{1,0:T(4,128)}, s32[4,64]{1,0:T(4,128)S(1)}, u32[]{:S(2)}, u32[]{:S(2)}) collective-permute-start(s32[4,64]{1,0:T(4,128)} %bitcast.20), channel_id=1, source_target_pairs={{0,2},{1,3},{2,0},{3,1},{4,6},{5,7},{6,4},{7,5},{8,10},{9,11},{10,... | collective-permute-start | bytes 3080 | tf_op jit(solution)/shard_map/ppermute | solution.py:683
  3.8 1.3 %collective-permute-start.2 = (s32[4,64]{1,0:T(4,128)S(1)}, s32[4,64]{1,0:T(4,128)S(1)}, u32[]{:S(2)}, u32[]{:S(2)}) collective-permute-start(s32[4,64]{1,0:T(4,128)S(1)} %collective-permute-done), channel_id=1, source_target_pairs={{0,2},{1,3},{2,0},{3,1},{4,6},{5,7},{6,4},{7,5},{8,10},{9,11},{10,... | collective-permute-start | bytes 3080 | tf_op jit(solution)/shard_map/ppermute | solution.py:683
  5.1 2.3 %shard_map.94 = (f32[512,512]{1,0:T(8,128)S(1)}, f32[512,384]{1,0:T(8,128)S(1)}, s32[384,128]{1,0:T(8,128)S(1)}) custom-call(f32[512,512]{1,0:T(8,128)} %bitcast.28, f32[512,512]{1,0:T(8,128)} %inverse.3, f32[512,384]{1,0:T(8,128)} %coupling.3, s32[6,64]{1,0:T(8,128)} %bitcast.30, s32[1,64]{1,0:T(1,128)} %bitcast.31), custom_call_target="tpu_custom_call" | custom-call | flops 805306368 | bytes 2885376 | tf_op jit(solution)/shard_map/pallas_call | solution.py:32
  7.5 0.0 collective-permute-done.2
  7.5 2.7 %collective-permute-start.3 = (s32[16,64]{1,0:T(8,128)S(1)}, s32[16,64]{1,0:T(8,128)S(1)}, u32[]{:S(2)}, u32[]{:S(2)}) collective-permute-start(s32[16,64]{1,0:T(8,128)S(1)} %pad_add_fusion.refs_0_), channel_id=1, source_target_pairs={{0,4},{1,5},{2,6},{3,7},{4,0},{5,1},{6,2},{7,3},{8,12},{9,13},{10,... | collective-permute-start | bytes 12296 | tf_op jit(solution)/shard_map/ppermute | solution.py:683
  10.1 1.4 %shard_map.95 = (f32[512,512]{1,0:T(8,128)}, f32[256,512]{1,0:T(8,128)S(1)}, f32[64,512]{1,0:T(8,128)S(1)}, f32[64,512]{1,0:T(8,128)S(1)}) custom-call(f32[512,512]{1,0:T(8,128)S(1)} %get-tuple-element.43.solved, f32[512,384]{1,0:T(8,128)S(1)} %get-tuple-element.44.coupling, s32[384,128]{1,0:T(8,128)S(1)} %get-tuple-element.45.table), custom_call_target="tpu_custom_call" | custom-call | flops 603979776 | bytes 2031616 | tf_op jit(solution)/shard_map/pallas_call | solution.py:32
  11.5 1.5 %collective-permute-start.4 = (f32[64,512]{1,0:T(8,128)S(1)}, f32[64,512]{1,0:T(8,128)S(1)}, u32[]{:S(2)}, u32[]{:S(2)}) collective-permute-start(f32[64,512]{1,0:T(8,128)S(1)} %get-tuple-element.50.top), channel_id=1, source_target_pairs={{0,8},{8,16},{16,24},{24,0},{1,9},{9,17},{17,25},{25,1},{2,10},{10... | collective-permute-start | bytes 393224 | tf_op jit(solution)/shard_map/ppermute | solution.py:672
  13.1 1.3 %shard_map.96 = (f32[128,512]{1,0:T(8,128)}, s32[128,128]{1,0:T(8,128)S(1)}, s32[8,128]{1,0:T(8,128)S(1)}) custom-call(s32[4,64]{1,0:T(4,128)S(1)} %bitcast.22, s32[16,64]{1,0:T(8,128)S(1)} %pad_add_fusion.refs_0_, s32[16,64]{1,0:T(8,128)S(1)} %collective-permute-done.3.refs_1_, f32[256,512]{1,0:T(8,128)S(1)} %get-tuple-element.46.refs_2_.sides), custom_call_target="tpu_custom_call" | custom-call | flops 6710886400 | bytes 533504 | tf_op jit(solution)/shard_map/pallas_call | solution.py:32
  14.4 3.6 %all-to-all-start = ((f32[8,16,512]{2,1,0:T(8,128)}), f32[8,16,512]{2,1,0:T(8,128)S(1)}, u32[]{:S(2)}, u32[]{:S(2)}) async-start(f32[8,16,512]{2,1,0:T(8,128)} %bitcast.5), calls=%async_computation | async-start | bytes 524288 | tf_op jit(solution)/shard_map/all_to_all | solution.py:669
  17.9 2.4 %collective-permute-start.5 = (f32[64,512]{1,0:T(8,128)S(1)}, f32[64,512]{1,0:T(8,128)S(1)}, u32[]{:S(2)}, u32[]{:S(2)}) collective-permute-start(f32[64,512]{1,0:T(8,128)S(1)} %get-tuple-element.49.bottom), channel_id=1, source_target_pairs={{8,0},{16,8},{24,16},{0,24},{9,1},{17,9},{25,17},{1,25},{10,2},{18... | collective-permute-start | bytes 393224 | tf_op jit(solution)/shard_map/ppermute | solution.py:675
  20.4 4.0 %shard_map.97 = (bf16[128,896]{1,0:T(8,128)(2,1)S(1)}, f32[256,512]{1,0:T(8,128)S(1)}, f32[64,512]{1,0:T(8,128)S(1)}, bf16[2,512,384]{2,1,0:T(8,128)(2,1)}, bf16[2,384,384]{2,1,0:T(8,128)(2,1)S(1)}) custom-call(s32[8,128]{1,0:T(8,128)S(1)} %get-tuple-element.47.marks, s32[128,128]{1,0:T(8,128)S(1)} %get-tuple-element.48.wanted, ...), custom_call_target="tpu_custom_call" | custom-call | flops 4026531840 | bytes 3280896 | tf_op jit(solution)/shard_map/pallas_call | solution.py:32
  24.3 3.3 %all-to-all-done = f32[8,16,512]{2,1,0:T(8,128)S(1)} async-done(((f32[8,16,512]{2,1,0:T(8,128)}), f32[8,16,512]{2,1,0:T(8,128)S(1)}, u32[]{:S(2)}, u32[]{:S(2)}) %all-to-all-start) | async-done | bytes 262176 | tf_op jit(solution)/shard_map/all_to_all | solution.py:669
  27.7 2.8 %shard_map.98 = (f32[192,512]{1,0:T(8,128)}, f32[512,384]{1,0:T(8,128)}, f32[256,512]{1,0:T(8,128)S(1)}, f32[64,512]{1,0:T(8,128)S(1)}, f32[64,512]{1,0:T(8,128)S(1)}, /*index=5*/f32[128,512]{1,0:T(8,128)}) custom-call(f32[256,512]{1,0:T(8,128)S(1)} %get-tuple-element.51.base, bf16[128,896]{1,0:T(8,128)(2,1)S(1)} %get-tuple-element.52.maps, ...), custom_call_target="tpu_custom_call" | custom-call | flops 452984832 | bytes 3014656 | tf_op jit(solution)/shard_map/pallas_call | solution.py:32
  30.5 1.5 %collective-permute-start.6 = (f32[64,512]{1,0:T(8,128)S(1)}, f32[64,512]{1,0:T(8,128)S(1)}, u32[]{:S(2)}, u32[]{:S(2)}) collective-permute-start(f32[64,512]{1,0:T(8,128)S(1)} %get-tuple-element.61.top), channel_id=1, source_target_pairs={{0,8},{8,16},{16,24},{24,0},{1,9},{9,17},{17,25},{25,1},{2,10},{10... | collective-permute-start | bytes 393224 | tf_op jit(solution)/shard_map/ppermute | solution.py:672
  32.0 3.4 %all-to-all-start.1 = ((f32[8,16,512]{2,1,0:T(8,128)}), f32[8,16,512]{2,1,0:T(8,128)S(1)}, u32[]{:S(2)}, u32[]{:S(2)}) async-start(f32[8,16,512]{2,1,0:T(8,128)} %bitcast.27), calls=%async_computation.1 | async-start | bytes 524288 | tf_op jit(solution)/shard_map/all_to_all | solution.py:669
  35.5 1.5 %collective-permute-start.7 = (f32[64,512]{1,0:T(8,128)S(1)}, f32[64,512]{1,0:T(8,128)S(1)}, u32[]{:S(2)}, u32[]{:S(2)}) collective-permute-start(f32[64,512]{1,0:T(8,128)S(1)} %get-tuple-element.60.bottom), channel_id=1, source_target_pairs={{8,0},{16,8},{24,16},{0,24},{9,1},{17,9},{25,17},{1,25},{10,2},{18... | collective-permute-start | bytes 393224 | tf_op jit(solution)/shard_map/ppermute | solution.py:675
  37.0 5.0 %shard_map.99 = (f32[512,512]{1,0:T(8,128)}, f32[512,128]{1,0:T(8,128)}, f32[512,64]{1,0:T(8,128)}, f32[512,384]{1,0:T(8,128)}, f32[256,512]{1,0:T(8,128)S(1)}, ...) custom-call(f32[192,512]{1,0:T(8,128)} %get-tuple-element.56.mine_in, ...), custom_call_target="tpu_custom_call" | custom-call | flops 4026531840 | bytes 4325376 | tf_op jit(solution)/shard_map/pallas_call | solution.py:32
  42.0 3.1 %all-to-all-done.1 = f32[8,16,512]{2,1,0:T(8,128)S(1)} async-done(((f32[8,16,512]{2,1,0:T(8,128)}), f32[8,16,512]{2,1,0:T(8,128)S(1)}, u32[]{:S(2)}, u32[]{:S(2)}) %all-to-all-start.1) | async-done | bytes 262176 | tf_op jit(solution)/shard_map/all_to_all | solution.py:669
  45.1 2.8 %shard_map.100 = (f32[192,512]{1,0:T(8,128)}, f32[512,384]{1,0:T(8,128)}, f32[32,1,128]{2,1,0:T(1,128)}) custom-call(f32[256,512]{1,0:T(8,128)S(1)} %get-tuple-element.62.base, bf16[128,896]{1,0:T(8,128)(2,1)S(1)} %get-tuple-element.52.maps, f32[128,512]{1,0:T(8,128)S(1)} %bitcast.17, f32[64,512]{1,0:T(8,128)S(1)} %get-tuple-element.64.below, ...), custom_call_target="tpu_custom_call" | custom-call | flops 452984832 | bytes 5013504 | tf_op jit(solution)/shard_map/pallas_call | solution.py:32
  47.9 2.6 %all-to-all-start.2 = ((f32[32,1,128]{2,1,0:T(1,128)}), f32[32,1,128]{2,1,0:T(1,128)S(1)}, u32[]{:S(2)}, u32[]{:S(2)}) async-start(f32[32,1,128]{2,1,0:T(1,128)} %get-tuple-element.68), calls=%async_computation.2 | async-start | bytes 32768 | tf_op jit(solution)/shard_map/all_to_all | solution.py:754
  50.5 2.6 %shard_map.101 = (f32[512,512]{1,0:T(8,128)S(1)}, f32[512,128]{1,0:T(8,128)}, f32[512,64]{1,0:T(8,128)}, f32[512,512]{1,0:T(8,128)S(1)}, f32[64,128]{1,0:T(8,128)S(1)}) custom-call(f32[192,512]{1,0:T(8,128)} %get-tuple-element.70.mine_in, f32[512,384]{1,0:T(8,128)} %get-tuple-element.71.flat_in, bf16[2,512,384]{2,1,0:T(8,128)(2,1)} %get-tuple-element.58.lift_in, ...), custom_call_target="tpu_custom_call" | custom-call | flops 603979776 | bytes 4456448 | tf_op jit(solution)/shard_map/pallas_call | solution.py:32
  53.1 4.5 %all-to-all-done.2.stats = f32[32,1,128]{2,1,0:T(1,128)S(1)} async-done(((f32[32,1,128]{2,1,0:T(1,128)}), f32[32,1,128]{2,1,0:T(1,128)S(1)}, u32[]{:S(2)}, u32[]{:S(2)}) %all-to-all-start.2) | async-done | bytes 16416 | tf_op jit(solution)/shard_map/all_to_all | solution.py:754
  57.6 2.4 %shard_map.102 = (f32[512,512]{1,0:T(8,128)}, f32[64,8,128]{2,1,0:T(8,128)}, f32[64,8,64]{2,1,0:T(8,128)}) custom-call(f32[32,1,128]{2,1,0:T(1,128)S(1)} %all-to-all-done.2.stats, f32[64,8,128]{2,1,0:T(8,128)} %bitcast.23, f32[64,8,128]{2,1,0:T(8,128)} %bitcast.25, f32[64,8,64]{2,1,0:T(8,128)} %bitcast.24, f32[64,8,64]{2,1,0:T(8,128)} %bitcast.26, ...), custom_call_target="tpu_custom_call" | custom-call | bytes 3981312 | tf_op jit(solution)/shard_map/pallas_call | solution.py:32
  (10 shorter events, 0.0 us)
Async XLA Ops:
  0.6 3.2 %collective-permute-start = (s32[4,64]{1,0:T(4,128)}, s32[4,64]{1,0:T(4,128)S(1)}, u32[]{:S(2)}, u32[]{:S(2)}) collective-permute-start(s32[4,64]{1,0:T(4,128)} %bitcast.19), channel_id=1, source_target_pairs={{0,1},{1,0},{2,3},{3,2},{4,5},{5,4},{6,7},{7,6},{8,9},{9,8},{10,11... | collective-permute-start | bytes 3080 | tf_op jit(solution)/shard_map/ppermute | solution.py:683
  1.1 6.3 %collective-permute-start.1 = (s32[4,64]{1,0:T(4,128)}, s32[4,64]{1,0:T(4,128)S(1)}, u32[]{:S(2)}, u32[]{:S(2)}) collective-permute-start(s32[4,64]{1,0:T(4,128)} %bitcast.20), channel_id=1, source_target_pairs={{0,2},{1,3},{2,0},{3,1},{4,6},{5,7},{6,4},{7,5},{8,10},{9,11},{10,... | collective-permute-start | bytes 3080 | tf_op jit(solution)/shard_map/ppermute | solution.py:683
  3.8 3.7 %collective-permute-start.2 = (s32[4,64]{1,0:T(4,128)S(1)}, s32[4,64]{1,0:T(4,128)S(1)}, u32[]{:S(2)}, u32[]{:S(2)}) collective-permute-start(s32[4,64]{1,0:T(4,128)S(1)} %collective-permute-done), channel_id=1, source_target_pairs={{0,2},{1,3},{2,0},{3,1},{4,6},{5,7},{6,4},{7,5},{8,10},{9,11},{10,... | collective-permute-start | bytes 3080 | tf_op jit(solution)/shard_map/ppermute | solution.py:683
  5.1 2.4 %copy-start = (s32[64,4]{0,1:T(4,128)S(1)}, s32[64,4]{0,1:T(4,128)}, u32[]{:S(2)}) copy-start(s32[64,4]{0,1:T(4,128)} %param.11) | copy-start | bytes 3076
  7.5 5.6 %collective-permute-start.3 = (s32[16,64]{1,0:T(8,128)S(1)}, s32[16,64]{1,0:T(8,128)S(1)}, u32[]{:S(2)}, u32[]{:S(2)}) collective-permute-start(s32[16,64]{1,0:T(8,128)S(1)} %pad_add_fusion.refs_0_), channel_id=1, source_target_pairs={{0,4},{1,5},{2,6},{3,7},{4,0},{5,1},{6,2},{7,3},{8,12},{9,13},{10,... | collective-permute-start | bytes 12296 | tf_op jit(solution)/shard_map/ppermute | solution.py:683
  11.5 8.9 %collective-permute-start.4 = (f32[64,512]{1,0:T(8,128)S(1)}, f32[64,512]{1,0:T(8,128)S(1)}, u32[]{:S(2)}, u32[]{:S(2)}) collective-permute-start(f32[64,512]{1,0:T(8,128)S(1)} %get-tuple-element.50.top), channel_id=1, source_target_pairs={{0,8},{8,16},{16,24},{24,0},{1,9},{9,17},{17,25},{25,1},{2,10},{10... | collective-permute-start | bytes 393224 | tf_op jit(solution)/shard_map/ppermute | solution.py:672
  14.4 13.3 %all-to-all-start = ((f32[8,16,512]{2,1,0:T(8,128)}), f32[8,16,512]{2,1,0:T(8,128)S(1)}, u32[]{:S(2)}, u32[]{:S(2)}) async-start(f32[8,16,512]{2,1,0:T(8,128)} %bitcast.5), calls=%async_computation | async-start | bytes 524288 | tf_op jit(solution)/shard_map/all_to_all | solution.py:669
  17.9 6.4 %collective-permute-start.5 = (f32[64,512]{1,0:T(8,128)S(1)}, f32[64,512]{1,0:T(8,128)S(1)}, u32[]{:S(2)}, u32[]{:S(2)}) collective-permute-start(f32[64,512]{1,0:T(8,128)S(1)} %get-tuple-element.49.bottom), channel_id=1, source_target_pairs={{8,0},{16,8},{24,16},{0,24},{9,1},{17,9},{25,17},{1,25},{10,2},{18... | collective-permute-start | bytes 393224 | tf_op jit(solution)/shard_map/ppermute | solution.py:675
  30.5 6.5 %collective-permute-start.6 = (f32[64,512]{1,0:T(8,128)S(1)}, f32[64,512]{1,0:T(8,128)S(1)}, u32[]{:S(2)}, u32[]{:S(2)}) collective-permute-start(f32[64,512]{1,0:T(8,128)S(1)} %get-tuple-element.61.top), channel_id=1, source_target_pairs={{0,8},{8,16},{16,24},{24,0},{1,9},{9,17},{17,25},{25,1},{2,10},{10... | collective-permute-start | bytes 393224 | tf_op jit(solution)/shard_map/ppermute | solution.py:672
  32.0 13.1 %all-to-all-start.1 = ((f32[8,16,512]{2,1,0:T(8,128)}), f32[8,16,512]{2,1,0:T(8,128)S(1)}, u32[]{:S(2)}, u32[]{:S(2)}) async-start(f32[8,16,512]{2,1,0:T(8,128)} %bitcast.27), calls=%async_computation.1 | async-start | bytes 524288 | tf_op jit(solution)/shard_map/all_to_all | solution.py:669
  35.5 6.5 %collective-permute-start.7 = (f32[64,512]{1,0:T(8,128)S(1)}, f32[64,512]{1,0:T(8,128)S(1)}, u32[]{:S(2)}, u32[]{:S(2)}) collective-permute-start(f32[64,512]{1,0:T(8,128)S(1)} %get-tuple-element.60.bottom), channel_id=1, source_target_pairs={{8,0},{16,8},{24,16},{0,24},{9,1},{17,9},{25,17},{1,25},{10,2},{18... | collective-permute-start | bytes 393224 | tf_op jit(solution)/shard_map/ppermute | solution.py:675
  47.9 9.6 %all-to-all-start.2 = ((f32[32,1,128]{2,1,0:T(1,128)}), f32[32,1,128]{2,1,0:T(1,128)S(1)}, u32[]{:S(2)}, u32[]{:S(2)}) async-start(f32[32,1,128]{2,1,0:T(1,128)} %get-tuple-element.68), calls=%async_computation.2 | async-start | bytes 32768 | tf_op jit(solution)/shard_map/all_to_all | solution.py:754
